TPU v7x, 256 devices: a whole 4x4x8 slice. The times are simulated.
256 devices in a mesh: section: 4 (over y), seq: 64 (over x, z, core).
Axes of the slice: x: 4, y: 4, z: 8, core: 2. Of those that a mesh axis runs over, the one named last changes fastest.
Arguments:
- arriving: bfloat16 [4, 32768, 1536], P('section', 'seq'), may hold values from -6 to 6
- queued: bfloat16 [32768, 1536], P('seq'), may hold values from -6 to 6
- sequence_norm_gain: float32 [4, 1536], P('section'), may hold values from 0.1 to 1.9
- block_factor: bfloat16 [4, 128, 256, 256], P('section', 'seq'), may hold values from -0.375 to 0.375
- cross_factor: bfloat16 [4, 256, 128, 128], P('section', 'seq'), may hold values from -0.5 to 0.5
- channel_gain: float32 [4, 1536], P('section'), may hold values from 0.1 to 1.9
- up_weight: bfloat16 [4, 4, 384, 1024], P('section'), may hold values from -0.3125 to 0.3125
- down_weight: bfloat16 [4, 4, 1024, 384], P('section'), may hold values from -0.1875 to 0.1875
Outputs:
- leading_sequence_output: bfloat16 [4, 32768, 1536], P('section', 'seq')
- second_output: bfloat16 [4, 32768, 1536], P('section', 'seq')
All inputs are finite; a program needn't handle non-finite values.
Results may differ from a plain program's by a relative error of at most 0.011.
Values may be sent and summed in bfloat16 or wider, within the bound.
No kernel may reach another device: no remote copies, remote signals or barrier semaphores. Data moves between devices by JAX's collectives and lax.ppermute only.
A program may use at most 128 MiB of HBM per device.

v0:
```python
import jax
import jax.numpy as jnp
from jax import lax
from jax.sharding import PartitionSpec as P

norm_epsilon_floor = 1e-05


def from_behind(value, axis, steps):
    count = lax.axis_size(axis)
    leading, last = (max(0, -steps), min(count, count - steps))
    return lax.ppermute(value, axis, [(source, source + steps) for source in range(leading, last)])


def normalize(values, gain):
    scale = lax.rsqrt(jnp.mean(values * values, axis=-1, keepdims=True) + norm_epsilon_floor)
    return (values * scale * gain).astype(jnp.bfloat16)


def channel_mixing(residual, channel_vector, up_mats, down_matrices):
    token_count, channels = residual.shape
    groups = up_mats.shape[0]
    normed_mid = normalize(residual, channel_vector).reshape(
        token_count, groups, channels // groups
    )
    expanded = jnp.einsum("tgc,gcf->tgf", normed_mid, up_mats, preferred_element_type=jnp.float32)
    gelu_activations = jax.nn.gelu(expanded, approximate=True).astype(jnp.bfloat16)
    reduced_hidden = jnp.einsum(
        "shb,hbl->shl", gelu_activations, down_matrices, preferred_element_type=jnp.float32
    )
    return (residual + reduced_hidden.reshape(token_count, channels)).astype(jnp.bfloat16)


def second_factor(cross_mats, columns):
    return jnp.einsum(
        "jim,mjd->ijd", cross_mats, columns, preferred_element_type=jnp.float32
    ).astype(jnp.bfloat16)


def apply_layer(stream, mix_row, block_mats, cross_mats, channel_vector, up_mats, down_matrices):
    token_count, channels = stream.shape
    local_blocks = block_mats.shape[0]
    block_size = block_mats.shape[1]
    stream_wide = stream.astype(jnp.float32)
    normed_in = normalize(stream_wide, mix_row).reshape(local_blocks, block_size, channels)
    within = jnp.einsum(
        "ipk,ikd->ipd", block_mats, normed_in, preferred_element_type=jnp.float32
    ).astype(jnp.bfloat16)
    columns = lax.all_to_all(within, "seq", split_axis=1, concat_axis=0, tiled=True)
    across = second_factor(cross_mats, columns)
    restored = lax.all_to_all(across, "seq", split_axis=0, concat_axis=1, tiled=True)
    residual = stream_wide + restored.reshape(token_count, channels).astype(jnp.float32)
    return channel_mixing(residual, channel_vector, up_mats, down_matrices)


def per_device(
    arriving,
    queued,
    sequence_norm_gain,
    block_factor,
    cross_factor,
    channel_gain,
    up_weight,
    down_weight,
):
    section_index = lax.axis_index("section")
    weights = (
        sequence_norm_gain[0],
        block_factor[0],
        cross_factor[0],
        channel_gain[0],
        up_weight[0],
        down_weight[0],
    )
    first_result = apply_layer(
        arriving[0], weights[0], weights[1], weights[2], weights[3], weights[4], weights[5]
    )
    received = from_behind(first_result, "section", 1)
    entering = jnp.where(section_index == 0, queued, received)
    second_result = apply_layer(
        entering, weights[0], weights[1], weights[2], weights[3], weights[4], weights[5]
    )
    return (first_result[None], second_result[None])


def solution(mesh):
    placed = (
        P("section", "seq", None),
        P("seq", None),
        P("section", None),
        P("section", "seq", None, None),
        P("section", "seq", None, None),
        P("section", None),
        P("section", None, None, None),
        P("section", None, None, None),
    )
    return jax.shard_map(
        per_device,
        mesh=mesh,
        in_specs=placed,
        out_specs=(P("section", "seq", None), P("section", "seq", None)),
        check_vma=False,
    )
```

profile of v0, /device:TPU:1, one launch (start us, length us, event | category | flops | bytes accessed | tf_op | source)
XLA Modules:
  0.0 338.8 jit_solution(10378272441326696693)
XLA Ops:
  0.7 3.6 %convert_element_type.123 = f32[1,512,1536]{2,1,0:T(8,128)} convert(bf16[1,512,1536]{2,1,0:T(8,128)(2,1)} %param.8) | non-fusion elementwise | flops 786432 | bytes 4718592 | tf_op jit(solution)/shard_map/convert_element_type | solution.py:44
  4.7 3.6 %copy.63 = f32[2,256,1536]{1,2,0:T(8,128)} copy(f32[2,256,1536]{2,1,0:T(8,128)} %bitcast.87) | data formatting | bytes 6291456 | tf_op jit(solution)/shard_map/convert_element_type | solution.py:44
  8.4 3.7 %fusion.30 = bf16[2,256,1536]{1,2,0:T(8,128)(2,1)} fusion(f32[2,256,1536]{1,2,0:T(8,128)} %copy.63, f32[1536]{0:T(1024)S(1)} %reduce, f32[2,256]{1,0:T(2,128)S(1)} %rsqrt.36, bf16[1,2,256,256]{3,2,1,0:T(8,128)(2,1)S(1)} %copy-done.6), kind=kOutput, calls=%fused_computation.49 | convolution fusion | flops 405798912 | bytes 4988928 | tf_op jit(solution)/shard_map/ipk,ikd->ipd/dot_general | solution.py:46
  12.1 4.9 %copy.64 = bf16[2,256,1536]{2,0,1:T(2,128)(2,1)} copy(bf16[2,256,1536]{1,2,0:T(8,128)(2,1)} %fusion.30) | data formatting | bytes 3145728 | tf_op jit(solution)/shard_map/convert_element_type | solution.py:48
  17.0 52.9 %all_to_all.54 = bf16[2,256,1536]{2,0,1:T(2,128)(2,1)S(1)} all-to-all(bf16[2,256,1536]{2,0,1:T(2,128)(2,1)} %copy.64), channel_id=1, replica_groups=mesh['section'=4,'seq'=64] {'seq'}, dimensions={1} | all-to-all | bytes 3145728 | tf_op jit(solution)/shard_map/all_to_all | solution.py:49
  72.4 3.9 %copy.67 = bf16[128,4,1536]{2,1,0:T(4,128)(2,1)} copy(bf16[128,4,1536]{0,2,1:T(8,128)(2,1)} %fusion.31) | data formatting | bytes 3145728 | tf_op jit(solution)/shard_map/convert_element_type | solution.py:37
  76.2 6.3 %all-to-all-start.1 = ((bf16[128,4,1536]{2,1,0:T(4,128)(2,1)}), bf16[128,4,1536]{2,1,0:T(4,128)(2,1)}, u32[]{:S(2)}, u32[]{:S(2)}) async-start(bf16[128,4,1536]{2,1,0:T(4,128)(2,1)} %copy.67), calls=%async_computation.1 | async-start | bytes 3145728 | tf_op jit(solution)/shard_map/all_to_all | solution.py:51
  82.5 4.3 %reshape.126 = f32[512,4,384]{2,1,0:T(4,128)} reshape(bf16[1,512,1536]{2,1,0:T(8,128)(2,1)} %param.8) | data formatting | bytes 4718592 | tf_op jit(solution)/shard_map/convert_element_type | solution.py:44
  88.2 34.1 %all-to-all-done.1 = bf16[128,4,1536]{2,1,0:T(4,128)(2,1)} async-done(((bf16[128,4,1536]{2,1,0:T(4,128)(2,1)}), bf16[128,4,1536]{2,1,0:T(4,128)(2,1)}, u32[]{:S(2)}, u32[]{:S(2)}) %all-to-all-start.1) | async-done | bytes 1572896 | tf_op jit(solution)/shard_map/all_to_all | solution.py:51
  122.3 2.3 convert_bitcast_fusion.1
  126.5 5.1 %reshape.127 = f32[512,4,384]{2,1,0:T(4,128)} reshape(f32[2,64,4,1536]{3,2,1,0:T(4,128)} %copy.68) | data formatting | bytes 6291456 | tf_op jit(solution)/shard_map/convert_element_type | solution.py:52
  131.6 4.9 %reshape.128 = f32[512,1536]{1,0:T(8,128)} reshape(f32[2,64,4,1536]{3,2,1,0:T(4,128)} %copy.68) | data formatting | bytes 6291456 | tf_op jit(solution)/shard_map/convert_element_type | solution.py:52
  136.6 3.0 multiply_reduce_fusion.1
  139.9 3.9 %multiply_convert_fusion.1 = bf16[512,4,384]{2,1,0:T(4,128)(2,1)} fusion(f32[512,4,384]{2,1,0:T(4,128)S(1)} %copy-done.5, f32[512,4,384]{2,1,0:T(4,128)} %reshape.127, f32[4,384]{1,0:T(4,128)S(1)} %copy-done.8, f32[512]{0:T(512)S(1)} %add_rsqrt_fusion.2), kind=kLoop, calls=%fused_computation.42 | loop fusion | flops 3145728 | bytes 7872512 | tf_op jit(solution)/shard_map/convert_element_type | solution.py:17
  143.8 8.8 %fusion.18 = f32[4,512,384]{1,2,0:T(8,128)} fusion(bf16[1,4,1024,384]{3,2,1,0:T(8,128)(2,1)S(1)} %copy-done, bf16[1,4,384,1024]{3,2,1,0:T(8,128)(2,1)} %param.14, bf16[512,4,384]{2,1,0:T(4,128)(2,1)} %multiply_convert_fusion.1), kind=kOutput, calls=%fused_computation.22 | convolution fusion | flops 3240099840 | bytes 11010048 | tf_op jit(solution)/shard_map/shb,hbl->shl/dot_general | solution.py:28
  152.6 3.5 %copy.74 = f32[512,1536]{1,0:T(8,128)} copy(f32[512,1536]{0,1:T(8,128)} %bitcast.85) | data formatting | bytes 6291456 | tf_op jit(solution)/shard_map/reshape | solution.py:31
  156.1 5.2 %add_convert_fusion.1 = bf16[512,1536]{1,0:T(8,128)(2,1)} fusion(f32[512,1536]{1,0:T(8,128)} %copy.74, f32[512,1536]{1,0:T(8,128)} %reshape.128, bf16[1,512,1536]{2,1,0:T(8,128)(2,1)} %param.8), kind=kLoop, calls=%fused_computation.40 | loop fusion | flops 3145728 | bytes 9437184 | tf_op jit(solution)/shard_map/convert_element_type | solution.py:31
  161.3 4.3 %collective-permute-start = (bf16[512,1536]{1,0:T(8,128)(2,1)}, bf16[512,1536]{1,0:T(8,128)(2,1)}, u32[]{:S(2)}, u32[]{:S(2)}) collective-permute-start(bf16[512,1536]{1,0:T(8,128)(2,1)} %add_convert_fusion.1), channel_id=1, source_target_pairs={{0,64},{64,128},{128,192},{1,65},{65,129},{129,193},{2,66},{66,130... | collective-permute-start | bytes 4718600 | tf_op jit(solution)/shard_map/ppermute | solution.py:12
  165.7 32.8 %collective-permute-done = bf16[512,1536]{1,0:T(8,128)(2,1)} collective-permute-done((bf16[512,1536]{1,0:T(8,128)(2,1)}, bf16[512,1536]{1,0:T(8,128)(2,1)}, u32[]{:S(2)}, u32[]{:S(2)}) %collective-permute-start) | collective-permute-done | bytes 1572896 | tf_op jit(solution)/shard_map/ppermute | solution.py:12
  204.0 4.9 %copy.76 = bf16[2,256,1536]{2,0,1:T(2,128)(2,1)} copy(bf16[2,256,1536]{1,2,0:T(8,128)(2,1)} %fusion.32) | data formatting | bytes 3145728 | tf_op jit(solution)/shard_map/convert_element_type | solution.py:48
  208.9 46.3 %all_to_all.55 = bf16[2,256,1536]{2,0,1:T(2,128)(2,1)S(1)} all-to-all(bf16[2,256,1536]{2,0,1:T(2,128)(2,1)} %copy.76), channel_id=1, replica_groups=mesh['section'=4,'seq'=64] {'seq'}, dimensions={1} | all-to-all | bytes 3145728 | tf_op jit(solution)/shard_map/all_to_all | solution.py:49
  257.7 4.0 %copy.79 = bf16[128,4,1536]{2,1,0:T(4,128)(2,1)} copy(bf16[128,4,1536]{0,2,1:T(8,128)(2,1)} %fusion.33) | data formatting | bytes 3145728 | tf_op jit(solution)/shard_map/convert_element_type | solution.py:37
  261.6 6.3 %all-to-all-start.3 = ((bf16[128,4,1536]{2,1,0:T(4,128)(2,1)}), bf16[128,4,1536]{2,1,0:T(4,128)(2,1)}, u32[]{:S(2)}, u32[]{:S(2)}) async-start(bf16[128,4,1536]{2,1,0:T(4,128)(2,1)} %copy.79), calls=%async_computation.3 | async-start | bytes 3145728 | tf_op jit(solution)/shard_map/all_to_all | solution.py:51
  267.9 5.0 %reshape.125 = f32[1,512,1536]{2,1,0:T(8,128)} reshape(f32[2,64,4,1536]{3,2,1,0:T(4,128)} %copy.68) | data formatting | bytes 6291456 | tf_op jit(solution)/shard_map/convert_element_type | solution.py:52
  272.9 3.5 %copy.73 = f32[1,512,1536]{2,1,0:T(8,128)} copy(f32[1,512,1536]{1,2,0:T(8,128)} %bitcast.86) | data formatting | bytes 6291456 | tf_op jit(solution)/shard_map/reshape | solution.py:31
  276.4 5.2 %add_convert_fusion.2 = bf16[1,512,1536]{2,1,0:T(8,128)(2,1)} fusion(f32[1,512,1536]{2,1,0:T(8,128)} %copy.73, f32[1,512,1536]{2,1,0:T(8,128)} %reshape.125, bf16[1,512,1536]{2,1,0:T(8,128)(2,1)} %param.8), kind=kLoop, calls=%fused_computation.41 | loop fusion | flops 3145728 | bytes 9437184 | tf_op jit(solution)/shard_map/convert_element_type | solution.py:31
  281.7 26.0 %all-to-all-done.3 = bf16[128,4,1536]{2,1,0:T(4,128)(2,1)} async-done(((bf16[128,4,1536]{2,1,0:T(4,128)(2,1)}), bf16[128,4,1536]{2,1,0:T(4,128)(2,1)}, u32[]{:S(2)}, u32[]{:S(2)}) %all-to-all-start.3) | async-done | bytes 1572896 | tf_op jit(solution)/shard_map/all_to_all | solution.py:51
  311.9 4.9 %reshape.129 = f32[512,1536]{1,0:T(8,128)} reshape(f32[2,64,4,1536]{3,2,1,0:T(4,128)} %copy.80) | data formatting | bytes 6291456 | tf_op jit(solution)/shard_map/convert_element_type | solution.py:52
  316.8 3.0 multiply_reduce_fusion
  322.2 7.8 %fusion.16 = f32[4,512,384]{1,2,0:T(8,128)} fusion(bf16[1,4,1024,384]{3,2,1,0:T(8,128)(2,1)S(1)} %copy-done, bf16[1,4,384,1024]{3,2,1,0:T(8,128)(2,1)} %param.14, bf16[64,4,8,384]{3,2,1,0:T(8,128)(2,1)} %bitcast.94), kind=kOutput, calls=%fused_computation.21 | convolution fusion | flops 3240099840 | bytes 11010048 | tf_op jit(solution)/shard_map/shb,hbl->shl/dot_general | solution.py:28
  329.9 3.6 %copy.83 = f32[512,1536]{1,0:T(8,128)} copy(f32[512,1536]{0,1:T(8,128)} %bitcast.93) | data formatting | bytes 6291456 | tf_op jit(solution)/shard_map/reshape | solution.py:31
  333.5 5.2 %fusion.42 = bf16[1,512,1536]{2,1,0:T(8,128)(2,1)} fusion(f32[512,1536]{1,0:T(8,128)} %copy.83, f32[512,1536]{1,0:T(8,128)} %reshape.129, bf16[512,1536]{1,0:T(8,128)(2,1)} %copy-done.3), kind=kLoop, calls=%fused_computation.53 | loop fusion | flops 3145728 | bytes 9437184 | tf_op jit(solution)/shard_map/broadcast_in_dim | solution.py:83
  (40 shorter events, 21.2 us)
Async XLA Ops:
  0.6 143.2 %copy-start = (bf16[1,4,1024,384]{3,2,1,0:T(8,128)(2,1)S(1)}, bf16[1,4,1024,384]{3,2,1,0:T(8,128)(2,1)}, u32[]{:S(2)}) copy-start(bf16[1,4,1024,384]{3,2,1,0:T(8,128)(2,1)} %param.15) | copy-start | bytes 9437188
  0.6 3.7 %copy-start.1 = (bf16[1,512,1536]{2,1,0:T(8,128)(2,1)S(1)}, bf16[1,512,1536]{2,1,0:T(8,128)(2,1)}, u32[]{:S(2)}) copy-start(bf16[1,512,1536]{2,1,0:T(8,128)(2,1)} %param.8) | copy-start | bytes 4718596
  4.7 3.7 %copy-start.9 = (f32[1,1536]{1,0:T(1,128)S(1)}, f32[1,1536]{1,0:T(1,128)}, u32[]{:S(2)}) copy-start(f32[1,1536]{1,0:T(1,128)} %param.10) | copy-start | bytes 18436
  4.7 3.7 %copy-start.6 = (bf16[1,2,256,256]{3,2,1,0:T(8,128)(2,1)S(1)}, bf16[1,2,256,256]{3,2,1,0:T(8,128)(2,1)}, u32[]{:S(2)}) copy-start(bf16[1,2,256,256]{3,2,1,0:T(8,128)(2,1)} %param.11) | copy-start | bytes 786436
  17.0 53.5 %copy-start.7 = (bf16[1,4,128,128]{3,2,1,0:T(8,128)(2,1)S(1)}, bf16[1,4,128,128]{3,2,1,0:T(8,128)(2,1)}, u32[]{:S(2)}) copy-start(bf16[1,4,128,128]{3,2,1,0:T(8,128)(2,1)} %param.12) | copy-start | bytes 393220
  76.2 46.0 %all-to-all-start.1 = ((bf16[128,4,1536]{2,1,0:T(4,128)(2,1)}), bf16[128,4,1536]{2,1,0:T(4,128)(2,1)}, u32[]{:S(2)}, u32[]{:S(2)}) async-start(bf16[128,4,1536]{2,1,0:T(4,128)(2,1)} %copy.67), calls=%async_computation.1 | async-start | bytes 3145728 | tf_op jit(solution)/shard_map/all_to_all | solution.py:51
  136.6 3.3 copy-start.5
  136.6 3.3 copy-start.8
  161.3 37.1 %collective-permute-start = (bf16[512,1536]{1,0:T(8,128)(2,1)}, bf16[512,1536]{1,0:T(8,128)(2,1)}, u32[]{:S(2)}, u32[]{:S(2)}) collective-permute-start(bf16[512,1536]{1,0:T(8,128)(2,1)} %add_convert_fusion.1), channel_id=1, source_target_pairs={{0,64},{64,128},{128,192},{1,65},{65,129},{129,193},{2,66},{66,130... | collective-permute-start | bytes 4718600 | tf_op jit(solution)/shard_map/ppermute | solution.py:12
  200.5 1.2 copy-start.3
  261.6 46.0 %all-to-all-start.3 = ((bf16[128,4,1536]{2,1,0:T(4,128)(2,1)}), bf16[128,4,1536]{2,1,0:T(4,128)(2,1)}, u32[]{:S(2)}, u32[]{:S(2)}) async-start(bf16[128,4,1536]{2,1,0:T(4,128)(2,1)} %copy.79), calls=%async_computation.3 | async-start | bytes 3145728 | tf_op jit(solution)/shard_map/all_to_all | solution.py:51
  316.8 3.3 copy-start.2
  316.8 3.8 %copy-start.4 = (bf16[512,1536]{1,0:T(8,128)(2,1)S(1)}, bf16[512,1536]{1,0:T(8,128)(2,1)}, u32[]{:S(2)}) copy-start(bf16[512,1536]{1,0:T(8,128)(2,1)} %copy-done.3) | copy-start | bytes 4718596
where the time goes:
time: 340 us; the launch traced here: 339 us
  blocking collectives  99.2 us (29%)
  waiting for transfers between devices  92.9 us (27%)
  local copies, waits for them, and re-layouts  64.1 us (19%)
  other arithmetic  39.1 us (12%)
  matrix products  25.8 us (8%)
  starting transfers between devices  16.9 us (5%)
    all_to_all x2, blocking collectives, apply_layer(): lax.all_to_all(within, 'seq', split_axis=1, concat_axis=0, tiled=True)  99.2 us
    all_to_all x2, waiting for transfers between devices, apply_layer(): lax.all_to_all(across, 'seq', split_axis=0, concat_axis=1, tiled=True)  60.1 us
    ppermute x1, waiting for transfers between devices, from_behind(): lax.ppermute(value, axis, [(source, source + steps) for source in range(l...  32.8 us
    convert_element_type x6, local copies, waits for them, and re-layouts, apply_layer(): restored.reshape(token_count, channels).astype(jnp.float32)  23.8 us
    dot_general x2, matrix products, channel_mixing(): jnp.einsum('shb,hbl->shl', gelu_activations, down_matrices, preferred_ele...  16.5 us
    all_to_all x2, starting transfers between devices, apply_layer(): lax.all_to_all(across, 'seq', split_axis=0, concat_axis=1, tiled=True)  12.6 us
    reshape x3, local copies, waits for them, and re-layouts, channel_mixing(): reduced_hidden.reshape(token_count, channels)  10.6 us
    convert_element_type x2, other arithmetic, channel_mixing(): (residual + reduced_hidden.reshape(token_count, channels)).astype(jnp.bfl...  10.5 us
  transfers between devices with their start and end apart: 3, of which 3 were waited for; matrix products, arithmetic and copies ran while one was open for 6% of the time, Pallas kernels for 0%

commit v1 on v0

v1 whole, which is shorter than its diff:
```python
import functools

import jax
import jax.numpy as jnp
from jax import lax
from jax.experimental import pallas as pl
from jax.experimental.pallas import tpu as pltpu
from jax.sharding import PartitionSpec as P

EPS = 1e-05
D = 1536
HALF = D // 2
BLK = 256
DEV = 64
GROUPS = 4
BF = jnp.bfloat16
F32 = jnp.float32


def call(kernel, out_shape, flops, bytes_accessed, transcendentals=0):
    return pl.pallas_call(
        kernel,
        out_shape=out_shape,
        cost_estimate=pl.CostEstimate(
            flops=flops, bytes_accessed=bytes_accessed, transcendentals=transcendentals
        ),
        compiler_params=pltpu.CompilerParams(vmem_limit_bytes=40 * 1024 * 1024),
    )


def dot(a, b):
    return jnp.dot(a, b, preferred_element_type=F32)


def normalize(values, gain):
    scale = lax.rsqrt(jnp.mean(values * values, axis=-1, keepdims=True) + EPS)
    return (values * scale * gain).astype(BF)


def packer(h):
    row = lax.broadcasted_iota(jnp.int32, (2 * BLK, BLK), 0)
    col = lax.broadcasted_iota(jnp.int32, (2 * BLK, BLK), 1)
    hit = ((row // 8) * 4 + row % 4 == col) & ((row % 8) // 4 == h)
    return jnp.where(hit, 1.0, 0.0).astype(BF)


def unpacker(h):
    row = lax.broadcasted_iota(jnp.int32, (BLK, 2 * BLK), 0)
    col = lax.broadcasted_iota(jnp.int32, (BLK, 2 * BLK), 1)
    hit = ((col // 8) * 4 + col % 4 == row) & ((col % 8) // 4 == h)
    return jnp.where(hit, 1.0, 0.0).astype(BF)


def within_of(x, gain, factor):
    normed = normalize(x, gain)
    mixed = dot(factor, normed).astype(BF)
    packed = dot(packer(0), mixed[:, :HALF]) + dot(packer(1), mixed[:, HALF:])
    return packed.astype(BF).reshape(DEV, 8, HALF)


def first_kernel(x_ref, gain_ref, factor_ref, out_ref):
    for b in range(2):
        x = x_ref[b * BLK : (b + 1) * BLK, :].astype(F32)
        out_ref[:, b] = within_of(x, gain_ref[...], factor_ref[b])


def later_kernel(b, flag_ref, x_ref, queued_ref, gain_ref, factor_ref, out_ref, entering_ref):
    x = jnp.where(flag_ref[0] == 0, queued_ref[b * BLK : (b + 1) * BLK, :], x_ref[...])
    entering_ref[...] = x
    out_ref[...] = within_of(x.astype(F32), gain_ref[...], factor_ref[b])


def spread_kernel(cross_ref, out_ref):
    n = 2 * BLK
    row = lax.broadcasted_iota(jnp.int32, (n, n), 0)
    col = lax.broadcasted_iota(jnp.int32, (n, n), 1)
    same = row % 8 == col % 8
    cross = cross_ref[...].reshape(n, 128)
    crow = lax.broadcasted_iota(jnp.int32, (128, n), 0)
    ccol = lax.broadcasted_iota(jnp.int32, (128, n), 1)
    for to in range(2):
        pick = col == (row % 4) * 128 + (row // 8) * 2 + to
        rows = dot(jnp.where(pick, 1.0, 0.0).astype(BF), cross).astype(BF)
        for b in range(2):
            pick = crow == (ccol // 8) * 2 + b
            full = dot(rows, jnp.where(pick, 1.0, 0.0).astype(BF))
            out_ref[to, b] = jnp.where(same, full, 0.0).astype(BF)


def cross_joint_kernel(to, spread_ref, r_ref, out_ref):
    total = dot(spread_ref[to, 0], r_ref[:, 0].reshape(2 * BLK, HALF))
    total += dot(spread_ref[to, 1], r_ref[:, 1].reshape(2 * BLK, HALF))
    out_ref[...] = total.astype(BF).reshape(DEV, 8, HALF)


def cross_both_kernel(spread_ref, r0_ref, r1_ref, out_ref):
    for to in range(2):
        total = dot(spread_ref[to, 0], r0_ref[...].reshape(2 * BLK, HALF))
        total += dot(spread_ref[to, 1], r1_ref[...].reshape(2 * BLK, HALF))
        out_ref[:, to] = total.astype(BF).reshape(DEV, 8, HALF)


def channel_rows(x, packed, gain, up_ref, down_ref, store):
    packed = packed.reshape(2 * BLK, HALF)
    across = jnp.concatenate([dot(unpacker(0), packed), dot(unpacker(1), packed)], axis=1)
    residual = x.astype(F32) + across
    normed = normalize(residual, gain)
    width = D // GROUPS
    for g in range(GROUPS):
        part = slice(g * width, (g + 1) * width)
        hidden = dot(normed[:, part], up_ref[g])
        act = jax.nn.gelu(hidden, approximate=True).astype(BF)
        store(part, (residual[:, part] + dot(act, down_ref[g])).astype(BF))


def channel_kernel(b, x_ref, packed_ref, gain_ref, up_ref, down_ref, out_ref):
    def store(part, value):
        out_ref[:, part] = value

    x = x_ref[b * BLK : (b + 1) * BLK, :]
    channel_rows(x, packed_ref[...], gain_ref[...], up_ref, down_ref, store)


def channel_both_kernel(x0_ref, x1_ref, packed_ref, gain_ref, up_ref, down_ref, out_ref):
    for b, x_ref in enumerate((x0_ref, x1_ref)):

        def store(part, value):
            out_ref[b * BLK : (b + 1) * BLK, part] = value

        channel_rows(x_ref[...], packed_ref[:, b], gain_ref[...], up_ref, down_ref, store)


def shape(*dims):
    return jax.ShapeDtypeStruct(dims, BF)


def exchange(value):
    return lax.all_to_all(value, "seq", split_axis=0, concat_axis=0, tiled=True)


def per_device(arriving, queued, norm_gain, block_factor, cross_factor, channel_gain, up, down):
    section = lax.axis_index("section")
    flag = jnp.full((1,), section, jnp.int32)
    x = arriving[0]
    factor, cross, up, down = block_factor[0], cross_factor[0], up[0], down[0]
    count = lax.axis_size("section")
    ahead = [(s, s + 1) for s in range(count - 1)]

    sent = call(first_kernel, shape(DEV, 2, 8, HALF), 1_200_000_000, 4_000_000)(
        x, norm_gain, factor
    )
    columns = exchange(sent)
    spread = call(spread_kernel, shape(2, 2, 2 * BLK, 2 * BLK), 500_000_000, 2_300_000)(cross)

    back = []
    for to in range(2):
        out = call(
            functools.partial(cross_joint_kernel, to), shape(DEV, 8, HALF), 800_000_000, 4_000_000
        )(spread, columns)
        back.append(exchange(out))

    firsts, entering, columns = [], [], []
    for b in range(2):
        first = call(
            functools.partial(channel_kernel, b), shape(BLK, D), 2_000_000_000, 9_000_000, 1_000_000
        )(x, back[b], channel_gain, up, down)
        firsts.append(first)
        received = lax.ppermute(first, "section", ahead)
        specs = [pl.BlockSpec(memory_space=pltpu.SMEM)] + [
            pl.BlockSpec(memory_space=pltpu.VMEM)
        ] * 4
        sent, enters = pl.pallas_call(
            functools.partial(later_kernel, b),
            out_shape=(shape(DEV, 8, HALF), shape(BLK, D)),
            in_specs=specs,
            cost_estimate=pl.CostEstimate(
                flops=600_000_000, bytes_accessed=4_000_000, transcendentals=0
            ),
            compiler_params=pltpu.CompilerParams(vmem_limit_bytes=40 * 1024 * 1024),
        )(flag, received, queued, norm_gain, factor)
        entering.append(enters)
        columns.append(exchange(sent))

    out = call(cross_both_kernel, shape(DEV, 2, 8, HALF), 1_600_000_000, 5_000_000)(
        spread, columns[0], columns[1]
    )
    packed = exchange(out)
    second = call(channel_both_kernel, shape(2 * BLK, D), 4_000_000_000, 11_000_000, 2_000_000)(
        entering[0], entering[1], packed, channel_gain, up, down
    )
    return jnp.concatenate(firsts, axis=0)[None], second[None]


def solution(mesh):
    placed = (
        P("section", "seq", None),
        P("seq", None),
        P("section", None),
        P("section", "seq", None, None),
        P("section", "seq", None, None),
        P("section", None),
        P("section", None, None, None),
        P("section", None, None, None),
    )
    return jax.shard_map(
        per_device,
        mesh=mesh,
        in_specs=placed,
        out_specs=(P("section", "seq", None), P("section", "seq", None)),
        check_vma=False,
    )
```

time: 340 us -> 279 us (0.82)
  blocking collectives: 99.2 us -> 34.1 us
  local copies, waits for them, and re-layouts: 64.1 us -> 26.5 us
  other arithmetic: 39.1 us -> 2.77 us
  starting transfers between devices: 16.9 us -> 51.6 us
  waiting for transfers between devices: 92.9 us -> 127 us
  Pallas kernels: 0 us -> 33.9 us
  matrix products: 25.8 us -> 0 us
    all_to_all x2 -> x1, blocking collectives: 99.2 us -> 34.1 us  [exchange(): return lax.all_to_all(value, 'seq', split_axis=0, concat_axis=0, tiled=True)]
    convert_element_type x12 -> x0, local copies, waits for them, and re-layouts: 49.4 us -> none  [the longest x6 23.8 us: apply_layer(): restored.reshape(token_count, channels).astype(jnp.float32)]
    all_to_all x2 -> x5, waiting for transfers between devices: 60.1 us -> 94.9 us  [exchange(): return lax.all_to_all(value, 'seq', split_axis=0, concat_axis=0, tiled=True)]
    pallas_call x0 -> x10, Pallas kernels: none -> 33.9 us  [the longest x1 9.26 us: per_device(): call(channel_both_kernel, shape(2 * BLK, D), 4000000000, 11000000, 2000000)]
    all_to_all x2 -> x5, starting transfers between devices: 12.6 us -> 43.4 us  [exchange(): return lax.all_to_all(value, 'seq', split_axis=0, concat_axis=0, tiled=True)]
    dot_general x6 -> x0, matrix products: 25.8 us -> none  [the longest x2 16.5 us: channel_mixing(): jnp.einsum('shb,hbl->shl', gelu_activations, down_matrices, preferred_ele...]
    convert_element_type x8 -> x0, other arithmetic: 24.7 us -> none  [the longest x2 10.5 us: channel_mixing(): (residual + reduced_hidden.reshape(token_count, channels)).astype(jnp.bfl...]
    unnamed x20 -> x54, local copies, waits for them, and re-layouts: 2.27 us -> 26.5 us
  transfers between devices with their start and end apart: 3 -> 7, of which waited for: 3 -> 5; matrix products, arithmetic and copies ran while one was open for 6% -> 1% of each run, Pallas kernels for 0% -> 6%
where the time goes in v1:
time: 279 us; the launch traced here: 277 us
  waiting for transfers between devices  127 us (46%)
  starting transfers between devices  51.6 us (18%)
  blocking collectives  34.1 us (12%)
  Pallas kernels  33.9 us (12%)
  local copies, waits for them, and re-layouts  26.5 us (9%)
    all_to_all x5, waiting for transfers between devices, exchange(): return lax.all_to_all(value, 'seq', split_axis=0, concat_axis=0, tiled=True)  94.9 us
    all_to_all x5, starting transfers between devices, exchange(): return lax.all_to_all(value, 'seq', split_axis=0, concat_axis=0, tiled=True)  43.4 us
    all_to_all x1, blocking collectives, exchange(): return lax.all_to_all(value, 'seq', split_axis=0, concat_axis=0, tiled=True)  34.1 us
    ppermute x2, waiting for transfers between devices, per_device(): received = lax.ppermute(first, 'section', ahead)  32.5 us
    unnamed x54, local copies, waits for them, and re-layouts  26.5 us
    pallas_call x1, Pallas kernels, per_device(): call(channel_both_kernel, shape(2 * BLK, D), 4000000000, 11000000, 2000000)  9.26 us
    pallas_call x2, Pallas kernels, per_device(): call(functools.partial(channel_kernel, b), shape(BLK, D), 2000000000, 900...  8.73 us
    ppermute x2, starting transfers between devices, per_device(): received = lax.ppermute(first, 'section', ahead)  8.22 us
  transfers between devices with their start and end apart: 7, of which 5 were waited for; matrix products, arithmetic and copies ran while one was open for 1% of the time, Pallas kernels for 6%

profile of v1, /device:TPU:1, one launch (start us, length us, event | category | flops | bytes accessed | tf_op | source)
XLA Modules:
  0.0 277.2 jit_solution(6379283874633500090)
XLA Ops:
  0.6 1.4 copy-done.6
  3.7 3.2 %shard_map.96 = bf16[64,2,8,768]{3,2,1,0:T(8,128)(2,1)} custom-call(bf16[512,1536]{1,0:T(8,128)(2,1)S(1)} %bitcast.15, f32[1,1536]{1,0:T(1,128)S(1)} %copy-done.20, bf16[2,256,256]{2,1,0:T(8,128)(2,1)S(1)} %bitcast.18), custom_call_target="tpu_custom_call" | custom-call | flops 1200000000 | bytes 4000000 | tf_op jit(solution)/shard_map/pallas_call | solution.py:149
  6.9 13.3 %all-to-all-start = ((bf16[64,2,8,768]{3,2,1,0:T(8,128)(2,1)}), bf16[64,2,8,768]{3,2,1,0:T(8,128)(2,1)}, u32[]{:S(2)}, u32[]{:S(2)}) async-start(bf16[64,2,8,768]{3,2,1,0:T(8,128)(2,1)} %shard_map.96), calls=%async_computation | async-start | bytes 3145728 | tf_op jit(solution)/shard_map/all_to_all | solution.py:138
  20.2 1.5 shard_map.95.spread_ref
  21.7 38.2 %all-to-all-done.r_ref = bf16[64,2,8,768]{3,2,1,0:T(8,128)(2,1)} async-done(((bf16[64,2,8,768]{3,2,1,0:T(8,128)(2,1)}), bf16[64,2,8,768]{3,2,1,0:T(8,128)(2,1)}, u32[]{:S(2)}, u32[]{:S(2)}) %all-to-all-start) | async-done | bytes 1572896 | tf_op jit(solution)/shard_map/all_to_all | solution.py:138
  60.0 2.4 shard_map.99
  63.2 6.1 %all-to-all-start.2 = ((bf16[64,8,768]{2,1,0:T(8,128)(2,1)}), bf16[64,8,768]{2,1,0:T(8,128)(2,1)S(1)}, u32[]{:S(2)}, u32[]{:S(2)}) async-start(bf16[64,8,768]{2,1,0:T(8,128)(2,1)} %copy-done.14), calls=%async_computation.2 | async-start | bytes 1572864 | tf_op jit(solution)/shard_map/all_to_all | solution.py:138
  69.4 2.4 shard_map.97
  72.6 19.7 %all-to-all-done.2.packed_ref = bf16[64,8,768]{2,1,0:T(8,128)(2,1)S(1)} async-done(((bf16[64,8,768]{2,1,0:T(8,128)(2,1)}), bf16[64,8,768]{2,1,0:T(8,128)(2,1)S(1)}, u32[]{:S(2)}, u32[]{:S(2)}) %all-to-all-start.2) | async-done | bytes 786464 | tf_op jit(solution)/shard_map/all_to_all | solution.py:138
  93.2 6.2 %all-to-all-start.1 = ((bf16[64,8,768]{2,1,0:T(8,128)(2,1)}), bf16[64,8,768]{2,1,0:T(8,128)(2,1)S(1)}, u32[]{:S(2)}, u32[]{:S(2)}) async-start(bf16[64,8,768]{2,1,0:T(8,128)(2,1)} %copy-done.13), calls=%async_computation.1 | async-start | bytes 1572864 | tf_op jit(solution)/shard_map/all_to_all | solution.py:138
  99.4 1.9 copy-done
  101.3 1.9 copy-done.3
  103.2 1.4 copy-done.7
  105.8 4.4 %shard_map.100 = bf16[256,1536]{1,0:T(8,128)(2,1)} custom-call(bf16[512,1536]{1,0:T(8,128)(2,1)S(1)} %bitcast.16, bf16[64,8,768]{2,1,0:T(8,128)(2,1)S(1)} %copy-done.12, f32[1,1536]{1,0:T(1,128)S(1)} %copy-done.22, bf16[4,384,1024]{2,1,0:T(8,128)(2,1)S(1)} %bitcast.9, bf16[4,1024,384]{2,1,0:T(8,128)(2,1)S(1)} %bitcast.12), custom_call_target="tpu_custom_call" | custom-call | flops 2000000000 | bytes 9000000 | tf_op jit(solution)/shard_map/pallas_call | solution.py:164
  110.1 4.1 %collective-permute-start.1 = (bf16[256,1536]{1,0:T(8,128)(2,1)}, bf16[256,1536]{1,0:T(8,128)(2,1)}, u32[]{:S(2)}, u32[]{:S(2)}) collective-permute-start(bf16[256,1536]{1,0:T(8,128)(2,1)} %shard_map.100), channel_id=1, source_target_pairs={{0,64},{64,128},{128,192},{1,65},{65,129},{129,193},{2,66},{66,130... | collective-permute-start | bytes 2359304 | tf_op jit(solution)/shard_map/ppermute | solution.py:168
  114.2 15.9 %collective-permute-done.1.x_ref = bf16[256,1536]{1,0:T(8,128)(2,1)} collective-permute-done((bf16[256,1536]{1,0:T(8,128)(2,1)}, bf16[256,1536]{1,0:T(8,128)(2,1)}, u32[]{:S(2)}, u32[]{:S(2)}) %collective-permute-start.1) | collective-permute-done | bytes 786464 | tf_op jit(solution)/shard_map/ppermute | solution.py:168
  130.1 1.4 copy-done.9
  131.5 2.3 shard_map.102
  135.6 11.4 %all-to-all-start.4 = ((bf16[64,8,768]{2,1,0:T(8,128)(2,1)}), bf16[64,8,768]{2,1,0:T(8,128)(2,1)}, u32[]{:S(2)}, u32[]{:S(2)}) async-start(bf16[64,8,768]{2,1,0:T(8,128)(2,1)} %copy-done.18), calls=%async_computation.4 | async-start | bytes 1572864 | tf_op jit(solution)/shard_map/all_to_all | solution.py:138
  147.1 1.9 copy-done.1
  149.0 1.9 copy-done.4
  150.8 1.4 copy-done.8
  152.3 4.4 %shard_map.98 = bf16[256,1536]{1,0:T(8,128)(2,1)} custom-call(bf16[512,1536]{1,0:T(8,128)(2,1)S(1)} %bitcast.17, bf16[64,8,768]{2,1,0:T(8,128)(2,1)S(1)} %all-to-all-done.1.packed_ref, f32[1,1536]{1,0:T(1,128)S(1)} %copy-done.22, bf16[4,384,1024]{2,1,0:T(8,128)(2,1)S(1)} %bitcast.10, bf16[4,1024,384]{2,1,0:T(8,128)(2,1)S(1)} %bitcast.13), custom_call_target="tpu_custom_call" | custom-call | flops 2000000000 | bytes 9000000 | tf_op jit(solution)/shard_map/pallas_call | solution.py:164
  156.6 4.1 %collective-permute-start = (bf16[256,1536]{1,0:T(8,128)(2,1)}, bf16[256,1536]{1,0:T(8,128)(2,1)S(1)}, u32[]{:S(2)}, u32[]{:S(2)}) collective-permute-start(bf16[256,1536]{1,0:T(8,128)(2,1)} %shard_map.98), channel_id=1, source_target_pairs={{0,64},{64,128},{128,192},{1,65},{65,129},{129,193},{2,66},{66,130... | collective-permute-start | bytes 2359304 | tf_op jit(solution)/shard_map/ppermute | solution.py:168
  160.8 16.6 %collective-permute-done.x_ref = bf16[256,1536]{1,0:T(8,128)(2,1)S(1)} collective-permute-done((bf16[256,1536]{1,0:T(8,128)(2,1)}, bf16[256,1536]{1,0:T(8,128)(2,1)S(1)}, u32[]{:S(2)}, u32[]{:S(2)}) %collective-permute-start) | collective-permute-done | bytes 786464 | tf_op jit(solution)/shard_map/ppermute | solution.py:168
  179.5 34.1 %all_to_all.30.r0_ref = bf16[64,8,768]{2,1,0:T(8,128)(2,1)S(1)} all-to-all(bf16[64,8,768]{2,1,0:T(8,128)(2,1)S(1)} %get-tuple-element.8), channel_id=1, replica_groups=mesh['section'=4,'seq'=64] {'seq'}, dimensions={0} | all-to-all | bytes 1572864 | tf_op jit(solution)/shard_map/all_to_all | solution.py:138
  213.6 2.9 %shard_map.103 = bf16[64,2,8,768]{3,2,1,0:T(8,128)(2,1)S(1)} custom-call(bf16[2,2,512,512]{3,2,1,0:T(8,128)(2,1)S(1)} %shard_map.95.spread_ref, bf16[64,8,768]{2,1,0:T(8,128)(2,1)S(1)} %all_to_all.30.r0_ref, bf16[64,8,768]{2,1,0:T(8,128)(2,1)} %all-to-all-done.4.r1_ref), custom_call_target="tpu_custom_call" | custom-call | flops 1600000000 | bytes 5000000 | tf_op jit(solution)/shard_map/pallas_call | solution.py:184
  217.7 6.4 %all-to-all-start.5 = ((bf16[64,2,8,768]{3,2,1,0:T(8,128)(2,1)}), bf16[64,2,8,768]{3,2,1,0:T(8,128)(2,1)}, u32[]{:S(2)}, u32[]{:S(2)}) async-start(bf16[64,2,8,768]{3,2,1,0:T(8,128)(2,1)} %copy-done.15), calls=%async_computation.5 | async-start | bytes 3145728 | tf_op jit(solution)/shard_map/all_to_all | solution.py:138
  224.1 2.8 maximum_bitcast_fusion
  226.8 36.9 %all-to-all-done.5.packed_ref = bf16[64,2,8,768]{3,2,1,0:T(8,128)(2,1)} async-done(((bf16[64,2,8,768]{3,2,1,0:T(8,128)(2,1)}), bf16[64,2,8,768]{3,2,1,0:T(8,128)(2,1)}, u32[]{:S(2)}, u32[]{:S(2)}) %all-to-all-start.5) | async-done | bytes 1572896 | tf_op jit(solution)/shard_map/all_to_all | solution.py:138
  263.8 1.9 copy-done.5
  267.9 9.3 %shard_map.104 = bf16[512,1536]{1,0:T(8,128)(2,1)} custom-call(bf16[256,1536]{1,0:T(8,128)(2,1)S(1)} %copy-done.26, bf16[256,1536]{1,0:T(8,128)(2,1)S(1)} %copy-done.24, bf16[64,2,8,768]{3,2,1,0:T(8,128)(2,1)} %all-to-all-done.5.packed_ref, f32[1,1536]{1,0:T(1,128)S(1)} %copy-done.22, bf16[4,384,1024]{2,1,0:T(8,128)(2,1)S(1)} %bitcast.11, ...), custom_call_target="tpu_custom_call" | custom-call | flops 4000000000 | bytes 11000000 | tf_op jit(solution)/shard_map/pallas_call | solution.py:188
  (48 shorter events, 12.7 us)
Async XLA Ops:
  0.6 1.4 copy-start.6
  2.0 0.9 copy-start.16
  6.9 13.3 %copy-start.19 = (bf16[1,4,128,128]{3,2,1,0:T(8,128)(2,1)S(1)}, bf16[1,4,128,128]{3,2,1,0:T(8,128)(2,1)}, u32[]{:S(2)}) copy-start(bf16[1,4,128,128]{3,2,1,0:T(8,128)(2,1)} %param.12) | copy-start | bytes 393220
  6.9 53.0 %all-to-all-start = ((bf16[64,2,8,768]{3,2,1,0:T(8,128)(2,1)}), bf16[64,2,8,768]{3,2,1,0:T(8,128)(2,1)}, u32[]{:S(2)}, u32[]{:S(2)}) async-start(bf16[64,2,8,768]{3,2,1,0:T(8,128)(2,1)} %shard_map.96), calls=%async_computation | async-start | bytes 3145728 | tf_op jit(solution)/shard_map/all_to_all | solution.py:138
  62.3 0.9 copy-start.14
  63.2 29.1 %all-to-all-start.2 = ((bf16[64,8,768]{2,1,0:T(8,128)(2,1)}), bf16[64,8,768]{2,1,0:T(8,128)(2,1)S(1)}, u32[]{:S(2)}, u32[]{:S(2)}) async-start(bf16[64,8,768]{2,1,0:T(8,128)(2,1)} %copy-done.14), calls=%async_computation.2 | async-start | bytes 1572864 | tf_op jit(solution)/shard_map/all_to_all | solution.py:138
  71.8 0.9 copy-start.13
  72.6 26.8 %copy-start.22 = (f32[1,1536]{1,0:T(1,128)S(1)}, f32[1,1536]{1,0:T(1,128)}, u32[]{:S(2)}) copy-start(f32[1,1536]{1,0:T(1,128)} %gain_ref.11) | copy-start | bytes 18436
  92.3 0.9 copy-start.11
  93.2 42.4 %all-to-all-start.1 = ((bf16[64,8,768]{2,1,0:T(8,128)(2,1)}), bf16[64,8,768]{2,1,0:T(8,128)(2,1)S(1)}, u32[]{:S(2)}, u32[]{:S(2)}) async-start(bf16[64,8,768]{2,1,0:T(8,128)(2,1)} %copy-done.13), calls=%async_computation.1 | async-start | bytes 1572864 | tf_op jit(solution)/shard_map/all_to_all | solution.py:138
  99.4 1.9 copy-start
  101.3 1.9 copy-start.3
  103.2 1.4 copy-start.7
  104.6 1.1 copy-start.12
  105.8 24.3 %copy-start.17 = (bf16[1,2,256,256]{3,2,1,0:T(8,128)(2,1)S(1)}, bf16[1,2,256,256]{3,2,1,0:T(8,128)(2,1)}, u32[]{:S(2)}) copy-start(bf16[1,2,256,256]{3,2,1,0:T(8,128)(2,1)} %param.11) | copy-start | bytes 786436
  105.8 24.3 %copy-start.21 = (f32[1,1536]{1,0:T(1,128)S(1)}, f32[1,1536]{1,0:T(1,128)}, u32[]{:S(2)}) copy-start(f32[1,1536]{1,0:T(1,128)} %gain_ref.10) | copy-start | bytes 18436
  110.1 20.0 %collective-permute-start.1 = (bf16[256,1536]{1,0:T(8,128)(2,1)}, bf16[256,1536]{1,0:T(8,128)(2,1)}, u32[]{:S(2)}, u32[]{:S(2)}) collective-permute-start(bf16[256,1536]{1,0:T(8,128)(2,1)} %shard_map.100), channel_id=1, source_target_pairs={{0,64},{64,128},{128,192},{1,65},{65,129},{129,193},{2,66},{66,130... | collective-permute-start | bytes 2359304 | tf_op jit(solution)/shard_map/ppermute | solution.py:168
  130.1 1.4 copy-start.9
  133.8 0.9 copy-start.18
  134.7 0.9 copy-start.23
  135.6 43.9 %all-to-all-start.4 = ((bf16[64,8,768]{2,1,0:T(8,128)(2,1)}), bf16[64,8,768]{2,1,0:T(8,128)(2,1)}, u32[]{:S(2)}, u32[]{:S(2)}) async-start(bf16[64,8,768]{2,1,0:T(8,128)(2,1)} %copy-done.18), calls=%async_computation.4 | async-start | bytes 1572864 | tf_op jit(solution)/shard_map/all_to_all | solution.py:138
  147.1 1.9 copy-start.1
  149.0 1.9 copy-start.4
  150.8 1.4 copy-start.8
  152.3 25.2 %copy-start.10 = (bf16[512,1536]{1,0:T(8,128)(2,1)S(1)}, bf16[512,1536]{1,0:T(8,128)(2,1)}, u32[]{:S(2)}) copy-start(bf16[512,1536]{1,0:T(8,128)(2,1)} %queued_ref.3) | copy-start | bytes 4718596
  156.6 20.8 %collective-permute-start = (bf16[256,1536]{1,0:T(8,128)(2,1)}, bf16[256,1536]{1,0:T(8,128)(2,1)S(1)}, u32[]{:S(2)}, u32[]{:S(2)}) collective-permute-start(bf16[256,1536]{1,0:T(8,128)(2,1)} %shard_map.98), channel_id=1, source_target_pairs={{0,64},{64,128},{128,192},{1,65},{65,129},{129,193},{2,66},{66,130... | collective-permute-start | bytes 2359304 | tf_op jit(solution)/shard_map/ppermute | solution.py:168
  216.5 1.1 copy-start.15
  217.7 46.1 %all-to-all-start.5 = ((bf16[64,2,8,768]{3,2,1,0:T(8,128)(2,1)}), bf16[64,2,8,768]{3,2,1,0:T(8,128)(2,1)}, u32[]{:S(2)}, u32[]{:S(2)}) async-start(bf16[64,2,8,768]{3,2,1,0:T(8,128)(2,1)} %copy-done.15), calls=%async_computation.5 | async-start | bytes 3145728 | tf_op jit(solution)/shard_map/all_to_all | solution.py:138
  224.0 39.7 %copy-start.2 = (bf16[1,4,384,1024]{3,2,1,0:T(8,128)(2,1)S(1)}, bf16[1,4,384,1024]{3,2,1,0:T(8,128)(2,1)}, u32[]{:S(2)}) copy-start(bf16[1,4,384,1024]{3,2,1,0:T(8,128)(2,1)} %param.14) | copy-start | bytes 9437188
  263.8 1.9 copy-start.5
  265.7 1.1 copy-start.24
  266.8 1.1 copy-start.26
  (2 other events, 1.6 us)

commit v2 on v1

v2 whole, which is shorter than its diff:
```python
import functools

import jax
import jax.numpy as jnp
from jax import lax
from jax.experimental import pallas as pl
from jax.experimental.pallas import tpu as pltpu
from jax.sharding import PartitionSpec as P

EPS = 1e-05
D = 1536
HALF = D // 2
BLK = 256
DEV = 64
GROUPS = 4
BF = jnp.bfloat16
F32 = jnp.float32


def call(kernel, out_shape, flops, bytes_accessed, transcendentals=0, scalars=0, arrays=0):
    specs = None
    if scalars:
        specs = [pl.BlockSpec(memory_space=pltpu.SMEM)] * scalars
        specs += [pl.BlockSpec(memory_space=pltpu.VMEM)] * arrays
    return pl.pallas_call(
        kernel,
        out_shape=out_shape,
        **({"in_specs": specs} if specs else {}),
        cost_estimate=pl.CostEstimate(
            flops=flops, bytes_accessed=bytes_accessed, transcendentals=transcendentals
        ),
        compiler_params=pltpu.CompilerParams(vmem_limit_bytes=44 * 1024 * 1024),
    )


def dot(a, b):
    return jnp.dot(a, b, preferred_element_type=F32)


def onehot(rows, cols, hit):
    r = lax.broadcasted_iota(jnp.int32, (rows, cols), 0)
    c = lax.broadcasted_iota(jnp.int32, (rows, cols), 1)
    return jnp.where(hit(r, c), 1.0, 0.0).astype(BF)


def packed_at(r, j, c, h, b):
    return (((r >> 3) * 4 + 2 * c + (r & 1)) == j) & (((r >> 1) & 3) == 2 * h + b)


def pack(c, h, b):
    return onehot(2 * BLK, BLK, lambda r, j: packed_at(r, j, c, h, b))


def unpack(c, h, b):
    return onehot(BLK, 2 * BLK, lambda j, r: packed_at(r, j, c, h, b))


def unpack_compact(h):
    return onehot(
        BLK, 2 * BLK, lambda q, r: r == ((q & 127) >> 1) * 8 + 4 * h + 2 * (q >> 7) + (q & 1)
    )


def pick(c):
    return onehot(BLK // 2, BLK, lambda q, j: j == (q >> 1) * 4 + 2 * c + (q & 1))


def place(c):
    return onehot(BLK, BLK // 2, lambda j, q: j == (q >> 1) * 4 + 2 * c + (q & 1))


def normalize(values, gain):
    scale = lax.rsqrt(jnp.mean(values * values, axis=-1, keepdims=True) + EPS)
    return (values * scale * gain).astype(BF)


def packed_part(c, mixed):
    total = None
    for b in range(2):
        for h in range(2):
            term = dot(pack(c, h, b), mixed[b][:, h * HALF : (h + 1) * HALF])
            total = term if total is None else total + term
    return total.astype(BF).reshape(DEV, 8, HALF)


def first_kernel(x_ref, gain_ref, factor_ref, out_ref):
    mixed = []
    for b in range(2):
        x = x_ref[b * BLK : (b + 1) * BLK, :].astype(F32)
        mixed.append(dot(factor_ref[b], normalize(x, gain_ref[...])).astype(BF))
    for c in range(2):
        out_ref[:, c] = packed_part(c, mixed)


def spread_kernel(cross_ref, out_ref):
    n = 2 * BLK
    row = lax.broadcasted_iota(jnp.int32, (n, n), 0)
    col = lax.broadcasted_iota(jnp.int32, (n, n), 1)
    same = ((row ^ col) & 5) == 0
    cross = cross_ref[...].reshape(n, 128)
    columns = onehot(128, n, lambda m, k: m == (k >> 3) * 2 + ((k >> 1) & 1))
    for c in range(2):
        rows = onehot(
            n, n, lambda r, k: k == (2 * c + (r & 1)) * 128 + (r >> 3) * 2 + ((r >> 1) & 1)
        )
        full = dot(dot(rows, cross).astype(BF), columns)
        out_ref[c] = jnp.where(same, full, 0.0).astype(BF)


def cross_both_kernel(spread_ref, r_ref, out_ref):
    for c in range(2):
        total = dot(spread_ref[c], r_ref[:, c].reshape(2 * BLK, HALF))
        out_ref[:, c] = total.astype(BF).reshape(DEV, 8, HALF)


def cross_kernel(c, spread_ref, r_ref, out_ref):
    total = dot(spread_ref[c], r_ref[...].reshape(2 * BLK, HALF))
    out_ref[...] = total.astype(BF).reshape(DEV, 8, HALF)


def channel_rows(residual, gain, up_ref, down_ref, store):
    normed = normalize(residual, gain)
    width = D // GROUPS
    for g in range(GROUPS):
        part = slice(g * width, (g + 1) * width)
        hidden = dot(normed[:, part], up_ref[g])
        act = jax.nn.gelu(hidden, approximate=True).astype(BF)
        store(part, (residual[:, part] + dot(act, down_ref[g])).astype(BF))


def middle_kernel(
    flag_ref,
    x_ref,
    across_ref,
    channel_ref,
    up_ref,
    down_ref,
    queued_ref,
    gain_ref,
    factor_ref,
    first_ref,
    kept_ref,
    mixed_ref,
    out_ref,
):
    packed = [across_ref[:, c].reshape(2 * BLK, HALF) for c in range(2)]
    mixed = []
    for b in range(2):
        rows = slice(b * BLK, (b + 1) * BLK)
        across = jnp.concatenate(
            [dot(unpack(0, h, b), packed[0]) + dot(unpack(1, h, b), packed[1]) for h in range(2)],
            axis=1,
        )

        def store(part, value):
            first_ref[rows, part] = value

        residual = x_ref[rows, :].astype(F32) + across
        channel_rows(residual, channel_ref[...], up_ref, down_ref, store)
        first = first_ref[rows, :]
        kept_ref[b * (BLK // 2) : (b + 1) * (BLK // 2), :] = dot(pick(0), first).astype(BF)
        entering = jnp.where(flag_ref[1] == 1, queued_ref[rows, :], first)
        normed = normalize(entering.astype(F32), gain_ref[...])
        mixed.append(dot(factor_ref[b], normed).astype(BF))
        mixed_ref[rows, :] = mixed[b]
    out_ref[...] = packed_part(0, mixed)


def remainder_kernel(first_ref, mixed_ref, kept_ref, out_ref):
    mixed = [mixed_ref[b * BLK : (b + 1) * BLK, :] for b in range(2)]
    out_ref[...] = packed_part(1, mixed)
    for b in range(2):
        first = first_ref[b * BLK : (b + 1) * BLK, :]
        kept_ref[b * (BLK // 2) : (b + 1) * (BLK // 2), :] = dot(pick(1), first).astype(BF)


def last_rows(c, flag_ref, queued_ref, x_ref, across_ref, channel_ref, up_ref, down_ref, store):
    queued = [
        dot(pick(c), queued_ref[b * BLK : (b + 1) * BLK, :]).astype(BF) for b in range(2)
    ]
    x = jnp.where(flag_ref[0] == 1, jnp.concatenate(queued, axis=0), x_ref[...])
    packed = across_ref[...].reshape(2 * BLK, HALF)
    across = jnp.concatenate([dot(unpack_compact(h), packed) for h in range(2)], axis=1)
    channel_rows(x.astype(F32) + across, channel_ref[...], up_ref, down_ref, store)


def last_kernel(
    flag_ref, queued_ref, x_ref, across_ref, channel_ref, up_ref, down_ref, out_ref
):
    def store(part, value):
        out_ref[:, part] = value

    last_rows(
        0, flag_ref, queued_ref, x_ref, across_ref, channel_ref, up_ref, down_ref, store
    )


def final_kernel(
    flag_ref, queued_ref, x_ref, across_ref, channel_ref, up_ref, down_ref, other_ref, out_ref
):
    def store(part, value):
        for b in range(2):
            rows = slice(b * (BLK // 2), (b + 1) * (BLK // 2))
            joined = dot(place(0), other_ref[rows, part]) + dot(place(1), value[rows])
            out_ref[b * BLK : (b + 1) * BLK, part] = joined.astype(BF)

    last_rows(
        1, flag_ref, queued_ref, x_ref, across_ref, channel_ref, up_ref, down_ref, store
    )


def shape(*dims):
    return jax.ShapeDtypeStruct(dims, BF)


def exchange(value):
    return lax.all_to_all(value, "seq", split_axis=0, concat_axis=0, tiled=True)


def per_device(arriving, queued, norm_gain, block_factor, cross_factor, channel_gain, up, down):
    section = lax.axis_index("section")
    count = lax.axis_size("section")
    flags = jnp.stack([section == 0, section == count - 1]).astype(jnp.int32)
    x = arriving[0]
    factor, cross, up, down = block_factor[0], cross_factor[0], up[0], down[0]

    def ahead(value):
        return lax.ppermute(value, "section", [(s, (s + 1) % count) for s in range(count)])

    def behind(value):
        return lax.ppermute(value, "section", [((s + 1) % count, s) for s in range(count)])

    message = shape(DEV, 8, HALF)
    both = shape(DEV, 2, 8, HALF)
    sent = call(first_kernel, both, 2_000_000_000, 4_000_000)(x, norm_gain, factor)
    columns = exchange(sent)
    spread = call(spread_kernel, shape(2, 2 * BLK, 2 * BLK), 400_000_000, 1_300_000)(cross)
    next_gain, next_factor = behind(norm_gain), behind(factor)

    out = call(cross_both_kernel, both, 800_000_000, 4_000_000)(spread, columns)
    across = exchange(out)

    first, kept0, mixed, sent0 = call(
        middle_kernel,
        (shape(2 * BLK, D), shape(BLK, D), shape(2 * BLK, D), message),
        7_000_000_000,
        18_000_000,
        2_000_000,
        1,
        8,
    )(flags, x, across, channel_gain, up, down, queued, next_gain, next_factor)
    columns0 = exchange(sent0)
    kept1, sent1 = call(
        remainder_kernel, (shape(BLK, D), message), 1_000_000_000, 5_000_000
    )(first, mixed)
    x0 = ahead(kept0)
    columns1 = exchange(sent1)
    columns0 = ahead(columns0)
    out0 = call(functools.partial(cross_kernel, 0), message, 400_000_000, 2_000_000)(
        spread, columns0
    )
    across0 = exchange(out0)
    columns1 = ahead(columns1)
    out1 = call(functools.partial(cross_kernel, 1), message, 400_000_000, 2_000_000)(
        spread, columns1
    )
    kept1, out1 = lax.optimization_barrier((kept1, out1))
    x1 = ahead(kept1)
    across1 = exchange(out1)
    other = call(last_kernel, shape(BLK, D), 2_500_000_000, 10_000_000, 1_000_000, 1, 6)(
        flags, queued, x0, across0, channel_gain, up, down
    )
    second = call(final_kernel, shape(2 * BLK, D), 3_000_000_000, 11_000_000, 1_000_000, 1, 7)(
        flags, queued, x1, across1, channel_gain, up, down, other
    )
    return first[None], second[None]


def solution(mesh):
    placed = (
        P("section", "seq", None),
        P("seq", None),
        P("section", None),
        P("section", "seq", None, None),
        P("section", "seq", None, None),
        P("section", None),
        P("section", None, None, None),
        P("section", None, None, None),
    )
    return jax.shard_map(
        per_device,
        mesh=mesh,
        in_specs=placed,
        out_specs=(P("section", "seq", None), P("section", "seq", None)),
        check_vma=False,
    )
```

time: 279 us -> 282 us (1.011)
  blocking collectives: 34.1 us -> 0 us
  waiting for transfers between devices: 127 us -> 161 us
  starting transfers between devices: 51.6 us -> 58.9 us
  local copies, waits for them, and re-layouts: 26.5 us -> 23.6 us
    ppermute x2 -> x6, waiting for transfers between devices: 32.5 us -> 71 us  [the longest x4 66.2 us: ahead(): lax.ppermute(value, 'section', [(s, (s + 1) % count) for s in range(count)])]
    all_to_all x1 -> x0, blocking collectives: 34.1 us -> none  [exchange(): return lax.all_to_all(value, 'seq', split_axis=0, concat_axis=0, tiled=True)]
    all_to_all x5 -> x6, starting transfers between devices: 43.4 us -> 53.5 us  [exchange(): return lax.all_to_all(value, 'seq', split_axis=0, concat_axis=0, tiled=True)]
    all_to_all x5 -> x6, waiting for transfers between devices: 94.9 us -> 89.9 us  [exchange(): return lax.all_to_all(value, 'seq', split_axis=0, concat_axis=0, tiled=True)]
    unnamed x54 -> x56, local copies, waits for them, and re-layouts: 26.5 us -> 23.6 us
    ppermute x2 -> x6, starting transfers between devices: 8.22 us -> 5.42 us  [the longest x2 3.28 us: behind(): lax.ppermute(value, 'section', [((s + 1) % count, s) for s in range(count)])]
    pallas_call x10 -> x9, Pallas kernels: 33.9 us -> 36.1 us  [the longest x1 13.7 us: per_device(): call(middle_kernel, (shape(2 * BLK, D), shape(BLK, D), shape(2 * BLK, D),...]
  transfers between devices with their start and end apart: 7 -> 12, of which waited for: 5 -> 9; matrix products, arithmetic and copies ran while one was open for 1% -> 0% of each run, Pallas kernels for 6% -> 4%
where the time goes in v2:
time: 282 us; the launch traced here: 280 us
  waiting for transfers between devices  161 us (57%)
  starting transfers between devices  58.9 us (21%)
  Pallas kernels  36.1 us (13%)
  local copies, waits for them, and re-layouts  23.6 us (8%)
    all_to_all x6, waiting for transfers between devices, exchange(): return lax.all_to_all(value, 'seq', split_axis=0, concat_axis=0, tiled=True)  89.9 us
    ppermute x4, waiting for transfers between devices, ahead(): lax.ppermute(value, 'section', [(s, (s + 1) % count) for s in range(count)])  66.2 us
    all_to_all x6, starting transfers between devices, exchange(): return lax.all_to_all(value, 'seq', split_axis=0, concat_axis=0, tiled=True)  53.5 us
    unnamed x56, local copies, waits for them, and re-layouts  23.6 us
    pallas_call x1, Pallas kernels, per_device(): call(middle_kernel, (shape(2 * BLK, D), shape(BLK, D), shape(2 * BLK, D),...  13.7 us
    pallas_call x1, Pallas kernels, per_device(): call(final_kernel, shape(2 * BLK, D), 3000000000, 11000000, 1000000, 1, 7)  7.23 us
  transfers between devices with their start and end apart: 12, of which 9 were waited for; matrix products, arithmetic and copies ran while one was open for 0% of the time, Pallas kernels for 4%

profile of v2, /device:TPU:1, one launch (start us, length us, event | category | flops | bytes accessed | tf_op | source)
XLA Modules:
  0.0 280.3 jit_solution(17063024971014613045)
XLA Ops:
  0.6 1.4 copy-done.15
  3.7 2.7 shard_map.96
  7.6 13.1 %all-to-all-start = ((bf16[64,2,8,768]{3,2,1,0:T(8,128)(2,1)}), bf16[64,2,8,768]{3,2,1,0:T(8,128)(2,1)S(1)}, u32[]{:S(2)}, u32[]{:S(2)}) async-start(bf16[64,2,8,768]{3,2,1,0:T(8,128)(2,1)} %copy-done.11), calls=%async_computation | async-start | bytes 3145728 | tf_op jit(solution)/shard_map/all_to_all | solution.py:217
  20.7 1.3 shard_map.95.spread_ref
  22.0 38.5 %all-to-all-done.r_ref = bf16[64,2,8,768]{3,2,1,0:T(8,128)(2,1)S(1)} async-done(((bf16[64,2,8,768]{3,2,1,0:T(8,128)(2,1)}), bf16[64,2,8,768]{3,2,1,0:T(8,128)(2,1)S(1)}, u32[]{:S(2)}, u32[]{:S(2)}) %all-to-all-start) | async-done | bytes 1572896 | tf_op jit(solution)/shard_map/all_to_all | solution.py:217
  60.5 2.1 shard_map.97
  62.6 6.4 %all-to-all-start.1 = ((bf16[64,2,8,768]{3,2,1,0:T(8,128)(2,1)}), bf16[64,2,8,768]{3,2,1,0:T(8,128)(2,1)}, u32[]{:S(2)}, u32[]{:S(2)}) async-start(bf16[64,2,8,768]{3,2,1,0:T(8,128)(2,1)} %shard_map.97), calls=%async_computation.1 | async-start | bytes 3145728 | tf_op jit(solution)/shard_map/all_to_all | solution.py:217
  69.1 2.8 %collective-permute-start.1 = (bf16[2,256,256]{2,1,0:T(8,128)(2,1)S(1)}, bf16[2,256,256]{2,1,0:T(8,128)(2,1)S(1)}, u32[]{:S(2)}, u32[]{:S(2)}) collective-permute-start(bf16[2,256,256]{2,1,0:T(8,128)(2,1)S(1)} %bitcast.18), channel_id=1, source_target_pairs={{64,0},{128,64},{192,128},{0,192},{65,1},{129,65},{193,129},{1,193... | collective-permute-start | bytes 786440 | tf_op jit(solution)/shard_map/ppermute | solution.py:231
  72.4 4.7 %collective-permute-done.gain_ref = f32[1,1536]{1,0:T(1,128)S(1)} collective-permute-done((f32[1,1536]{1,0:T(1,128)S(1)}, f32[1,1536]{1,0:T(1,128)S(1)}, u32[]{:S(2)}, u32[]{:S(2)}) %collective-permute-start) | collective-permute-done | bytes 6176 | tf_op jit(solution)/shard_map/ppermute | solution.py:231
  77.2 31.6 %all-to-all-done.1.across_ref = bf16[64,2,8,768]{3,2,1,0:T(8,128)(2,1)} async-done(((bf16[64,2,8,768]{3,2,1,0:T(8,128)(2,1)}), bf16[64,2,8,768]{3,2,1,0:T(8,128)(2,1)}, u32[]{:S(2)}, u32[]{:S(2)}) %all-to-all-start.1) | async-done | bytes 1572896 | tf_op jit(solution)/shard_map/all_to_all | solution.py:217
  108.8 1.4 copy-done.16
  110.2 13.7 %shard_map.98 = (bf16[512,1536]{1,0:T(8,128)(2,1)}, bf16[256,1536]{1,0:T(8,128)(2,1)S(1)}, bf16[512,1536]{1,0:T(8,128)(2,1)S(1)}, bf16[64,8,768]{2,1,0:T(8,128)(2,1)}) custom-call(s32[2]{0:T(128)S(1)} %add_convert_fusion.flag_ref, bf16[512,1536]{1,0:T(8,128)(2,1)S(1)} %bitcast.16, bf16[64,2,8,768]{3,2,1,0:T(8,128)(2,1)} %all-to-all-done.1.across_ref, ...), custom_call_target="tpu_custom_call" | custom-call | flops 7000000000 | bytes 18000000 | tf_op jit(solution)/shard_map/pallas_call | solution.py:243
  125.9 6.2 %all-to-all-start.4 = ((bf16[64,8,768]{2,1,0:T(8,128)(2,1)}), bf16[64,8,768]{2,1,0:T(8,128)(2,1)S(1)}, u32[]{:S(2)}, u32[]{:S(2)}) async-start(bf16[64,8,768]{2,1,0:T(8,128)(2,1)} %get-tuple-element.17), calls=%async_computation.4 | async-start | bytes 1572864 | tf_op jit(solution)/shard_map/all_to_all | solution.py:217
  132.2 1.4 copy-done.26
  133.6 2.1 shard_map.99
  136.6 18.5 %all-to-all-done.4 = bf16[64,8,768]{2,1,0:T(8,128)(2,1)S(1)} async-done(((bf16[64,8,768]{2,1,0:T(8,128)(2,1)}), bf16[64,8,768]{2,1,0:T(8,128)(2,1)S(1)}, u32[]{:S(2)}, u32[]{:S(2)}) %all-to-all-start.4) | async-done | bytes 786464 | tf_op jit(solution)/shard_map/all_to_all | solution.py:217
  155.2 6.2 %all-to-all-start.2 = ((bf16[64,8,768]{2,1,0:T(8,128)(2,1)}), bf16[64,8,768]{2,1,0:T(8,128)(2,1)S(1)}, u32[]{:S(2)}, u32[]{:S(2)}) async-start(bf16[64,8,768]{2,1,0:T(8,128)(2,1)} %get-tuple-element.13), calls=%async_computation.2 | async-start | bytes 1572864 | tf_op jit(solution)/shard_map/all_to_all | solution.py:217
  161.4 1.6 collective-permute-start.5
  163.0 18.7 %collective-permute-done.5.r_ref = bf16[64,8,768]{2,1,0:T(8,128)(2,1)S(1)} collective-permute-done((bf16[64,8,768]{2,1,0:T(8,128)(2,1)S(1)}, bf16[64,8,768]{2,1,0:T(8,128)(2,1)S(1)}, u32[]{:S(2)}, u32[]{:S(2)}) %collective-permute-start.5) | collective-permute-done | bytes 786464 | tf_op jit(solution)/shard_map/ppermute | solution.py:228
  181.7 1.5 shard_map.101
  185.2 10.2 %all-to-all-start.5 = ((bf16[64,8,768]{2,1,0:T(8,128)(2,1)}), bf16[64,8,768]{2,1,0:T(8,128)(2,1)}, u32[]{:S(2)}, u32[]{:S(2)}) async-start(bf16[64,8,768]{2,1,0:T(8,128)(2,1)} %shard_map.101), calls=%async_computation.5 | async-start | bytes 1572864 | tf_op jit(solution)/shard_map/all_to_all | solution.py:217
  195.5 20.1 %collective-permute-done.2.r_ref = bf16[64,8,768]{2,1,0:T(8,128)(2,1)S(1)} collective-permute-done((bf16[64,8,768]{2,1,0:T(8,128)(2,1)}, bf16[64,8,768]{2,1,0:T(8,128)(2,1)S(1)}, u32[]{:S(2)}, u32[]{:S(2)}) %collective-permute-start.2) | collective-permute-done | bytes 786464 | tf_op jit(solution)/shard_map/ppermute | solution.py:228
  215.6 1.2 copy-done.4
  218.3 11.4 %all-to-all-start.3 = ((bf16[64,8,768]{2,1,0:T(8,128)(2,1)}), bf16[64,8,768]{2,1,0:T(8,128)(2,1)}, u32[]{:S(2)}, u32[]{:S(2)}) async-start(bf16[64,8,768]{2,1,0:T(8,128)(2,1)} %copy-done.8), calls=%async_computation.3 | async-start | bytes 1572864 | tf_op jit(solution)/shard_map/all_to_all | solution.py:217
  230.1 19.7 %collective-permute-done.4.x_ref = bf16[256,1536]{1,0:T(8,128)(2,1)S(1)} collective-permute-done((bf16[256,1536]{1,0:T(8,128)(2,1)}, bf16[256,1536]{1,0:T(8,128)(2,1)S(1)}, u32[]{:S(2)}, u32[]{:S(2)}) %collective-permute-start.4) | collective-permute-done | bytes 786464 | tf_op jit(solution)/shard_map/ppermute | solution.py:228
  249.9 1.9 copy-done.1
  251.8 1.4 copy-done.6
  253.2 4.9 %shard_map.102.other_ref = bf16[256,1536]{1,0:T(8,128)(2,1)S(1)} custom-call(s32[2]{0:T(128)S(1)} %add_convert_fusion.flag_ref, bf16[512,1536]{1,0:T(8,128)(2,1)S(1)} %copy-done.6, bf16[256,1536]{1,0:T(8,128)(2,1)S(1)} %collective-permute-done.4.x_ref, bf16[64,8,768]{2,1,0:T(8,128)(2,1)} %all-to-all-done.5.across_ref, f32[1,1536]{1,0:T(1,128)S(1)} %copy-done.14, ...), custom_call_target="tpu_custom_call" | custom-call | flops 2500000000 | bytes 10000000 | tf_op jit(solution)/shard_map/pallas_call | solution.py:270
  258.9 7.7 %collective-permute-done.3.x_ref = bf16[256,1536]{1,0:T(8,128)(2,1)S(1)} collective-permute-done((bf16[256,1536]{1,0:T(8,128)(2,1)}, bf16[256,1536]{1,0:T(8,128)(2,1)S(1)}, u32[]{:S(2)}, u32[]{:S(2)}) %collective-permute-start.3) | collective-permute-done | bytes 786464 | tf_op jit(solution)/shard_map/ppermute | solution.py:228
  267.5 1.9 copy-done.2
  269.4 1.4 copy-done.7
  273.1 7.2 %shard_map.103 = bf16[512,1536]{1,0:T(8,128)(2,1)} custom-call(s32[2]{0:T(128)S(1)} %add_convert_fusion.flag_ref, bf16[512,1536]{1,0:T(8,128)(2,1)S(1)} %copy-done.7, bf16[256,1536]{1,0:T(8,128)(2,1)S(1)} %copy-done.13, bf16[64,8,768]{2,1,0:T(8,128)(2,1)} %all-to-all-done.3.across_ref, f32[1,1536]{1,0:T(1,128)S(1)} %copy-done.14, ...), custom_call_target="tpu_custom_call" | custom-call | flops 3000000000 | bytes 11000000 | tf_op jit(solution)/shard_map/pallas_call | solution.py:273
  (58 shorter events, 14.4 us)
Async XLA Ops:
  0.6 1.4 copy-start.15
  6.4 1.1 copy-start.11
  7.6 13.1 %copy-start.21 = (bf16[1,4,128,128]{3,2,1,0:T(8,128)(2,1)S(1)}, bf16[1,4,128,128]{3,2,1,0:T(8,128)(2,1)}, u32[]{:S(2)}) copy-start(bf16[1,4,128,128]{3,2,1,0:T(8,128)(2,1)} %param.12) | copy-start | bytes 393220
  7.6 52.9 %all-to-all-start = ((bf16[64,2,8,768]{3,2,1,0:T(8,128)(2,1)}), bf16[64,2,8,768]{3,2,1,0:T(8,128)(2,1)S(1)}, u32[]{:S(2)}, u32[]{:S(2)}) async-start(bf16[64,2,8,768]{3,2,1,0:T(8,128)(2,1)} %copy-done.11), calls=%async_computation | async-start | bytes 3145728 | tf_op jit(solution)/shard_map/all_to_all | solution.py:217
  22.0 159.7 %copy-start.3 = (bf16[2,512,512]{2,1,0:T(8,128)(2,1)}, bf16[2,512,512]{2,1,0:T(8,128)(2,1)S(1)}, u32[]{:S(2)}) copy-start(bf16[2,512,512]{2,1,0:T(8,128)(2,1)S(1)} %shard_map.95.spread_ref) | copy-start | bytes 3145732
  62.6 6.4 %copy-start.20 = (bf16[1,2,256,256]{3,2,1,0:T(8,128)(2,1)S(1)}, bf16[1,2,256,256]{3,2,1,0:T(8,128)(2,1)}, u32[]{:S(2)}) copy-start(bf16[1,2,256,256]{3,2,1,0:T(8,128)(2,1)} %param.11) | copy-start | bytes 786436
  62.6 9.3 %copy-start.23 = (f32[1,1536]{1,0:T(1,128)S(1)}, f32[1,1536]{1,0:T(1,128)}, u32[]{:S(2)}) copy-start(f32[1,1536]{1,0:T(1,128)} %gain_ref.1) | copy-start | bytes 18436
  62.6 46.2 %copy-start.5 = (bf16[512,1536]{1,0:T(8,128)(2,1)S(1)}, bf16[512,1536]{1,0:T(8,128)(2,1)}, u32[]{:S(2)}) copy-start(bf16[512,1536]{1,0:T(8,128)(2,1)} %queued_ref.5) | copy-start | bytes 4718596
  62.6 46.2 %copy-start.14 = (f32[1,1536]{1,0:T(1,128)S(1)}, f32[1,1536]{1,0:T(1,128)}, u32[]{:S(2)}) copy-start(f32[1,1536]{1,0:T(1,128)} %channel_ref.5) | copy-start | bytes 18436
  62.6 46.2 %all-to-all-start.1 = ((bf16[64,2,8,768]{3,2,1,0:T(8,128)(2,1)}), bf16[64,2,8,768]{3,2,1,0:T(8,128)(2,1)}, u32[]{:S(2)}, u32[]{:S(2)}) async-start(bf16[64,2,8,768]{3,2,1,0:T(8,128)(2,1)} %shard_map.97), calls=%async_computation.1 | async-start | bytes 3145728 | tf_op jit(solution)/shard_map/all_to_all | solution.py:217
  69.1 8.1 %collective-permute-start.1 = (bf16[2,256,256]{2,1,0:T(8,128)(2,1)S(1)}, bf16[2,256,256]{2,1,0:T(8,128)(2,1)S(1)}, u32[]{:S(2)}, u32[]{:S(2)}) collective-permute-start(bf16[2,256,256]{2,1,0:T(8,128)(2,1)S(1)} %bitcast.18), channel_id=1, source_target_pairs={{64,0},{128,64},{192,128},{0,192},{65,1},{129,65},{193,129},{1,193... | collective-permute-start | bytes 786440 | tf_op jit(solution)/shard_map/ppermute | solution.py:231
  71.9 5.3 %collective-permute-start = (f32[1,1536]{1,0:T(1,128)S(1)}, f32[1,1536]{1,0:T(1,128)S(1)}, u32[]{:S(2)}, u32[]{:S(2)}) collective-permute-start(f32[1,1536]{1,0:T(1,128)S(1)} %copy-done.23), channel_id=1, source_target_pairs={{64,0},{128,64},{192,128},{0,192},{65,1},{129,65},{193,129},{1,193... | collective-permute-start | bytes 18440 | tf_op jit(solution)/shard_map/ppermute | solution.py:231
  108.8 1.4 copy-start.16
  124.8 1.1 copy-start.25
  125.9 6.3 %copy-start.24 = (bf16[512,1536]{1,0:T(8,128)(2,1)S(1)}, bf16[512,1536]{1,0:T(8,128)(2,1)}, u32[]{:S(2)}) copy-start(bf16[512,1536]{1,0:T(8,128)(2,1)} %get-tuple-element.10.first_ref) | copy-start | bytes 4718596
  125.9 29.2 %all-to-all-start.4 = ((bf16[64,8,768]{2,1,0:T(8,128)(2,1)}), bf16[64,8,768]{2,1,0:T(8,128)(2,1)S(1)}, u32[]{:S(2)}, u32[]{:S(2)}) async-start(bf16[64,8,768]{2,1,0:T(8,128)(2,1)} %get-tuple-element.17), calls=%async_computation.4 | async-start | bytes 1572864 | tf_op jit(solution)/shard_map/all_to_all | solution.py:217
  132.2 1.4 copy-start.26
  155.2 29.2 %all-to-all-start.2 = ((bf16[64,8,768]{2,1,0:T(8,128)(2,1)}), bf16[64,8,768]{2,1,0:T(8,128)(2,1)S(1)}, u32[]{:S(2)}, u32[]{:S(2)}) async-start(bf16[64,8,768]{2,1,0:T(8,128)(2,1)} %get-tuple-element.13), calls=%async_computation.2 | async-start | bytes 1572864 | tf_op jit(solution)/shard_map/all_to_all | solution.py:217
  161.4 20.3 %collective-permute-start.5 = (bf16[64,8,768]{2,1,0:T(8,128)(2,1)S(1)}, bf16[64,8,768]{2,1,0:T(8,128)(2,1)S(1)}, u32[]{:S(2)}, u32[]{:S(2)}) collective-permute-start(bf16[64,8,768]{2,1,0:T(8,128)(2,1)S(1)} %all-to-all-done.4), channel_id=1, source_target_pairs={{0,64},{64,128},{128,192},{192,0},{1,65},{65,129},{129,193},{193,1... | collective-permute-start | bytes 2359304 | tf_op jit(solution)/shard_map/ppermute | solution.py:228
  185.2 33.1 %all-to-all-start.5 = ((bf16[64,8,768]{2,1,0:T(8,128)(2,1)}), bf16[64,8,768]{2,1,0:T(8,128)(2,1)}, u32[]{:S(2)}, u32[]{:S(2)}) async-start(bf16[64,8,768]{2,1,0:T(8,128)(2,1)} %shard_map.101), calls=%async_computation.5 | async-start | bytes 1572864 | tf_op jit(solution)/shard_map/all_to_all | solution.py:217
  195.4 54.5 %copy-start = (bf16[1,4,384,1024]{3,2,1,0:T(8,128)(2,1)S(1)}, bf16[1,4,384,1024]{3,2,1,0:T(8,128)(2,1)}, u32[]{:S(2)}) copy-start(bf16[1,4,384,1024]{3,2,1,0:T(8,128)(2,1)} %param.14) | copy-start | bytes 9437188
  195.4 20.2 %collective-permute-start.2 = (bf16[64,8,768]{2,1,0:T(8,128)(2,1)}, bf16[64,8,768]{2,1,0:T(8,128)(2,1)S(1)}, u32[]{:S(2)}, u32[]{:S(2)}) collective-permute-start(bf16[64,8,768]{2,1,0:T(8,128)(2,1)} %copy-done.27), channel_id=1, source_target_pairs={{0,64},{64,128},{128,192},{192,0},{1,65},{65,129},{129,193},{193,1... | collective-permute-start | bytes 2359304 | tf_op jit(solution)/shard_map/ppermute | solution.py:228
  215.6 1.2 copy-start.4
  218.3 49.2 %all-to-all-start.3 = ((bf16[64,8,768]{2,1,0:T(8,128)(2,1)}), bf16[64,8,768]{2,1,0:T(8,128)(2,1)}, u32[]{:S(2)}, u32[]{:S(2)}) async-start(bf16[64,8,768]{2,1,0:T(8,128)(2,1)} %copy-done.8), calls=%async_computation.3 | async-start | bytes 1572864 | tf_op jit(solution)/shard_map/all_to_all | solution.py:217
  229.7 20.2 %collective-permute-start.4 = (bf16[256,1536]{1,0:T(8,128)(2,1)}, bf16[256,1536]{1,0:T(8,128)(2,1)S(1)}, u32[]{:S(2)}, u32[]{:S(2)}) collective-permute-start(bf16[256,1536]{1,0:T(8,128)(2,1)} %copy-done.17), channel_id=1, source_target_pairs={{0,64},{64,128},{128,192},{192,0},{1,65},{65,129},{129,193},{193,1... | collective-permute-start | bytes 2359304 | tf_op jit(solution)/shard_map/ppermute | solution.py:228
  229.8 36.8 %collective-permute-start.3 = (bf16[256,1536]{1,0:T(8,128)(2,1)}, bf16[256,1536]{1,0:T(8,128)(2,1)S(1)}, u32[]{:S(2)}, u32[]{:S(2)}) collective-permute-start(bf16[256,1536]{1,0:T(8,128)(2,1)} %copy-done.18), channel_id=1, source_target_pairs={{0,64},{64,128},{128,192},{192,0},{1,65},{65,129},{129,193},{193,1... | collective-permute-start | bytes 2359304 | tf_op jit(solution)/shard_map/ppermute | solution.py:228
  249.9 1.9 copy-start.1
  251.8 1.4 copy-start.6
  267.5 1.9 copy-start.2
  269.4 1.4 copy-start.7
  270.8 1.1 copy-start.10
  271.9 1.1 copy-start.13
  (8 other events, 7.0 us)

commit v3 on v2

v3 whole, which is shorter than its diff:
```python
import functools

import jax
import jax.numpy as jnp
from jax import lax
from jax.experimental import pallas as pl
from jax.experimental.pallas import tpu as pltpu
from jax.sharding import PartitionSpec as P

EPS = 1e-05
D = 1536
HALF = D // 2
BLK = 256
DEV = 64
GROUPS = 4
BF = jnp.bfloat16
F32 = jnp.float32


def call(kernel, out_shape, places, results, cost, scratch=()):
    kinds = {"s": pltpu.SMEM, "v": pltpu.VMEM, "h": pltpu.HBM}
    outs = [pl.BlockSpec(memory_space=kinds[p]) for p in results]
    flops, bytes_accessed, transcendentals = cost
    return pl.pallas_call(
        kernel,
        out_shape=out_shape,
        in_specs=[pl.BlockSpec(memory_space=kinds[p]) for p in places],
        out_specs=outs if len(outs) > 1 else outs[0],
        scratch_shapes=scratch,
        cost_estimate=pl.CostEstimate(
            flops=flops, bytes_accessed=bytes_accessed, transcendentals=transcendentals
        ),
        compiler_params=pltpu.CompilerParams(vmem_limit_bytes=44 * 1024 * 1024),
    )


def copies(pairs, sems):
    started = [
        pltpu.make_async_copy(source, target, sems.at[i])
        for i, (source, target) in enumerate(pairs)
    ]
    for copy in started:
        copy.start()
    return started


def dot(a, b):
    return jnp.dot(a, b, preferred_element_type=F32)


def onehot(rows, cols, hit):
    r = lax.broadcasted_iota(jnp.int32, (rows, cols), 0)
    c = lax.broadcasted_iota(jnp.int32, (rows, cols), 1)
    return jnp.where(hit(r, c), 1.0, 0.0).astype(BF)


def packed_at(r, j, c, h, b):
    return (((r >> 3) * 4 + 2 * c + (r & 1)) == j) & (((r >> 1) & 3) == 2 * h + b)


def pack(c, h, b):
    return onehot(2 * BLK, BLK, lambda r, j: packed_at(r, j, c, h, b))


def unpack(c, h, b):
    return onehot(BLK, 2 * BLK, lambda j, r: packed_at(r, j, c, h, b))


def unpack_compact(h):
    return onehot(
        BLK, 2 * BLK, lambda q, r: r == ((q & 127) >> 1) * 8 + 4 * h + 2 * (q >> 7) + (q & 1)
    )


def pick(c):
    return onehot(BLK // 2, BLK, lambda q, j: j == (q >> 1) * 4 + 2 * c + (q & 1))


def place(c):
    return onehot(BLK, BLK // 2, lambda j, q: j == (q >> 1) * 4 + 2 * c + (q & 1))


def normalize(values, gain):
    scale = lax.rsqrt(jnp.mean(values * values, axis=-1, keepdims=True) + EPS)
    return (values * scale * gain).astype(BF)


def packed_part(packs, mixed):
    total = None
    for b in range(2):
        for h in range(2):
            term = dot(packs(h, b), mixed[b][:, h * HALF : (h + 1) * HALF])
            total = term if total is None else total + term
    return total.astype(BF).reshape(DEV, 8, HALF)


def first_kernel(x_ref, gain_ref, factor_ref, out_ref, x_buf, factor_buf, out_buf, sems, out_sems):
    rows = [pl.ds(b * BLK, BLK) for b in range(2)]
    loads = copies(
        [
            (x_ref.at[rows[0]], x_buf.at[rows[0]]),
            (factor_ref, factor_buf),
            (x_ref.at[rows[1]], x_buf.at[rows[1]]),
        ],
        sems,
    )
    mixed = []
    for b in range(2):
        loads[2 * b].wait()
        normed = normalize(x_buf[rows[b], :].astype(F32), gain_ref[...])
        if b == 0:
            loads[1].wait()
        mixed.append(dot(factor_buf[b], normed).astype(BF))
    stores = []
    for c in range(2):
        out_buf[c] = packed_part(functools.partial(pack, c), mixed)
        stores.append(pltpu.make_async_copy(out_buf.at[c], out_ref.at[:, c], out_sems.at[c]))
        stores[c].start()
    for store in stores:
        store.wait()


def spread_kernel(cross_ref, out_ref, pack_ref, unpack_ref, compact_ref, pick_ref, place_ref):
    n = 2 * BLK
    row = lax.broadcasted_iota(jnp.int32, (n, n), 0)
    col = lax.broadcasted_iota(jnp.int32, (n, n), 1)
    same = ((row ^ col) & 5) == 0
    cross = cross_ref[...].reshape(n, 128)
    columns = onehot(128, n, lambda m, k: m == (k >> 3) * 2 + ((k >> 1) & 1))
    for c in range(2):
        rows = onehot(
            n, n, lambda r, k: k == (2 * c + (r & 1)) * 128 + (r >> 3) * 2 + ((r >> 1) & 1)
        )
        full = dot(dot(rows, cross).astype(BF), columns)
        out_ref[c] = jnp.where(same, full, 0.0).astype(BF)
        for h in range(2):
            for b in range(2):
                pack_ref[c, h, b] = pack(c, h, b)
                unpack_ref[c, h, b] = unpack(c, h, b)
        compact_ref[c] = unpack_compact(c)
        pick_ref[c] = pick(c)
        place_ref[c] = place(c)


def cross_both_kernel(spread_ref, r_ref, out_ref):
    for c in range(2):
        total = dot(spread_ref[c], r_ref[:, c].reshape(2 * BLK, HALF))
        out_ref[:, c] = total.astype(BF).reshape(DEV, 8, HALF)


def cross_kernel(c, spread_ref, r_ref, out_ref):
    total = dot(spread_ref[c], r_ref[...].reshape(2 * BLK, HALF))
    out_ref[...] = total.astype(BF).reshape(DEV, 8, HALF)


def gelu(hidden):
    value = hidden.astype(BF)
    half = value * BF(0.5)
    inner = value * (BF(0.7978845608028654) + BF(0.7978845608028654 * 0.044715) * (value * value))
    return half + half * jnp.tanh(inner)


def channel_rows(residual, gain, up, down, store):
    normed = normalize(residual, gain)
    width = D // GROUPS
    for g in range(GROUPS):
        part = slice(g * width, (g + 1) * width)
        act = gelu(dot(normed[:, part], up(g)))
        store(g, part, (residual[:, part] + dot(act, down(g))).astype(BF))


def weight_loads(up_ref, down_ref, up_buf, down_buf, sems):
    pairs = []
    for g in range(GROUPS):
        pairs += [(up_ref.at[g], up_buf.at[g]), (down_ref.at[g], down_buf.at[g])]
    loads = copies(pairs, sems)
    waited = set()

    def get(k, buf, g):
        if (k, g) not in waited:
            waited.add((k, g))
            loads[2 * g + k].wait()
        return buf[g]

    return functools.partial(get, 0, up_buf), functools.partial(get, 1, down_buf)


def middle_kernel(
    flag_ref,
    x_ref,
    across_ref,
    channel_ref,
    up_ref,
    down_ref,
    queued_ref,
    gain_ref,
    factor_ref,
    pack_ref,
    unpack_ref,
    pick_ref,
    first_ref,
    kept_ref,
    mixed_ref,
    out_ref,
    across_buf,
    up_buf,
    down_buf,
    first_buf,
    out_buf,
    sems,
    weight_sems,
):
    loads = copies(
        [(across_ref.at[:, 0], across_buf.at[0]), (across_ref.at[:, 1], across_buf.at[1])],
        sems,
    )
    up, down = weight_loads(up_ref, down_ref, up_buf, down_buf, weight_sems)
    for load in loads:
        load.wait()
    packed = [across_buf[c].reshape(2 * BLK, HALF) for c in range(2)]
    mixed, stores = [], []
    for b in range(2):
        rows = slice(b * BLK, (b + 1) * BLK)
        across = jnp.concatenate(
            [
                dot(unpack_ref[0, h, b], packed[0]) + dot(unpack_ref[1, h, b], packed[1])
                for h in range(2)
            ],
            axis=1,
        )

        def store(g, part, value):
            first_buf[rows, part] = value

        residual = x_ref[rows, :].astype(F32) + across
        channel_rows(residual, channel_ref[...], up, down, store)
        window = pl.ds(b * BLK, BLK)
        stores.append(
            pltpu.make_async_copy(first_buf.at[window], first_ref.at[window], sems.at[2 + b])
        )
        stores[b].start()
        first = first_buf[rows, :]
        kept_ref[b * (BLK // 2) : (b + 1) * (BLK // 2), :] = dot(pick_ref[0], first).astype(BF)
        entering = jnp.where(flag_ref[1] == 1, queued_ref[rows, :], first)
        normed = normalize(entering.astype(F32), gain_ref[...])
        mixed.append(dot(factor_ref[b], normed).astype(BF))
        mixed_ref[rows, :] = mixed[b]
    out_buf[...] = packed_part(lambda h, b: pack_ref[0, h, b], mixed)
    stores.append(pltpu.make_async_copy(out_buf, out_ref, sems.at[4]))
    stores[2].start()
    for store in stores:
        store.wait()


def remainder_kernel(first_ref, mixed_ref, pack_ref, pick_ref, kept_ref, out_ref):
    mixed = [mixed_ref[b * BLK : (b + 1) * BLK, :] for b in range(2)]
    out_ref[...] = packed_part(lambda h, b: pack_ref[1, h, b], mixed)
    for b in range(2):
        first = first_ref[b * BLK : (b + 1) * BLK, :]
        kept_ref[b * (BLK // 2) : (b + 1) * (BLK // 2), :] = dot(pick_ref[1], first).astype(BF)


def last_rows(c, flag_ref, queued_ref, x_ref, pick_ref, compact_ref, across_buf, load):
    queued = [
        dot(pick_ref[c], queued_ref[b * BLK : (b + 1) * BLK, :]).astype(BF) for b in range(2)
    ]
    x = jnp.where(flag_ref[0] == 1, jnp.concatenate(queued, axis=0), x_ref[...])
    load.wait()
    packed = across_buf[...].reshape(2 * BLK, HALF)
    across = jnp.concatenate([dot(compact_ref[h], packed) for h in range(2)], axis=1)
    return x.astype(F32) + across


def last_kernel(
    flag_ref,
    queued_ref,
    x_ref,
    across_ref,
    channel_ref,
    up_ref,
    down_ref,
    pick_ref,
    compact_ref,
    out_ref,
    across_buf,
    up_buf,
    down_buf,
    sems,
    weight_sems,
):
    (load,) = copies([(across_ref, across_buf)], sems)
    up, down = weight_loads(up_ref, down_ref, up_buf, down_buf, weight_sems)

    def store(g, part, value):
        out_ref[:, part] = value

    residual = last_rows(
        0, flag_ref, queued_ref, x_ref, pick_ref, compact_ref, across_buf, load
    )
    channel_rows(residual, channel_ref[...], up, down, store)


def final_kernel(
    flag_ref,
    queued_ref,
    x_ref,
    across_ref,
    channel_ref,
    up_ref,
    down_ref,
    pick_ref,
    compact_ref,
    place_ref,
    other_ref,
    out_ref,
    across_buf,
    up_buf,
    down_buf,
    out_buf,
    sems,
    weight_sems,
    out_sems,
):
    (load,) = copies([(across_ref, across_buf)], sems)
    up, down = weight_loads(up_ref, down_ref, up_buf, down_buf, weight_sems)
    stores = []

    def store(g, part, value):
        for b in range(2):
            rows = slice(b * (BLK // 2), (b + 1) * (BLK // 2))
            joined = dot(place_ref[0], other_ref[rows, part]) + dot(place_ref[1], value[rows])
            out_buf[b * BLK : (b + 1) * BLK, part] = joined.astype(BF)
        width = pl.ds(part.start, part.stop - part.start)
        stores.append(
            pltpu.make_async_copy(out_buf.at[:, width], out_ref.at[:, width], out_sems.at[g])
        )
        stores[g].start()

    residual = last_rows(
        1, flag_ref, queued_ref, x_ref, pick_ref, compact_ref, across_buf, load
    )
    channel_rows(residual, channel_ref[...], up, down, store)
    for copy in stores:
        copy.wait()


def shape(*dims):
    return jax.ShapeDtypeStruct(dims, BF)


def hbm(value):
    return pltpu.with_memory_space_constraint(value, pltpu.HBM)


def exchange(value):
    return lax.all_to_all(value, "seq", split_axis=0, concat_axis=0, tiled=True)


def per_device(arriving, queued, norm_gain, block_factor, cross_factor, channel_gain, up, down):
    section = lax.axis_index("section")
    count = lax.axis_size("section")
    flags = jnp.stack([section == 0, section == count - 1]).astype(jnp.int32)
    x = arriving[0]
    factor, cross = block_factor[0], cross_factor[0]
    up, down, held_x, held_factor = (hbm(v) for v in (up[0], down[0], x, factor))

    def ahead(value):
        return lax.ppermute(value, "section", [(s, (s + 1) % count) for s in range(count)])

    def behind(value):
        return lax.ppermute(value, "section", [((s + 1) % count, s) for s in range(count)])

    message = shape(DEV, 8, HALF)
    both = shape(DEV, 2, 8, HALF)
    sequence, part_rows = shape(2 * BLK, D), shape(BLK, D)
    message_buf = pltpu.VMEM((DEV, 8, HALF), BF)
    pair_buf = pltpu.VMEM((2, DEV, 8, HALF), BF)
    sequence_buf = pltpu.VMEM((2 * BLK, D), BF)
    weight_bufs = [pltpu.VMEM(up.shape, BF), pltpu.VMEM(down.shape, BF)]
    weight_sems = pltpu.SemaphoreType.DMA((2 * GROUPS,))

    def sems(n):
        return pltpu.SemaphoreType.DMA((n,))

    sent = call(
        first_kernel,
        both,
        "hvh",
        "h",
        (2_000_000_000, 4_000_000, 0),
        [sequence_buf, pltpu.VMEM(factor.shape, BF), pair_buf, sems(3), sems(2)],
    )(held_x, norm_gain, held_factor)
    columns = exchange(sent)
    spread, packs, unpacks, compact, picks, places = call(
        spread_kernel,
        (
            shape(2, 2 * BLK, 2 * BLK),
            shape(2, 2, 2, 2 * BLK, BLK),
            shape(2, 2, 2, BLK, 2 * BLK),
            shape(2, BLK, 2 * BLK),
            shape(2, BLK // 2, BLK),
            shape(2, BLK, BLK // 2),
        ),
        "v",
        "vvvvvv",
        (400_000_000, 6_000_000, 0),
    )(cross)
    next_gain, next_factor = behind(norm_gain), behind(factor)

    out = call(cross_both_kernel, both, "vv", "v", (800_000_000, 4_000_000, 0))(spread, columns)
    across = hbm(exchange(out))

    first, kept0, mixed, sent0 = call(
        middle_kernel,
        (sequence, part_rows, sequence, message),
        "svhvhhvvvvvv",
        "hvvh",
        (7_000_000_000, 18_000_000, 2_000_000),
        [pair_buf, *weight_bufs, sequence_buf, message_buf, sems(5), weight_sems],
    )(
        flags,
        x,
        across,
        channel_gain,
        up,
        down,
        queued,
        next_gain,
        next_factor,
        packs,
        unpacks,
        picks,
    )
    x0 = ahead(kept0)
    columns0 = exchange(sent0)
    columns0, x0 = lax.optimization_barrier((columns0, x0))
    kept1, sent1 = call(
        remainder_kernel, (part_rows, message), "vvvv", "vv", (1_000_000_000, 5_000_000, 0)
    )(first, mixed, packs, picks)
    columns0, sent1 = lax.optimization_barrier((columns0, sent1))
    columns0 = ahead(columns0)
    columns1 = exchange(sent1)
    out0 = call(
        functools.partial(cross_kernel, 0), message, "vv", "v", (400_000_000, 2_000_000, 0)
    )(spread, columns0)
    across0 = hbm(exchange(out0))
    columns1 = ahead(columns1)
    kept1, columns1 = lax.optimization_barrier((kept1, columns1))
    x1 = ahead(kept1)
    out1 = call(
        functools.partial(cross_kernel, 1), message, "vv", "v", (400_000_000, 2_000_000, 0)
    )(spread, columns1)
    across1 = hbm(exchange(out1))
    other = call(
        last_kernel,
        part_rows,
        "svvhvhhvv",
        "v",
        (2_500_000_000, 10_000_000, 1_000_000),
        [message_buf, *weight_bufs, sems(1), weight_sems],
    )(flags, queued, x0, across0, channel_gain, up, down, picks, compact)
    second = call(
        final_kernel,
        sequence,
        "svvhvhhvvvv",
        "h",
        (3_000_000_000, 11_000_000, 1_000_000),
        [message_buf, *weight_bufs, sequence_buf, sems(1), weight_sems, sems(GROUPS)],
    )(flags, queued, x1, across1, channel_gain, up, down, picks, compact, places, other)
    return first[None], second[None]


def solution(mesh):
    placed = (
        P("section", "seq", None),
        P("seq", None),
        P("section", None),
        P("section", "seq", None, None),
        P("section", "seq", None, None),
        P("section", None),
        P("section", None, None, None),
        P("section", None, None, None),
    )
    return jax.shard_map(
        per_device,
        mesh=mesh,
        in_specs=placed,
        out_specs=(P("section", "seq", None), P("section", "seq", None)),
        check_vma=False,
    )
```

time: 282 us -> 280 us (level); the launches traced: 280 us -> 274 us
  waiting for transfers between devices: 161 us -> 139 us
  Pallas kernels: 36.1 us -> 46.1 us
  starting transfers between devices: 58.9 us -> 67.8 us
  local copies, waits for them, and re-layouts: 23.6 us -> 19.8 us
    all_to_all x6, waiting for transfers between devices: 89.9 us -> 72.5 us  [exchange(): return lax.all_to_all(value, 'seq', split_axis=0, concat_axis=0, tiled=True)]
    pallas_call x9, Pallas kernels: 36.1 us -> 46.1 us  [the longest x1 14.9 us: per_device(): call(middle_kernel, (sequence, part_rows, sequence, message), 'svhvhhvvvv...]
    all_to_all x6, starting transfers between devices: 53.5 us -> 61.4 us  [exchange(): return lax.all_to_all(value, 'seq', split_axis=0, concat_axis=0, tiled=True)]
    ppermute x4, waiting for transfers between devices: 66.2 us -> 62.1 us  [ahead(): lax.ppermute(value, 'section', [(s, (s + 1) % count) for s in range(count)])]
    unnamed x56 -> x42, local copies, waits for them, and re-layouts: 23.6 us -> 19.8 us
  transfers between devices with their start and end apart: 12 -> 12, of which waited for: 9 -> 11; matrix products, arithmetic and copies ran while one was open for 0% -> 0% of each run, Pallas kernels for 4% -> 5%
where the time goes in v3:
time: 280 us; the launch traced here: 274 us
  waiting for transfers between devices  139 us (50%)
  starting transfers between devices  67.8 us (24%)
  Pallas kernels  46.1 us (16%)
  local copies, waits for them, and re-layouts  19.8 us (7%)
    all_to_all x6, waiting for transfers between devices, exchange(): return lax.all_to_all(value, 'seq', split_axis=0, concat_axis=0, tiled=True)  72.5 us
    ppermute x4, waiting for transfers between devices, ahead(): lax.ppermute(value, 'section', [(s, (s + 1) % count) for s in range(count)])  62.1 us
    all_to_all x6, starting transfers between devices, exchange(): return lax.all_to_all(value, 'seq', split_axis=0, concat_axis=0, tiled=True)  61.4 us
    unnamed x42, local copies, waits for them, and re-layouts  19.8 us
    pallas_call x1, Pallas kernels, per_device(): call(middle_kernel, (sequence, part_rows, sequence, message), 'svhvhhvvvv...  14.9 us
    pallas_call x1, Pallas kernels, per_device(): call(final_kernel, sequence, 'svvhvhhvvvv', 'h', (3000000000, 11000000, 1...  8.6 us
    pallas_call x1, Pallas kernels, per_device(): call(last_kernel, part_rows, 'svvhvhhvv', 'v', (2500000000, 10000000, 100...  7.22 us
    pallas_call x1, Pallas kernels, per_device(): call(first_kernel, both, 'hvh', 'h', (2000000000, 4000000, 0), [sequence_...  5.97 us
  transfers between devices with their start and end apart: 12, of which 11 were waited for; matrix products, arithmetic and copies ran while one was open for 0% of the time, Pallas kernels for 5%

profile of v3, /device:TPU:1, one launch (start us, length us, event | category | flops | bytes accessed | tf_op | source)
XLA Modules:
  0.0 274.1 jit_solution(4260482994967480446)
XLA Ops:
  1.3 6.0 %shard_map.96 = bf16[64,2,8,768]{3,2,1,0:T(8,128)(2,1)S(1)} custom-call(bf16[512,1536]{1,0:T(8,128)(2,1)} %bitcast.10, f32[1,1536]{1,0:T(1,128)S(1)} %copy-done.18, bf16[2,256,256]{2,1,0:T(8,128)(2,1)} %bitcast.20), custom_call_target="tpu_custom_call" | custom-call | flops 2000000000 | bytes 4000000 | tf_op jit(solution)/shard_map/pallas_call | solution.py:385
  8.5 13.1 %all-to-all-start = ((bf16[64,2,8,768]{3,2,1,0:T(8,128)(2,1)}), bf16[64,2,8,768]{3,2,1,0:T(8,128)(2,1)S(1)}, u32[]{:S(2)}, u32[]{:S(2)}) async-start(bf16[64,2,8,768]{3,2,1,0:T(8,128)(2,1)} %copy-done.4), calls=%async_computation | async-start | bytes 3145728 | tf_op jit(solution)/shard_map/all_to_all | solution.py:356
  21.6 2.2 shard_map.95
  26.5 34.9 %all-to-all-done.r_ref = bf16[64,2,8,768]{3,2,1,0:T(8,128)(2,1)S(1)} async-done(((bf16[64,2,8,768]{3,2,1,0:T(8,128)(2,1)}), bf16[64,2,8,768]{3,2,1,0:T(8,128)(2,1)S(1)}, u32[]{:S(2)}, u32[]{:S(2)}) %all-to-all-start) | async-done | bytes 1572896 | tf_op jit(solution)/shard_map/all_to_all | solution.py:356
  61.4 2.1 shard_map.97
  63.5 6.4 %all-to-all-start.1 = ((bf16[64,2,8,768]{3,2,1,0:T(8,128)(2,1)}), bf16[64,2,8,768]{3,2,1,0:T(8,128)(2,1)}, u32[]{:S(2)}, u32[]{:S(2)}) async-start(bf16[64,2,8,768]{3,2,1,0:T(8,128)(2,1)} %shard_map.97), calls=%async_computation.1 | async-start | bytes 3145728 | tf_op jit(solution)/shard_map/all_to_all | solution.py:356
  69.9 2.8 %collective-permute-start.1 = (bf16[2,256,256]{2,1,0:T(8,128)(2,1)}, bf16[2,256,256]{2,1,0:T(8,128)(2,1)}, u32[]{:S(2)}, u32[]{:S(2)}) collective-permute-start(bf16[2,256,256]{2,1,0:T(8,128)(2,1)} %bitcast.21), channel_id=1, source_target_pairs={{64,0},{128,64},{192,128},{0,192},{65,1},{129,65},{193,129},{1,193... | collective-permute-start | bytes 786440 | tf_op jit(solution)/shard_map/ppermute | solution.py:371
  73.5 4.7 %collective-permute-done.gain_ref = f32[1,1536]{1,0:T(1,128)S(1)} collective-permute-done((f32[1,1536]{1,0:T(1,128)S(1)}, f32[1,1536]{1,0:T(1,128)S(1)}, u32[]{:S(2)}, u32[]{:S(2)}) %collective-permute-start) | collective-permute-done | bytes 6176 | tf_op jit(solution)/shard_map/ppermute | solution.py:371
  78.2 31.4 %all-to-all-done.1.across_ref = bf16[64,2,8,768]{3,2,1,0:T(8,128)(2,1)} async-done(((bf16[64,2,8,768]{3,2,1,0:T(8,128)(2,1)}), bf16[64,2,8,768]{3,2,1,0:T(8,128)(2,1)}, u32[]{:S(2)}, u32[]{:S(2)}) %all-to-all-start.1) | async-done | bytes 1572896 | tf_op jit(solution)/shard_map/all_to_all | solution.py:356
  109.7 1.6 copy-done.2
  111.3 1.4 copy-done.15
  112.7 14.9 %shard_map.98 = (bf16[512,1536]{1,0:T(8,128)(2,1)}, bf16[256,1536]{1,0:T(8,128)(2,1)S(1)}, bf16[512,1536]{1,0:T(8,128)(2,1)S(1)}, bf16[64,8,768]{2,1,0:T(8,128)(2,1)S(1)}) custom-call(s32[2]{0:T(128)S(1)} %add_convert_fusion.flag_ref, bf16[512,1536]{1,0:T(8,128)(2,1)S(1)} %bitcast.11, bf16[64,2,8,768]{3,2,1,0:T(8,128)(2,1)} %all-to-all-done.1.across_ref, ...), custom_call_target="tpu_custom_call" | custom-call | flops 7000000000 | bytes 18000000 | tf_op jit(solution)/shard_map/pallas_call | solution.py:413
  130.5 6.3 %all-to-all-start.2 = ((bf16[64,8,768]{2,1,0:T(8,128)(2,1)}), bf16[64,8,768]{2,1,0:T(8,128)(2,1)}, u32[]{:S(2)}, u32[]{:S(2)}) async-start(bf16[64,8,768]{2,1,0:T(8,128)(2,1)} %copy-done.13), calls=%async_computation.2 | async-start | bytes 1572864 | tf_op jit(solution)/shard_map/all_to_all | solution.py:356
  136.8 1.4 collective-permute-start.2
  138.2 1.6 copy-done.3
  139.8 1.4 copy-done.5
  141.2 1.4 copy-done.7
  142.6 2.1 shard_map.99
  145.6 11.5 %collective-permute-done.2.x_ref = bf16[256,1536]{1,0:T(8,128)(2,1)S(1)} collective-permute-done((bf16[256,1536]{1,0:T(8,128)(2,1)}, bf16[256,1536]{1,0:T(8,128)(2,1)S(1)}, u32[]{:S(2)}, u32[]{:S(2)}) %collective-permute-start.2) | collective-permute-done | bytes 786464 | tf_op jit(solution)/shard_map/ppermute | solution.py:368
  158.0 1.7 all-to-all-done.2
  159.8 15.2 %all-to-all-start.3 = ((bf16[64,8,768]{2,1,0:T(8,128)(2,1)}), bf16[64,8,768]{2,1,0:T(8,128)(2,1)}, u32[]{:S(2)}, u32[]{:S(2)}) async-start(bf16[64,8,768]{2,1,0:T(8,128)(2,1)} %copy-done.12), calls=%async_computation.3 | async-start | bytes 1572864 | tf_op jit(solution)/shard_map/all_to_all | solution.py:356
  176.4 18.8 %collective-permute-done.5.r_ref = bf16[64,8,768]{2,1,0:T(8,128)(2,1)S(1)} collective-permute-done((bf16[64,8,768]{2,1,0:T(8,128)(2,1)}, bf16[64,8,768]{2,1,0:T(8,128)(2,1)S(1)}, u32[]{:S(2)}, u32[]{:S(2)}) %collective-permute-start.5) | collective-permute-done | bytes 786464 | tf_op jit(solution)/shard_map/ppermute | solution.py:368
  195.2 1.5 shard_map.101
  196.6 1.4 all-to-all-done.3
  198.0 10.2 %all-to-all-start.5 = ((bf16[64,8,768]{2,1,0:T(8,128)(2,1)}), bf16[64,8,768]{2,1,0:T(8,128)(2,1)}, u32[]{:S(2)}, u32[]{:S(2)}) async-start(bf16[64,8,768]{2,1,0:T(8,128)(2,1)} %shard_map.101), calls=%async_computation.5 | async-start | bytes 1572864 | tf_op jit(solution)/shard_map/all_to_all | solution.py:356
  208.3 20.1 %collective-permute-done.3.r_ref = bf16[64,8,768]{2,1,0:T(8,128)(2,1)S(1)} collective-permute-done((bf16[64,8,768]{2,1,0:T(8,128)(2,1)}, bf16[64,8,768]{2,1,0:T(8,128)(2,1)S(1)}, u32[]{:S(2)}, u32[]{:S(2)}) %collective-permute-start.3) | collective-permute-done | bytes 786464 | tf_op jit(solution)/shard_map/ppermute | solution.py:368
  228.4 1.5 shard_map.100
  231.1 10.1 %all-to-all-start.4 = ((bf16[64,8,768]{2,1,0:T(8,128)(2,1)}), bf16[64,8,768]{2,1,0:T(8,128)(2,1)}, u32[]{:S(2)}, u32[]{:S(2)}) async-start(bf16[64,8,768]{2,1,0:T(8,128)(2,1)} %shard_map.100), calls=%async_computation.4 | async-start | bytes 1572864 | tf_op jit(solution)/shard_map/all_to_all | solution.py:356
  242.5 7.2 %shard_map.102.other_ref = bf16[256,1536]{1,0:T(8,128)(2,1)S(1)} custom-call(s32[2]{0:T(128)S(1)} %add_convert_fusion.flag_ref, bf16[512,1536]{1,0:T(8,128)(2,1)S(1)} %copy-done, bf16[256,1536]{1,0:T(8,128)(2,1)S(1)} %copy-done.9, bf16[64,8,768]{2,1,0:T(8,128)(2,1)} %all-to-all-done.5.across_ref, f32[1,1536]{1,0:T(1,128)S(1)} %copy-done.14, ...), custom_call_target="tpu_custom_call" | custom-call | flops 2500000000 | bytes 10000000 | tf_op jit(solution)/shard_map/pallas_call | solution.py:454
  249.7 11.7 %collective-permute-done.4.x_ref = bf16[256,1536]{1,0:T(8,128)(2,1)S(1)} collective-permute-done((bf16[256,1536]{1,0:T(8,128)(2,1)}, bf16[256,1536]{1,0:T(8,128)(2,1)S(1)}, u32[]{:S(2)}, u32[]{:S(2)}) %collective-permute-start.4) | collective-permute-done | bytes 786464 | tf_op jit(solution)/shard_map/ppermute | solution.py:368
  262.3 1.9 all-to-all-done.4.across_ref
  265.3 8.6 %shard_map.103 = bf16[512,1536]{1,0:T(8,128)(2,1)} custom-call(s32[2]{0:T(128)S(1)} %add_convert_fusion.flag_ref, bf16[512,1536]{1,0:T(8,128)(2,1)S(1)} %copy-done, bf16[256,1536]{1,0:T(8,128)(2,1)S(1)} %copy-done.11, bf16[64,8,768]{2,1,0:T(8,128)(2,1)} %all-to-all-done.4.across_ref, f32[1,1536]{1,0:T(1,128)S(1)} %copy-done.14, ...), custom_call_target="tpu_custom_call" | custom-call | flops 3000000000 | bytes 11000000 | tf_op jit(solution)/shard_map/pallas_call | solution.py:462
  (44 shorter events, 16.0 us)
Async XLA Ops:
  7.3 1.1 copy-start.4
  8.5 13.1 %copy-start.17 = (bf16[1,4,128,128]{3,2,1,0:T(8,128)(2,1)S(1)}, bf16[1,4,128,128]{3,2,1,0:T(8,128)(2,1)}, u32[]{:S(2)}) copy-start(bf16[1,4,128,128]{3,2,1,0:T(8,128)(2,1)} %param.12) | copy-start | bytes 393220
  8.5 52.9 %all-to-all-start = ((bf16[64,2,8,768]{3,2,1,0:T(8,128)(2,1)}), bf16[64,2,8,768]{3,2,1,0:T(8,128)(2,1)S(1)}, u32[]{:S(2)}, u32[]{:S(2)}) async-start(bf16[64,2,8,768]{3,2,1,0:T(8,128)(2,1)} %copy-done.4), calls=%async_computation | async-start | bytes 3145728 | tf_op jit(solution)/shard_map/all_to_all | solution.py:356
  23.8 1.4 copy-start.1
  25.2 1.3 copy-start.20
  63.5 9.2 %copy-start.19 = (f32[1,1536]{1,0:T(1,128)S(1)}, f32[1,1536]{1,0:T(1,128)}, u32[]{:S(2)}) copy-start(f32[1,1536]{1,0:T(1,128)} %gain_ref.1) | copy-start | bytes 18436
  63.5 46.2 %copy-start = (bf16[512,1536]{1,0:T(8,128)(2,1)S(1)}, bf16[512,1536]{1,0:T(8,128)(2,1)}, u32[]{:S(2)}) copy-start(bf16[512,1536]{1,0:T(8,128)(2,1)} %queued_ref.5) | copy-start | bytes 4718596
  63.5 46.2 %copy-start.14 = (f32[1,1536]{1,0:T(1,128)S(1)}, f32[1,1536]{1,0:T(1,128)}, u32[]{:S(2)}) copy-start(f32[1,1536]{1,0:T(1,128)} %channel_ref.5) | copy-start | bytes 18436
  63.5 46.2 %all-to-all-start.1 = ((bf16[64,2,8,768]{3,2,1,0:T(8,128)(2,1)}), bf16[64,2,8,768]{3,2,1,0:T(8,128)(2,1)}, u32[]{:S(2)}, u32[]{:S(2)}) async-start(bf16[64,2,8,768]{3,2,1,0:T(8,128)(2,1)} %shard_map.97), calls=%async_computation.1 | async-start | bytes 3145728 | tf_op jit(solution)/shard_map/all_to_all | solution.py:356
  69.9 8.3 %collective-permute-start.1 = (bf16[2,256,256]{2,1,0:T(8,128)(2,1)}, bf16[2,256,256]{2,1,0:T(8,128)(2,1)}, u32[]{:S(2)}, u32[]{:S(2)}) collective-permute-start(bf16[2,256,256]{2,1,0:T(8,128)(2,1)} %bitcast.21), channel_id=1, source_target_pairs={{64,0},{128,64},{192,128},{0,192},{65,1},{129,65},{193,129},{1,193... | collective-permute-start | bytes 786440 | tf_op jit(solution)/shard_map/ppermute | solution.py:371
  72.8 5.5 %collective-permute-start = (f32[1,1536]{1,0:T(1,128)S(1)}, f32[1,1536]{1,0:T(1,128)S(1)}, u32[]{:S(2)}, u32[]{:S(2)}) collective-permute-start(f32[1,1536]{1,0:T(1,128)S(1)} %copy-done.19), channel_id=1, source_target_pairs={{64,0},{128,64},{192,128},{0,192},{65,1},{129,65},{193,129},{1,193... | collective-permute-start | bytes 18440 | tf_op jit(solution)/shard_map/ppermute | solution.py:371
  109.7 1.6 copy-start.2
  111.3 1.4 copy-start.15
  127.6 1.1 copy-start.6
  128.8 0.9 copy-start.13
  129.7 0.9 copy-start.16
  130.5 29.2 %all-to-all-start.2 = ((bf16[64,8,768]{2,1,0:T(8,128)(2,1)}), bf16[64,8,768]{2,1,0:T(8,128)(2,1)}, u32[]{:S(2)}, u32[]{:S(2)}) async-start(bf16[64,8,768]{2,1,0:T(8,128)(2,1)} %copy-done.13), calls=%async_computation.2 | async-start | bytes 1572864 | tf_op jit(solution)/shard_map/all_to_all | solution.py:356
  136.8 20.3 %collective-permute-start.2 = (bf16[256,1536]{1,0:T(8,128)(2,1)}, bf16[256,1536]{1,0:T(8,128)(2,1)S(1)}, u32[]{:S(2)}, u32[]{:S(2)}) collective-permute-start(bf16[256,1536]{1,0:T(8,128)(2,1)} %copy-done.16), channel_id=1, source_target_pairs={{0,64},{64,128},{128,192},{192,0},{1,65},{65,129},{129,193},{193,1... | collective-permute-start | bytes 2359304 | tf_op jit(solution)/shard_map/ppermute | solution.py:368
  138.2 1.6 copy-start.3
  139.8 1.4 copy-start.5
  141.2 1.4 copy-start.7
  144.7 0.9 copy-start.12
  157.1 0.9 copy-start.8
  159.8 38.3 %all-to-all-start.3 = ((bf16[64,8,768]{2,1,0:T(8,128)(2,1)}), bf16[64,8,768]{2,1,0:T(8,128)(2,1)}, u32[]{:S(2)}, u32[]{:S(2)}) async-start(bf16[64,8,768]{2,1,0:T(8,128)(2,1)} %copy-done.12), calls=%async_computation.3 | async-start | bytes 1572864 | tf_op jit(solution)/shard_map/all_to_all | solution.py:356
  175.0 20.2 %collective-permute-start.5 = (bf16[64,8,768]{2,1,0:T(8,128)(2,1)}, bf16[64,8,768]{2,1,0:T(8,128)(2,1)S(1)}, u32[]{:S(2)}, u32[]{:S(2)}) collective-permute-start(bf16[64,8,768]{2,1,0:T(8,128)(2,1)} %all-to-all-done.2), channel_id=1, source_target_pairs={{0,64},{64,128},{128,192},{192,0},{1,65},{65,129},{129,193},{193,1... | collective-permute-start | bytes 2359304 | tf_op jit(solution)/shard_map/ppermute | solution.py:368
  198.0 33.1 %all-to-all-start.5 = ((bf16[64,8,768]{2,1,0:T(8,128)(2,1)}), bf16[64,8,768]{2,1,0:T(8,128)(2,1)}, u32[]{:S(2)}, u32[]{:S(2)}) async-start(bf16[64,8,768]{2,1,0:T(8,128)(2,1)} %shard_map.101), calls=%async_computation.5 | async-start | bytes 1572864 | tf_op jit(solution)/shard_map/all_to_all | solution.py:356
  208.2 20.2 %collective-permute-start.3 = (bf16[64,8,768]{2,1,0:T(8,128)(2,1)}, bf16[64,8,768]{2,1,0:T(8,128)(2,1)S(1)}, u32[]{:S(2)}, u32[]{:S(2)}) collective-permute-start(bf16[64,8,768]{2,1,0:T(8,128)(2,1)} %all-to-all-done.3), channel_id=1, source_target_pairs={{0,64},{64,128},{128,192},{192,0},{1,65},{65,129},{129,193},{193,1... | collective-permute-start | bytes 2359304 | tf_op jit(solution)/shard_map/ppermute | solution.py:368
  231.1 33.1 %all-to-all-start.4 = ((bf16[64,8,768]{2,1,0:T(8,128)(2,1)}), bf16[64,8,768]{2,1,0:T(8,128)(2,1)}, u32[]{:S(2)}, u32[]{:S(2)}) async-start(bf16[64,8,768]{2,1,0:T(8,128)(2,1)} %shard_map.100), calls=%async_computation.4 | async-start | bytes 1572864 | tf_op jit(solution)/shard_map/all_to_all | solution.py:356
  241.3 20.2 %collective-permute-start.4 = (bf16[256,1536]{1,0:T(8,128)(2,1)}, bf16[256,1536]{1,0:T(8,128)(2,1)S(1)}, u32[]{:S(2)}, u32[]{:S(2)}) collective-permute-start(bf16[256,1536]{1,0:T(8,128)(2,1)} %get-tuple-element.32), channel_id=1, source_target_pairs={{0,64},{64,128},{128,192},{192,0},{1,65},{65,129},{129,193},{193,1... | collective-permute-start | bytes 2359304 | tf_op jit(solution)/shard_map/ppermute | solution.py:368
  241.4 1.1 copy-start.9
  261.5 0.9 copy-start.10
  264.2 1.1 copy-start.11
  (1 other events, 0.7 us)

commit v4 on v2

v4 whole, which is shorter than its diff:
```python
import functools

import jax
import jax.numpy as jnp
from jax import lax
from jax.experimental import pallas as pl
from jax.experimental.pallas import tpu as pltpu
from jax.sharding import PartitionSpec as P

EPS = 1e-05
LONG = 20_000_000_000
D = 1536
HALF = D // 2
BLK = 256
DEV = 64
GROUPS = 4
WIDTH = D // GROUPS
BF = jnp.bfloat16
F32 = jnp.float32


def call(kernel, out_shape, inputs, scratch, cost, flags=None, near=(), mib=32):
    outs = out_shape if isinstance(out_shape, tuple) else (out_shape,)
    held = pl.BlockSpec(memory_space=pl.ANY)
    nearby = pl.BlockSpec(memory_space=pltpu.VMEM)
    scalars = [] if flags is None else [pl.BlockSpec(memory_space=pltpu.SMEM)]
    flops, bytes_accessed, transcendentals = cost
    results = pl.pallas_call(
        kernel,
        out_shape=outs,
        in_specs=scalars + [nearby if n in near else held for n in range(len(inputs))],
        out_specs=[held] * len(outs),
        scratch_shapes=scratch,
        cost_estimate=pl.CostEstimate(
            flops=flops, bytes_accessed=bytes_accessed, transcendentals=transcendentals
        ),
        compiler_params=pltpu.CompilerParams(vmem_limit_bytes=mib * 1024 * 1024),
    )(
        *([] if flags is None else [flags]),
        *[
            pltpu.with_memory_space_constraint(v, pltpu.VMEM) if n in near else v
            for n, v in enumerate(inputs)
        ],
    )
    return results if isinstance(out_shape, tuple) else results[0]


def hbm(value):
    return pltpu.with_memory_space_constraint(value, pltpu.HBM)


class Copies:
    def __init__(self, sems):
        self.sems, self.made = sems, []

    def start(self, source, target):
        copy = pltpu.make_async_copy(source, target, self.sems.at[len(self.made)])
        copy.start()
        self.made.append([copy, False])
        return len(self.made) - 1

    def wait(self, *which):
        for n in which or range(len(self.made)):
            if not self.made[n][1]:
                self.made[n][0].wait()
                self.made[n][1] = True


def columns_of(g):
    return pl.ds(g * WIDTH, WIDTH)


def dot(a, b):
    return jnp.dot(a, b, preferred_element_type=F32)


def onehot(rows, cols, hit):
    r = lax.broadcasted_iota(jnp.int32, (rows, cols), 0)
    c = lax.broadcasted_iota(jnp.int32, (rows, cols), 1)
    return jnp.where(hit(r, c), 1.0, 0.0).astype(BF)


def packed_at(r, j, c, h, b):
    return (((r >> 3) * 4 + 2 * c + (r & 1)) == j) & (((r >> 1) & 3) == 2 * h + b)


def pack(c, h, b):
    return onehot(2 * BLK, BLK, lambda r, j: packed_at(r, j, c, h, b))


def whole_at(r, j, b):
    return (((r >> 3) * 4 + (r & 3)) == j) & (((r >> 2) & 1) == b)


def unpack_compact(h):
    return onehot(
        BLK, 2 * BLK, lambda q, r: r == ((q & 127) >> 1) * 8 + 4 * h + 2 * (q >> 7) + (q & 1)
    )


def pick(c):
    return onehot(BLK // 2, BLK, lambda q, j: j == (q >> 1) * 4 + 2 * c + (q & 1))


def place(c):
    return onehot(BLK, BLK // 2, lambda j, q: j == (q >> 1) * 4 + 2 * c + (q & 1))


def normalize(values, gain):
    scale = lax.rsqrt(jnp.mean(values * values, axis=-1, keepdims=True) + EPS)
    return (values * scale * gain).astype(BF)


def packed_part(packs, mixed):
    total = None
    for b in range(2):
        for h in range(2):
            term = dot(packs(h, b), mixed[b][:, h * HALF : (h + 1) * HALF])
            total = term if total is None else total + term
    return total.astype(BF).reshape(-1, 8, HALF)


def first_kernel(x_ref, gain_ref, factor_ref, out_ref, x_buf, gain_buf, factor_buf, out_buf, sems):
    copies = Copies(sems)
    rows = [pl.ds(b * BLK, BLK) for b in range(2)]
    loads = [
        copies.start(x_ref.at[rows[0]], x_buf.at[rows[0]]),
        copies.start(gain_ref, gain_buf),
        copies.start(factor_ref, factor_buf),
        copies.start(x_ref.at[rows[1]], x_buf.at[rows[1]]),
    ]
    packs = [onehot(2 * BLK, BLK, lambda r, j: whole_at(r, j, b)) for b in range(2)]
    mixed = []
    for b in range(2):
        copies.wait(loads[3 * b], loads[1], loads[2])
        normed = normalize(x_buf[rows[b], :].astype(F32), gain_buf[...])
        mixed.append(dot(factor_buf[b], normed).astype(BF))
    for g in range(GROUPS):
        part = columns_of(g)
        at = slice(g * WIDTH, (g + 1) * WIDTH)
        total = dot(packs[0], mixed[0][:, at]) + dot(packs[1], mixed[1][:, at])
        out_buf[:, :, part] = total.astype(BF).reshape(DEV, 8, WIDTH)
        copies.start(out_buf.at[:, :, part], out_ref.at[:, :, part])
    copies.wait()


def spread_kernel(cross_ref, whole_ref, out_ref, cross_buf, whole_buf, out_buf, sems):
    copies = Copies(sems)
    copies.start(cross_ref, cross_buf)
    copies.wait()
    n = 2 * BLK
    row = lax.broadcasted_iota(jnp.int32, (n, n), 0)
    col = lax.broadcasted_iota(jnp.int32, (n, n), 1)
    cross = cross_buf[...].reshape(n, 128)

    def spread(rows, columns, mask):
        full = dot(dot(onehot(n, n, rows), cross).astype(BF), onehot(128, n, columns))
        return jnp.where(((row ^ col) & mask) == 0, full, 0.0).astype(BF)

    whole_buf[...] = spread(
        lambda r, k: k == (r & 3) * 128 + (r >> 3) * 2 + ((r >> 2) & 1),
        lambda m, k: m == (k >> 3) * 2 + ((k >> 2) & 1),
        3,
    )
    copies.start(whole_buf, whole_ref)
    for c in range(2):
        out_buf[c] = spread(
            lambda r, k: k == (2 * c + (r & 1)) * 128 + (r >> 3) * 2 + ((r >> 1) & 1),
            lambda m, k: m == (k >> 3) * 2 + ((k >> 1) & 1),
            5,
        )
    copies.start(out_buf, out_ref)
    copies.wait()


def cross_kernel(c, spread_ref, r_ref, out_ref, spread_buf, out_buf, sems):
    copies = Copies(sems)
    copies.start(spread_ref if c is None else spread_ref.at[c], spread_buf)
    copies.wait()
    for g in range(out_ref.shape[2] // WIDTH):
        part = columns_of(g)
        total = dot(spread_buf[...], r_ref[:, :, part].reshape(2 * BLK, WIDTH))
        out_buf[:, :, part] = total.astype(BF).reshape(DEV, 8, WIDTH)
        copies.start(out_buf.at[:, :, part], out_ref.at[:, :, part])
    copies.wait()


def gelu(hidden):
    value = hidden.astype(BF)
    half = value * BF(0.5)
    inner = value * (BF(0.7978845608028654) + BF(0.7978845608028654 * 0.044715) * (value * value))
    return half + half * jnp.tanh(inner)


def channel_rows(residual, gain, up, down, store):
    normed = normalize(residual, gain)
    for g in range(GROUPS):
        part = slice(g * WIDTH, (g + 1) * WIDTH)
        act = gelu(dot(normed[:, part], up(g)))
        store(g, part, (residual[:, part] + dot(act, down(g))).astype(BF))


def weight_loads(copies, up_ref, down_ref, up_buf, down_buf):
    loads = [
        (
            copies.start(up_ref.at[g], up_buf.at[g]),
            copies.start(down_ref.at[g], down_buf.at[g]),
        )
        for g in range(GROUPS)
    ]

    def up(g):
        copies.wait(loads[g][0])
        return up_buf[g]

    def down(g):
        copies.wait(loads[g][1])
        return down_buf[g]

    return up, down


def middle_kernel(
    flag_ref,
    x_ref,
    across_ref,
    channel_ref,
    up_ref,
    down_ref,
    queued_ref,
    gain_ref,
    factor_ref,
    first_ref,
    entering_ref,
    mixed_ref,
    out_ref,
    x_buf,
    channel_buf,
    up_buf,
    down_buf,
    gain_buf,
    factor_buf,
    first_buf,
    entering_buf,
    mixed_buf,
    out_buf,
    sems,
    queued_sem,
):
    copies = Copies(sems)
    channel_load = copies.start(channel_ref, channel_buf)
    rows = [pl.ds(b * BLK, BLK) for b in range(2)]
    x_loads = [copies.start(x_ref.at[rows[b]], x_buf.at[rows[b]]) for b in range(2)]
    up, down = weight_loads(copies, up_ref, down_ref, up_buf, down_buf)
    late = [copies.start(gain_ref, gain_buf), copies.start(factor_ref, factor_buf)]
    queued = pltpu.make_async_copy(queued_ref, entering_buf, queued_sem.at[0])
    last = flag_ref[0] == 1

    @pl.when(last)
    def _():
        queued.start()

    unpacks = [onehot(BLK, 2 * BLK, lambda j, r: whole_at(r, j, b)) for b in range(2)]
    residuals = [[], []]
    for g in range(GROUPS):
        packed = across_ref[:, :, columns_of(g)].reshape(2 * BLK, WIDTH)
        for b in range(2):
            residuals[b].append(dot(unpacks[b], packed))
    copies.wait(channel_load)
    for b in range(2):

        def store(g, part, value):
            first_buf[rows[b], part] = value

        copies.wait(x_loads[b])
        residual = x_buf[rows[b], :].astype(F32) + jnp.concatenate(residuals[b], axis=1)
        channel_rows(residual, channel_buf[...], up, down, store)
        copies.start(first_buf.at[rows[b]], first_ref.at[rows[b]])

    @pl.when(last)
    def _():
        queued.wait()

    @pl.when(jnp.logical_not(last))
    def _():
        entering_buf[...] = first_buf[...]

    copies.wait(*late)
    mixed = []
    for b in range(2):
        copies.start(entering_buf.at[rows[b]], entering_ref.at[rows[b]])
        normed = normalize(entering_buf[rows[b], :].astype(F32), gain_buf[...])
        mixed.append(dot(factor_buf[b], normed).astype(BF))
        mixed_buf[rows[b], :] = mixed[b]
        copies.start(mixed_buf.at[rows[b]], mixed_ref.at[rows[b]])
    for n in range(2):
        part = slice(n * BLK, (n + 1) * BLK)
        devices = pl.ds(n * (DEV // 2), DEV // 2)
        out_buf[devices] = packed_part(lambda h, b: pack(0, h, b)[part], mixed)
        copies.start(out_buf.at[devices], out_ref.at[devices])
    copies.wait()


def remainder_kernel(
    entering_ref,
    mixed_ref,
    kept0_ref,
    kept1_ref,
    out_ref,
    entering_buf,
    mixed_buf,
    kept_buf,
    out_buf,
    sems,
):
    copies = Copies(sems)
    copies.start(entering_ref, entering_buf)
    copies.start(mixed_ref, mixed_buf)
    copies.wait(0)
    for c, kept_ref in enumerate((kept0_ref, kept1_ref)):
        for b in range(2):
            rows = pl.ds(b * (BLK // 2), BLK // 2)
            kept = dot(pick(c), entering_buf[b * BLK : (b + 1) * BLK, :])
            kept_buf[c, rows, :] = kept.astype(BF)
        copies.start(kept_buf.at[c], kept_ref)
    copies.wait(1)
    mixed = [mixed_buf[b * BLK : (b + 1) * BLK, :] for b in range(2)]
    out_buf[...] = packed_part(functools.partial(pack, 1), mixed)
    copies.start(out_buf, out_ref)
    copies.wait()


def last_kernel(
    x_ref,
    across_ref,
    channel_ref,
    up_ref,
    down_ref,
    *rest,
):
    whole = len(rest) > 7
    if whole:
        other_ref, out_ref, x_buf, channel_buf, up_buf, down_buf, other_buf, out_buf, sems = rest
    else:
        out_ref, x_buf, channel_buf, up_buf, down_buf, out_buf, sems = rest
    copies = Copies(sems)
    loads = [
        copies.start(x_ref, x_buf),
        copies.start(channel_ref, channel_buf),
    ]
    up, down = weight_loads(copies, up_ref, down_ref, up_buf, down_buf)
    if whole:
        other = copies.start(other_ref, other_buf)

    def store(g, part, value):
        if whole:
            copies.wait(other)
            for b in range(2):
                rows = slice(b * (BLK // 2), (b + 1) * (BLK // 2))
                joined = dot(places[0], other_buf[rows, part]) + dot(places[1], value[rows])
                out_buf[b * BLK : (b + 1) * BLK, part] = joined.astype(BF)
        else:
            out_buf[:, part] = value
        copies.start(out_buf.at[:, columns_of(g)], out_ref.at[:, columns_of(g)])

    places = [place(c) for c in range(2)] if whole else None
    compact = [unpack_compact(h) for h in range(2)]
    copies.wait(*loads)
    packed = across_ref[...].reshape(2 * BLK, HALF)
    across = jnp.concatenate([dot(compact[h], packed) for h in range(2)], axis=1)
    channel_rows(x_buf[...].astype(F32) + across, channel_buf[...], up, down, store)
    copies.wait()


def pass_kernel(value_ref, other_ref, out_ref):
    pass


def after(value, other, near=False):
    return pl.pallas_call(
        pass_kernel,
        out_shape=jax.ShapeDtypeStruct(value.shape, value.dtype),
        in_specs=[
            pl.BlockSpec(memory_space=pl.ANY),
            pl.BlockSpec(memory_space=pltpu.VMEM if near else pl.ANY),
        ],
        out_specs=pl.BlockSpec(memory_space=pl.ANY),
        input_output_aliases={0: 0},
        cost_estimate=pl.CostEstimate(flops=LONG, bytes_accessed=0, transcendentals=0),
    )(value, pltpu.with_memory_space_constraint(other, pltpu.VMEM) if near else other)


def shape(*dims):
    return jax.ShapeDtypeStruct(dims, BF)


def exchange(value):
    return lax.all_to_all(hbm(value), "seq", split_axis=0, concat_axis=0, tiled=True)


def per_device(arriving, queued, norm_gain, block_factor, cross_factor, channel_gain, up, down):
    section = lax.axis_index("section")
    count = lax.axis_size("section")
    flags = jnp.full((1,), section == count - 1, jnp.int32)
    x = arriving[0]
    factor, cross, up, down = block_factor[0], cross_factor[0], up[0], down[0]
    held_x, held_factor, held_gain = hbm(x), hbm(factor), hbm(norm_gain)
    cross, up, down, queued, channel_gain = (
        hbm(v) for v in (cross, up, down, queued, channel_gain)
    )

    def ahead(value):
        return lax.ppermute(value, "section", [(s, (s + 1) % count) for s in range(count)])

    def behind(value):
        return lax.ppermute(value, "section", [((s + 1) % count, s) for s in range(count)])

    message, both = shape(DEV, 8, HALF), shape(DEV, 8, D)
    sequence, part_rows = shape(2 * BLK, D), shape(BLK, D)
    far = pltpu.HBM(sequence.shape, BF)

    def buf(value):
        return pltpu.VMEM(value.shape, value.dtype)

    def sems(n):
        return pltpu.SemaphoreType.DMA((n,))

    sent = call(
        first_kernel,
        both,
        [held_x, held_gain, held_factor],
        [buf(x), buf(norm_gain), buf(factor), buf(both), sems(8)],
        (2_000_000_000, 4_000_000, 0),
    )
    columns = exchange(sent)
    square = shape(2 * BLK, 2 * BLK)
    whole, spread = call(
        spread_kernel,
        (square, shape(2, 2 * BLK, 2 * BLK)),
        [cross],
        [buf(cross), buf(square), buf(shape(2, 2 * BLK, 2 * BLK)), sems(3)],
        (600_000_000, 5_000_000, 0),
    )
    next_gain, next_factor = behind(norm_gain), behind(factor)

    out = call(
        functools.partial(cross_kernel, None),
        both,
        [whole, columns],
        [buf(square), buf(both), sems(5)],
        (800_000_000, 4_000_000, 0),
        near=(1,),
        mib=16,
    )
    across = exchange(out)

    first, entering, mixed, sent0 = call(
        middle_kernel,
        (sequence, far, far, message),
        [held_x, across, channel_gain, up, down, queued, next_gain, next_factor],
        [
            buf(x),
            buf(channel_gain),
            buf(up),
            buf(down),
            buf(norm_gain),
            buf(factor),
            buf(x),
            buf(x),
            buf(x),
            buf(message),
            sems(21),
            sems(1),
        ],
        (7_000_000_000, 18_000_000, 2_000_000),
        flags,
        near=(1,),
    )
    columns0 = exchange(sent0)
    kept0, kept1, sent1 = call(
        remainder_kernel,
        (part_rows, part_rows, message),
        [entering, mixed],
        [buf(x), buf(x), buf(shape(2, BLK, D)), buf(message), sems(5)],
        (1_000_000_000, 5_000_000, 0),
    )
    x0 = ahead(kept0)
    columns0, x0 = lax.optimization_barrier((columns0, x0))
    columns0, sent1 = lax.optimization_barrier((columns0, sent1))
    columns0 = ahead(columns0)
    columns1 = exchange(sent1)

    def crossed(c, value):
        return call(
            functools.partial(cross_kernel, c),
            message,
            [spread, value],
            [buf(square), buf(message), sems(3)],
            (LONG, 2_000_000, 0),
            near=(1,),
            mib=12,
        )

    across0 = exchange(after(crossed(0, columns0), columns1))
    columns1 = ahead(columns1)
    kept1, columns1 = lax.optimization_barrier((kept1, columns1))
    x1 = ahead(kept1)
    across1 = exchange(after(crossed(1, columns1), across0, True))
    bufs = [buf(part_rows), buf(channel_gain), buf(up), buf(down)]
    other = call(
        last_kernel,
        pltpu.HBM(part_rows.shape, BF),
        [x0, across0, channel_gain, up, down],
        [*bufs, buf(part_rows), sems(14)],
        (2_500_000_000, 10_000_000, 1_000_000),
        near=(1,),
    )
    second = call(
        last_kernel,
        sequence,
        [hbm(x1), across1, channel_gain, up, down, hbm(other)],
        [*bufs, buf(part_rows), buf(sequence), sems(15)],
        (3_000_000_000, 11_000_000, 1_000_000),
        near=(1,),
    )
    return first.reshape(1, *x.shape), second.reshape(1, *x.shape)


def solution(mesh):
    placed = (
        P("section", "seq", None),
        P("seq", None),
        P("section", None),
        P("section", "seq", None, None),
        P("section", "seq", None, None),
        P("section", None),
        P("section", None, None, None),
        P("section", None, None, None),
    )
    return jax.shard_map(
        per_device,
        mesh=mesh,
        in_specs=placed,
        out_specs=(P("section", "seq", None), P("section", "seq", None)),
        check_vma=False,
    )
```

time: 282 us -> 252 us (0.89)
  local copies, waits for them, and re-layouts: 23.6 us -> 6.66 us
  waiting for transfers between devices: 161 us -> 146 us
  Pallas kernels: 36.1 us -> 39.4 us
    unnamed x56 -> x18, local copies, waits for them, and re-layouts: 23.6 us -> 6.66 us
    ppermute x4, waiting for transfers between devices: 66.2 us -> 51.3 us  [ahead(): lax.ppermute(value, 'section', [(s, (s + 1) % count) for s in range(count)])]
    all_to_all x6, starting transfers between devices: 53.5 us -> 50.1 us  [exchange(): lax.all_to_all(hbm(value), 'seq', split_axis=0, concat_axis=0, tiled=True)]
    pallas_call x9 -> x11, Pallas kernels: 36.1 us -> 39.4 us  [the longest x9 39.4 us: call(): pl.pallas_call(kernel, out_shape=outs, in_specs=scalars + [nearby if n in...]
  transfers between devices with their start and end apart: 12 -> 12, of which waited for: 9 -> 10; matrix products, arithmetic and copies ran while one was open for 0% -> 0% of each run, Pallas kernels for 4% -> 5%
where the time goes in v4:
time: 252 us; the launch traced here: 251 us
  waiting for transfers between devices  146 us (58%)
  starting transfers between devices  57.6 us (23%)
  Pallas kernels  39.4 us (16%)
  local copies, waits for them, and re-layouts  6.66 us (3%)
    all_to_all x6, waiting for transfers between devices, exchange(): lax.all_to_all(hbm(value), 'seq', split_axis=0, concat_axis=0, tiled=True)  90.2 us
    ppermute x4, waiting for transfers between devices, ahead(): lax.ppermute(value, 'section', [(s, (s + 1) % count) for s in range(count)])  51.3 us
    all_to_all x6, starting transfers between devices, exchange(): lax.all_to_all(hbm(value), 'seq', split_axis=0, concat_axis=0, tiled=True)  50.1 us
    pallas_call x9, Pallas kernels, call(): pl.pallas_call(kernel, out_shape=outs, in_specs=scalars + [nearby if n in...  39.4 us
    unnamed x18, local copies, waits for them, and re-layouts  6.66 us
  transfers between devices with their start and end apart: 12, of which 10 were waited for; matrix products, arithmetic and copies ran while one was open for 0% of the time, Pallas kernels for 5%

profile of v4, /device:TPU:1, one launch (start us, length us, event | category | flops | bytes accessed | tf_op | source)
XLA Modules:
  0.0 251.1 jit_solution(8998367129440289809)
XLA Ops:
  0.6 4.3 %shard_map.96 = bf16[64,8,1536]{2,1,0:T(8,128)(2,1)} custom-call(bf16[512,1536]{1,0:T(8,128)(2,1)} %bitcast.14, f32[1,1536]{1,0:T(1,128)} %gain_ref.1, bf16[2,256,256]{2,1,0:T(8,128)(2,1)} %bitcast.16), custom_call_target="tpu_custom_call" | custom-call | flops 2000000000 | bytes 4000000 | tf_op jit(solution)/shard_map/pallas_call | solution.py:28
  5.0 13.0 %all-to-all-start = ((bf16[64,8,1536]{2,1,0:T(8,128)(2,1)}), bf16[64,8,1536]{2,1,0:T(8,128)(2,1)S(1)}, u32[]{:S(2)}, u32[]{:S(2)}) async-start(bf16[64,8,1536]{2,1,0:T(8,128)(2,1)} %shard_map.96), calls=%async_computation | async-start | bytes 3145728 | tf_op jit(solution)/shard_map/all_to_all | solution.py:398
  18.0 2.7 %shard_map.95 = (bf16[512,512]{1,0:T(8,128)(2,1)S(1)}, bf16[2,512,512]{2,1,0:T(8,128)(2,1)S(1)}) custom-call(bf16[4,128,128]{2,1,0:T(8,128)(2,1)} %bitcast.18), custom_call_target="tpu_custom_call" | custom-call | flops 600000000 | bytes 5000000 | tf_op jit(solution)/shard_map/pallas_call | solution.py:28
  21.6 36.1 %all-to-all-done.r_ref = bf16[64,8,1536]{2,1,0:T(8,128)(2,1)S(1)} async-done(((bf16[64,8,1536]{2,1,0:T(8,128)(2,1)}), bf16[64,8,1536]{2,1,0:T(8,128)(2,1)S(1)}, u32[]{:S(2)}, u32[]{:S(2)}) %all-to-all-start) | async-done | bytes 1572896 | tf_op jit(solution)/shard_map/all_to_all | solution.py:398
  57.7 2.1 shard_map.97
  59.9 6.3 %all-to-all-start.1 = ((bf16[64,8,1536]{2,1,0:T(8,128)(2,1)}), bf16[64,8,1536]{2,1,0:T(8,128)(2,1)S(1)}, u32[]{:S(2)}, u32[]{:S(2)}) async-start(bf16[64,8,1536]{2,1,0:T(8,128)(2,1)} %shard_map.97), calls=%async_computation.1 | async-start | bytes 3145728 | tf_op jit(solution)/shard_map/all_to_all | solution.py:398
  66.1 2.8 %collective-permute-start.1 = (bf16[2,256,256]{2,1,0:T(8,128)(2,1)S(1)}, bf16[2,256,256]{2,1,0:T(8,128)(2,1)S(1)}, u32[]{:S(2)}, u32[]{:S(2)}) collective-permute-start(bf16[2,256,256]{2,1,0:T(8,128)(2,1)S(1)} %bitcast.17), channel_id=1, source_target_pairs={{64,0},{128,64},{192,128},{0,192},{65,1},{129,65},{193,129},{1,193... | collective-permute-start | bytes 786440 | tf_op jit(solution)/shard_map/ppermute | solution.py:416
  69.4 4.9 %collective-permute-done.gain_ref = f32[1,1536]{1,0:T(1,128)S(1)} collective-permute-done((f32[1,1536]{1,0:T(1,128)S(1)}, f32[1,1536]{1,0:T(1,128)S(1)}, u32[]{:S(2)}, u32[]{:S(2)}) %collective-permute-start) | collective-permute-done | bytes 6176 | tf_op jit(solution)/shard_map/ppermute | solution.py:416
  74.3 31.6 %all-to-all-done.1.across_ref = bf16[64,8,1536]{2,1,0:T(8,128)(2,1)S(1)} async-done(((bf16[64,8,1536]{2,1,0:T(8,128)(2,1)}), bf16[64,8,1536]{2,1,0:T(8,128)(2,1)S(1)}, u32[]{:S(2)}, u32[]{:S(2)}) %all-to-all-start.1) | async-done | bytes 1572896 | tf_op jit(solution)/shard_map/all_to_all | solution.py:398
  105.9 11.1 %shard_map.98 = (bf16[512,1536]{1,0:T(8,128)(2,1)}, bf16[512,1536]{1,0:T(8,128)(2,1)}, bf16[512,1536]{1,0:T(8,128)(2,1)}, bf16[64,8,768]{2,1,0:T(8,128)(2,1)}) custom-call(s32[1]{0:T(128)} %bitcast.flag_ref, bf16[512,1536]{1,0:T(8,128)(2,1)} %bitcast.15, bf16[64,8,1536]{2,1,0:T(8,128)(2,1)S(1)} %all-to-all-done.1.across_ref, f32[1,1536]{1,0:T(1,128)} %channel_ref.5, ...), custom_call_target="tpu_custom_call" | custom-call | flops 7000000000 | bytes 18000000 | tf_op jit(solution)/shard_map/pallas_call | solution.py:28
  117.1 6.4 %all-to-all-start.2 = ((bf16[64,8,768]{2,1,0:T(8,128)(2,1)}), bf16[64,8,768]{2,1,0:T(8,128)(2,1)}, u32[]{:S(2)}, u32[]{:S(2)}) async-start(bf16[64,8,768]{2,1,0:T(8,128)(2,1)} %get-tuple-element.22), calls=%async_computation.2 | async-start | bytes 1572864 | tf_op jit(solution)/shard_map/all_to_all | solution.py:398
  123.5 1.4 copy-done.3
  124.9 3.0 %shard_map.99 = (bf16[256,1536]{1,0:T(8,128)(2,1)S(1)}, bf16[256,1536]{1,0:T(8,128)(2,1)S(1)}, bf16[64,8,768]{2,1,0:T(8,128)(2,1)}) custom-call(bf16[512,1536]{1,0:T(8,128)(2,1)S(1)} %copy-done.2, bf16[512,1536]{1,0:T(8,128)(2,1)S(1)} %copy-done.3), custom_call_target="tpu_custom_call" | custom-call | flops 1000000000 | bytes 5000000 | tf_op jit(solution)/shard_map/pallas_call | solution.py:28
  128.0 1.6 collective-permute-start.2
  129.6 18.5 %collective-permute-done.2.x_ref = bf16[256,1536]{1,0:T(8,128)(2,1)S(1)} collective-permute-done((bf16[256,1536]{1,0:T(8,128)(2,1)S(1)}, bf16[256,1536]{1,0:T(8,128)(2,1)S(1)}, u32[]{:S(2)}, u32[]{:S(2)}) %collective-permute-start.2) | collective-permute-done | bytes 786464 | tf_op jit(solution)/shard_map/ppermute | solution.py:413
  148.2 11.8 %all-to-all-start.3 = ((bf16[64,8,768]{2,1,0:T(8,128)(2,1)}), bf16[64,8,768]{2,1,0:T(8,128)(2,1)}, u32[]{:S(2)}, u32[]{:S(2)}) async-start(bf16[64,8,768]{2,1,0:T(8,128)(2,1)} %get-tuple-element.26), calls=%async_computation.3 | async-start | bytes 1572864 | tf_op jit(solution)/shard_map/all_to_all | solution.py:398
  159.9 7.3 %collective-permute-done.5.r_ref = bf16[64,8,768]{2,1,0:T(8,128)(2,1)S(1)} collective-permute-done((bf16[64,8,768]{2,1,0:T(8,128)(2,1)}, bf16[64,8,768]{2,1,0:T(8,128)(2,1)S(1)}, u32[]{:S(2)}, u32[]{:S(2)}) %collective-permute-start.5) | collective-permute-done | bytes 786464 | tf_op jit(solution)/shard_map/ppermute | solution.py:413
  167.3 1.2 copy-done.5
  168.5 1.0 shard_map.101.value_ref
  170.5 12.4 %all-to-all-done.3.other_ref = bf16[64,8,768]{2,1,0:T(8,128)(2,1)} async-done(((bf16[64,8,768]{2,1,0:T(8,128)(2,1)}), bf16[64,8,768]{2,1,0:T(8,128)(2,1)}, u32[]{:S(2)}, u32[]{:S(2)}) %all-to-all-start.3) | async-done | bytes 786464 | tf_op jit(solution)/shard_map/all_to_all | solution.py:398
  182.9 1.3 collective-permute-start.3
  184.2 6.5 %all-to-all-start.4 = ((bf16[64,8,768]{2,1,0:T(8,128)(2,1)}), bf16[64,8,768]{2,1,0:T(8,128)(2,1)S(1)}, u32[]{:S(2)}, u32[]{:S(2)}) async-start(bf16[64,8,768]{2,1,0:T(8,128)(2,1)} %shard_map.102), calls=%async_computation.4 | async-start | bytes 1572864 | tf_op jit(solution)/shard_map/all_to_all | solution.py:398
  190.6 12.4 %collective-permute-done.3.r_ref = bf16[64,8,768]{2,1,0:T(8,128)(2,1)S(1)} collective-permute-done((bf16[64,8,768]{2,1,0:T(8,128)(2,1)}, bf16[64,8,768]{2,1,0:T(8,128)(2,1)S(1)}, u32[]{:S(2)}, u32[]{:S(2)}) %collective-permute-start.3) | collective-permute-done | bytes 786464 | tf_op jit(solution)/shard_map/ppermute | solution.py:413
  203.0 1.2 copy-done.6
  204.2 1.0 shard_map.100.value_ref
  206.2 7.5 %all-to-all-done.4.other_ref.across_ref = bf16[64,8,768]{2,1,0:T(8,128)(2,1)S(1)} async-done(((bf16[64,8,768]{2,1,0:T(8,128)(2,1)}), bf16[64,8,768]{2,1,0:T(8,128)(2,1)S(1)}, u32[]{:S(2)}, u32[]{:S(2)}) %all-to-all-start.4) | async-done | bytes 786464 | tf_op jit(solution)/shard_map/all_to_all | solution.py:398
  213.6 6.2 %all-to-all-start.5 = ((bf16[64,8,768]{2,1,0:T(8,128)(2,1)}), bf16[64,8,768]{2,1,0:T(8,128)(2,1)S(1)}, u32[]{:S(2)}, u32[]{:S(2)}) async-start(bf16[64,8,768]{2,1,0:T(8,128)(2,1)} %shard_map.103), calls=%async_computation.5 | async-start | bytes 1572864 | tf_op jit(solution)/shard_map/all_to_all | solution.py:398
  219.8 1.2 collective-permute-start.4
  221.1 6.0 %shard_map.104.rest_0_ = bf16[256,1536]{1,0:T(8,128)(2,1)} custom-call(bf16[256,1536]{1,0:T(8,128)(2,1)S(1)} %collective-permute-done.2.x_ref, bf16[64,8,768]{2,1,0:T(8,128)(2,1)S(1)} %all-to-all-done.4.other_ref.across_ref, f32[1,1536]{1,0:T(1,128)} %channel_ref.5, bf16[4,384,1024]{2,1,0:T(8,128)(2,1)} %bitcast.9, bf16[4,1024,384]{2,1,0:T(8,128)(2,1)} %bitcast.12), custom_call_target="tpu_custom_call" | custom-call | flops 2500000000 | bytes 10000000 | tf_op jit(solution)/shard_map/pallas_call | solution.py:28
  227.0 13.1 %collective-permute-done.4.x_ref = bf16[256,1536]{1,0:T(8,128)(2,1)} collective-permute-done((bf16[256,1536]{1,0:T(8,128)(2,1)S(1)}, bf16[256,1536]{1,0:T(8,128)(2,1)}, u32[]{:S(2)}, u32[]{:S(2)}) %collective-permute-start.4) | collective-permute-done | bytes 786464 | tf_op jit(solution)/shard_map/ppermute | solution.py:413
  240.1 2.7 %all-to-all-done.5.across_ref = bf16[64,8,768]{2,1,0:T(8,128)(2,1)S(1)} async-done(((bf16[64,8,768]{2,1,0:T(8,128)(2,1)}), bf16[64,8,768]{2,1,0:T(8,128)(2,1)S(1)}, u32[]{:S(2)}, u32[]{:S(2)}) %all-to-all-start.5) | async-done | bytes 786464 | tf_op jit(solution)/shard_map/all_to_all | solution.py:398
  242.8 8.1 %shard_map.105 = bf16[512,1536]{1,0:T(8,128)(2,1)} custom-call(bf16[256,1536]{1,0:T(8,128)(2,1)} %collective-permute-done.4.x_ref, bf16[64,8,768]{2,1,0:T(8,128)(2,1)S(1)} %all-to-all-done.5.across_ref, f32[1,1536]{1,0:T(1,128)} %channel_ref.5, bf16[4,384,1024]{2,1,0:T(8,128)(2,1)} %bitcast.10, bf16[4,1024,384]{2,1,0:T(8,128)(2,1)} %bitcast.13, ...), custom_call_target="tpu_custom_call" | custom-call | flops 3000000000 | bytes 11000000 | tf_op jit(solution)/shard_map/pallas_call | solution.py:28
  (21 shorter events, 3.4 us)
Async XLA Ops:
  5.0 52.8 %all-to-all-start = ((bf16[64,8,1536]{2,1,0:T(8,128)(2,1)}), bf16[64,8,1536]{2,1,0:T(8,128)(2,1)S(1)}, u32[]{:S(2)}, u32[]{:S(2)}) async-start(bf16[64,8,1536]{2,1,0:T(8,128)(2,1)} %shard_map.96), calls=%async_computation | async-start | bytes 3145728 | tf_op jit(solution)/shard_map/all_to_all | solution.py:398
  20.6 1.0 copy-start.4
  59.8 6.3 %copy-start.7 = (bf16[1,2,256,256]{3,2,1,0:T(8,128)(2,1)S(1)}, bf16[1,2,256,256]{3,2,1,0:T(8,128)(2,1)}, u32[]{:S(2)}) copy-start(bf16[1,2,256,256]{3,2,1,0:T(8,128)(2,1)} %param.11) | copy-start | bytes 786436
  59.8 9.1 %copy-start.8 = (f32[1,1536]{1,0:T(1,128)S(1)}, f32[1,1536]{1,0:T(1,128)}, u32[]{:S(2)}) copy-start(f32[1,1536]{1,0:T(1,128)} %gain_ref.1) | copy-start | bytes 18436
  59.9 46.1 %all-to-all-start.1 = ((bf16[64,8,1536]{2,1,0:T(8,128)(2,1)}), bf16[64,8,1536]{2,1,0:T(8,128)(2,1)S(1)}, u32[]{:S(2)}, u32[]{:S(2)}) async-start(bf16[64,8,1536]{2,1,0:T(8,128)(2,1)} %shard_map.97), calls=%async_computation.1 | async-start | bytes 3145728 | tf_op jit(solution)/shard_map/all_to_all | solution.py:398
  66.1 8.2 %collective-permute-start.1 = (bf16[2,256,256]{2,1,0:T(8,128)(2,1)S(1)}, bf16[2,256,256]{2,1,0:T(8,128)(2,1)S(1)}, u32[]{:S(2)}, u32[]{:S(2)}) collective-permute-start(bf16[2,256,256]{2,1,0:T(8,128)(2,1)S(1)} %bitcast.17), channel_id=1, source_target_pairs={{64,0},{128,64},{192,128},{0,192},{65,1},{129,65},{193,129},{1,193... | collective-permute-start | bytes 786440 | tf_op jit(solution)/shard_map/ppermute | solution.py:416
  69.0 5.4 %collective-permute-start = (f32[1,1536]{1,0:T(1,128)S(1)}, f32[1,1536]{1,0:T(1,128)S(1)}, u32[]{:S(2)}, u32[]{:S(2)}) collective-permute-start(f32[1,1536]{1,0:T(1,128)S(1)} %copy-done.8), channel_id=1, source_target_pairs={{64,0},{128,64},{192,128},{0,192},{65,1},{129,65},{193,129},{1,193... | collective-permute-start | bytes 18440 | tf_op jit(solution)/shard_map/ppermute | solution.py:416
  117.1 6.4 %copy-start.2 = (bf16[512,1536]{1,0:T(8,128)(2,1)S(1)}, bf16[512,1536]{1,0:T(8,128)(2,1)}, u32[]{:S(2)}) copy-start(bf16[512,1536]{1,0:T(8,128)(2,1)} %get-tuple-element.19.entering_ref) | copy-start | bytes 4718596
  117.1 31.0 %all-to-all-start.2 = ((bf16[64,8,768]{2,1,0:T(8,128)(2,1)}), bf16[64,8,768]{2,1,0:T(8,128)(2,1)}, u32[]{:S(2)}, u32[]{:S(2)}) async-start(bf16[64,8,768]{2,1,0:T(8,128)(2,1)} %get-tuple-element.22), calls=%async_computation.2 | async-start | bytes 1572864 | tf_op jit(solution)/shard_map/all_to_all | solution.py:398
  123.5 1.4 copy-start.3
  128.0 20.1 %collective-permute-start.2 = (bf16[256,1536]{1,0:T(8,128)(2,1)S(1)}, bf16[256,1536]{1,0:T(8,128)(2,1)S(1)}, u32[]{:S(2)}, u32[]{:S(2)}) collective-permute-start(bf16[256,1536]{1,0:T(8,128)(2,1)S(1)} %get-tuple-element.23), channel_id=1, source_target_pairs={{0,64},{64,128},{128,192},{192,0},{1,65},{65,129},{129,193},{193,1... | collective-permute-start | bytes 2359304 | tf_op jit(solution)/shard_map/ppermute | solution.py:413
  148.1 19.2 %collective-permute-start.5 = (bf16[64,8,768]{2,1,0:T(8,128)(2,1)}, bf16[64,8,768]{2,1,0:T(8,128)(2,1)S(1)}, u32[]{:S(2)}, u32[]{:S(2)}) collective-permute-start(bf16[64,8,768]{2,1,0:T(8,128)(2,1)} %all-to-all-done.2), channel_id=1, source_target_pairs={{0,64},{64,128},{128,192},{192,0},{1,65},{65,129},{129,193},{193,1... | collective-permute-start | bytes 2359304 | tf_op jit(solution)/shard_map/ppermute | solution.py:413
  148.2 34.7 %all-to-all-start.3 = ((bf16[64,8,768]{2,1,0:T(8,128)(2,1)}), bf16[64,8,768]{2,1,0:T(8,128)(2,1)}, u32[]{:S(2)}, u32[]{:S(2)}) async-start(bf16[64,8,768]{2,1,0:T(8,128)(2,1)} %get-tuple-element.26), calls=%async_computation.3 | async-start | bytes 1572864 | tf_op jit(solution)/shard_map/all_to_all | solution.py:398
  167.3 1.2 copy-start.5
  169.5 0.9 copy-start
  182.9 20.1 %collective-permute-start.3 = (bf16[64,8,768]{2,1,0:T(8,128)(2,1)}, bf16[64,8,768]{2,1,0:T(8,128)(2,1)S(1)}, u32[]{:S(2)}, u32[]{:S(2)}) collective-permute-start(bf16[64,8,768]{2,1,0:T(8,128)(2,1)} %all-to-all-done.3.other_ref), channel_id=1, source_target_pairs={{0,64},{64,128},{128,192},{192,0},{1,65},{65,129},{129,193},{193,1... | collective-permute-start | bytes 2359304 | tf_op jit(solution)/shard_map/ppermute | solution.py:413
  184.2 29.5 %all-to-all-start.4 = ((bf16[64,8,768]{2,1,0:T(8,128)(2,1)}), bf16[64,8,768]{2,1,0:T(8,128)(2,1)S(1)}, u32[]{:S(2)}, u32[]{:S(2)}) async-start(bf16[64,8,768]{2,1,0:T(8,128)(2,1)} %shard_map.102), calls=%async_computation.4 | async-start | bytes 1572864 | tf_op jit(solution)/shard_map/all_to_all | solution.py:398
  203.0 1.2 copy-start.6
  205.3 0.9 copy-start.1
  213.6 29.2 %all-to-all-start.5 = ((bf16[64,8,768]{2,1,0:T(8,128)(2,1)}), bf16[64,8,768]{2,1,0:T(8,128)(2,1)S(1)}, u32[]{:S(2)}, u32[]{:S(2)}) async-start(bf16[64,8,768]{2,1,0:T(8,128)(2,1)} %shard_map.103), calls=%async_computation.5 | async-start | bytes 1572864 | tf_op jit(solution)/shard_map/all_to_all | solution.py:398
  219.8 20.3 %collective-permute-start.4 = (bf16[256,1536]{1,0:T(8,128)(2,1)S(1)}, bf16[256,1536]{1,0:T(8,128)(2,1)}, u32[]{:S(2)}, u32[]{:S(2)}) collective-permute-start(bf16[256,1536]{1,0:T(8,128)(2,1)S(1)} %get-tuple-element.27), channel_id=1, source_target_pairs={{0,64},{64,128},{128,192},{192,0},{1,65},{65,129},{129,193},{193,1... | collective-permute-start | bytes 2359304 | tf_op jit(solution)/shard_map/ppermute | solution.py:413

commit v5 on v4

--- a/solution.py
+++ b/solution.py
@@ -175,11 +175,13 @@
 
 def cross_kernel(c, spread_ref, r_ref, out_ref, spread_buf, out_buf, sems):
     copies = Copies(sems)
-    copies.start(spread_ref if c is None else spread_ref.at[c], spread_buf)
-    copies.wait()
+    if c is not None:
+        copies.start(spread_ref.at[c], spread_buf)
+        copies.wait()
+        spread_ref = spread_buf
     for g in range(out_ref.shape[2] // WIDTH):
         part = columns_of(g)
-        total = dot(spread_buf[...], r_ref[:, :, part].reshape(2 * BLK, WIDTH))
+        total = dot(spread_ref[...], r_ref[:, :, part].reshape(2 * BLK, WIDTH))
         out_buf[:, :, part] = total.astype(BF).reshape(DEV, 8, WIDTH)
         copies.start(out_buf.at[:, :, part], out_ref.at[:, :, part])
     copies.wait()
@@ -201,15 +203,20 @@
 
 
 def weight_loads(copies, up_ref, down_ref, up_buf, down_buf):
-    loads = [
-        (
-            copies.start(up_ref.at[g], up_buf.at[g]),
-            copies.start(down_ref.at[g], down_buf.at[g]),
-        )
-        for g in range(GROUPS)
-    ]
+    loads = {}
+
+    def start(g):
+        if g < GROUPS and g not in loads:
+            loads[g] = (
+                copies.start(up_ref.at[g], up_buf.at[g]),
+                copies.start(down_ref.at[g], down_buf.at[g]),
+            )
+
+    start(0)
+    start(1)
 
     def up(g):
+        start(g + 2)
         copies.wait(loads[g][0])
         return up_buf[g]
 
@@ -217,7 +224,7 @@
         copies.wait(loads[g][1])
         return down_buf[g]
 
-    return up, down
+    return up, down, start
 
 
 def middle_kernel(
@@ -233,80 +240,16 @@
     first_ref,
     entering_ref,
     mixed_ref,
+    kept_ref,
     out_ref,
     x_buf,
     channel_buf,
     up_buf,
     down_buf,
+    queued_buf,
     gain_buf,
     factor_buf,
     first_buf,
-    entering_buf,
-    mixed_buf,
-    out_buf,
-    sems,
-    queued_sem,
-):
-    copies = Copies(sems)
-    channel_load = copies.start(channel_ref, channel_buf)
-    rows = [pl.ds(b * BLK, BLK) for b in range(2)]
-    x_loads = [copies.start(x_ref.at[rows[b]], x_buf.at[rows[b]]) for b in range(2)]
-    up, down = weight_loads(copies, up_ref, down_ref, up_buf, down_buf)
-    late = [copies.start(gain_ref, gain_buf), copies.start(factor_ref, factor_buf)]
-    queued = pltpu.make_async_copy(queued_ref, entering_buf, queued_sem.at[0])
-    last = flag_ref[0] == 1
-
-    @pl.when(last)
-    def _():
-        queued.start()
-
-    unpacks = [onehot(BLK, 2 * BLK, lambda j, r: whole_at(r, j, b)) for b in range(2)]
-    residuals = [[], []]
-    for g in range(GROUPS):
-        packed = across_ref[:, :, columns_of(g)].reshape(2 * BLK, WIDTH)
-        for b in range(2):
-            residuals[b].append(dot(unpacks[b], packed))
-    copies.wait(channel_load)
-    for b in range(2):
-
-        def store(g, part, value):
-            first_buf[rows[b], part] = value
-
-        copies.wait(x_loads[b])
-        residual = x_buf[rows[b], :].astype(F32) + jnp.concatenate(residuals[b], axis=1)
-        channel_rows(residual, channel_buf[...], up, down, store)
-        copies.start(first_buf.at[rows[b]], first_ref.at[rows[b]])
-
-    @pl.when(last)
-    def _():
-        queued.wait()
-
-    @pl.when(jnp.logical_not(last))
-    def _():
-        entering_buf[...] = first_buf[...]
-
-    copies.wait(*late)
-    mixed = []
-    for b in range(2):
-        copies.start(entering_buf.at[rows[b]], entering_ref.at[rows[b]])
-        normed = normalize(entering_buf[rows[b], :].astype(F32), gain_buf[...])
-        mixed.append(dot(factor_buf[b], normed).astype(BF))
-        mixed_buf[rows[b], :] = mixed[b]
-        copies.start(mixed_buf.at[rows[b]], mixed_ref.at[rows[b]])
-    for n in range(2):
-        part = slice(n * BLK, (n + 1) * BLK)
-        devices = pl.ds(n * (DEV // 2), DEV // 2)
-        out_buf[devices] = packed_part(lambda h, b: pack(0, h, b)[part], mixed)
-        copies.start(out_buf.at[devices], out_ref.at[devices])
-    copies.wait()
-
-
-def remainder_kernel(
-    entering_ref,
-    mixed_ref,
-    kept0_ref,
-    kept1_ref,
-    out_ref,
     entering_buf,
     mixed_buf,
     kept_buf,
@@ -314,19 +257,73 @@
     sems,
 ):
     copies = Copies(sems)
+    rows = [pl.ds(b * BLK, BLK) for b in range(2)]
+    x_loads = [copies.start(x_ref.at[rows[0]], x_buf.at[rows[0]])]
+    channel_load = copies.start(channel_ref, channel_buf)
+    up, down, start = weight_loads(copies, up_ref, down_ref, up_buf, down_buf)
+    x_loads.append(copies.start(x_ref.at[rows[1]], x_buf.at[rows[1]]))
+    for g in range(2, GROUPS):
+        start(g)
+    late = [
+        copies.start(gain_ref, gain_buf),
+        copies.start(factor_ref, factor_buf),
+        copies.start(queued_ref, queued_buf),
+    ]
+    unpacks = [onehot(BLK, 2 * BLK, lambda j, r: whole_at(r, j, b)) for b in range(2)]
+    packs = [[pack(0, h, b) for h in range(2)] for b in range(2)]
+    picked = pick(0)
+    last = flag_ref[0] == 1
+    residuals = [[], []]
+    for g in range(GROUPS):
+        packed = across_ref[:, :, columns_of(g)].reshape(2 * BLK, WIDTH)
+        for b in range(2):
+            residuals[b].append(dot(unpacks[b], packed))
+    copies.wait(channel_load)
+    mixed = []
+    for b in range(2):
+
+        def store(g, part, value):
+            first_buf[rows[b], part] = value
+
+        copies.wait(x_loads[b])
+        residual = x_buf[rows[b], :].astype(F32) + jnp.concatenate(residuals[b], axis=1)
+        channel_rows(residual, channel_buf[...], up, down, store)
+        if b == 0:
+            copies.wait(*late)
+        copies.start(first_buf.at[rows[b]], first_ref.at[rows[b]])
+        entering = jnp.where(last, queued_buf[rows[b], :], first_buf[rows[b], :])
+        entering_buf[rows[b], :] = entering
+        copies.start(entering_buf.at[rows[b]], entering_ref.at[rows[b]])
+        half = pl.ds(b * (BLK // 2), BLK // 2)
+        kept_buf[half, :] = dot(picked, entering).astype(BF)
+        mixed.append(dot(factor_buf[b], normalize(entering.astype(F32), gain_buf[...])).astype(BF))
+        mixed_buf[rows[b], :] = mixed[b]
+        copies.start(mixed_buf.at[rows[b]], mixed_ref.at[rows[b]])
+    copies.start(kept_buf, kept_ref)
+    for n in range(2):
+        part = slice(n * BLK, (n + 1) * BLK)
+        devices = pl.ds(n * (DEV // 2), DEV // 2)
+        out_buf[devices] = packed_part(lambda h, b: packs[b][h][part], mixed)
+        copies.start(out_buf.at[devices], out_ref.at[devices])
+    copies.wait()
+
+
+def remainder_kernel(
+    entering_ref, mixed_ref, kept_ref, out_ref, entering_buf, mixed_buf, kept_buf, out_buf, sems
+):
+    copies = Copies(sems)
+    copies.start(mixed_ref, mixed_buf)
     copies.start(entering_ref, entering_buf)
-    copies.start(mixed_ref, mixed_buf)
     copies.wait(0)
-    for c, kept_ref in enumerate((kept0_ref, kept1_ref)):
-        for b in range(2):
-            rows = pl.ds(b * (BLK // 2), BLK // 2)
-            kept = dot(pick(c), entering_buf[b * BLK : (b + 1) * BLK, :])
-            kept_buf[c, rows, :] = kept.astype(BF)
-        copies.start(kept_buf.at[c], kept_ref)
-    copies.wait(1)
     mixed = [mixed_buf[b * BLK : (b + 1) * BLK, :] for b in range(2)]
     out_buf[...] = packed_part(functools.partial(pack, 1), mixed)
     copies.start(out_buf, out_ref)
+    copies.wait(1)
+    for b in range(2):
+        rows = pl.ds(b * (BLK // 2), BLK // 2)
+        kept = dot(pick(1), entering_buf[b * BLK : (b + 1) * BLK, :])
+        kept_buf[rows, :] = kept.astype(BF)
+    copies.start(kept_buf, kept_ref)
     copies.wait()
 
 
@@ -348,7 +345,7 @@
         copies.start(x_ref, x_buf),
         copies.start(channel_ref, channel_buf),
     ]
-    up, down = weight_loads(copies, up_ref, down_ref, up_buf, down_buf)
+    up, down, start = weight_loads(copies, up_ref, down_ref, up_buf, down_buf)
     if whole:
         other = copies.start(other_ref, other_buf)
 
@@ -366,6 +363,8 @@
     places = [place(c) for c in range(2)] if whole else None
     compact = [unpack_compact(h) for h in range(2)]
     copies.wait(*loads)
+    start(2)
+    start(3)
     packed = across_ref[...].reshape(2 * BLK, HALF)
     across = jnp.concatenate([dot(compact[h], packed) for h in range(2)], axis=1)
     channel_rows(x_buf[...].astype(F32) + across, channel_buf[...], up, down, store)
@@ -449,42 +448,43 @@
         [whole, columns],
         [buf(square), buf(both), sems(5)],
         (800_000_000, 4_000_000, 0),
-        near=(1,),
+        near=(0, 1),
         mib=16,
     )
     across = exchange(out)
 
-    first, entering, mixed, sent0 = call(
+    first, entering, mixed, kept0, sent0 = call(
         middle_kernel,
-        (sequence, far, far, message),
+        (sequence, far, far, part_rows, message),
         [held_x, across, channel_gain, up, down, queued, next_gain, next_factor],
         [
             buf(x),
             buf(channel_gain),
             buf(up),
             buf(down),
+            buf(x),
             buf(norm_gain),
             buf(factor),
             buf(x),
             buf(x),
             buf(x),
+            buf(part_rows),
             buf(message),
-            sems(21),
-            sems(1),
+            sems(23),
         ],
         (7_000_000_000, 18_000_000, 2_000_000),
         flags,
         near=(1,),
     )
     columns0 = exchange(sent0)
-    kept0, kept1, sent1 = call(
+    x0 = ahead(kept0)
+    kept1, sent1 = call(
         remainder_kernel,
-        (part_rows, part_rows, message),
+        (part_rows, message),
         [entering, mixed],
-        [buf(x), buf(x), buf(shape(2, BLK, D)), buf(message), sems(5)],
+        [buf(x), buf(x), buf(part_rows), buf(message), sems(4)],
         (1_000_000_000, 5_000_000, 0),
     )
-    x0 = ahead(kept0)
     columns0, x0 = lax.optimization_barrier((columns0, x0))
     columns0, sent1 = lax.optimization_barrier((columns0, sent1))
     columns0 = ahead(columns0)

time: 252 us -> 247 us (0.980)
    all_to_all x6, starting transfers between devices: 50.1 us -> 46.3 us  [exchange(): lax.all_to_all(hbm(value), 'seq', split_axis=0, concat_axis=0, tiled=True)]
  transfers between devices with their start and end apart: 12 -> 12, of which waited for: 10 -> 11; matrix products, arithmetic and copies ran while one was open for 0% -> 0% of each run, Pallas kernels for 5% -> 5%
where the time goes in v5:
time: 247 us
  waiting for transfers between devices  145 us (59%)
  starting transfers between devices  55.1 us (22%)
  Pallas kernels  38.5 us (16%)
  local copies, waits for them, and re-layouts  6.67 us (3%)
    all_to_all x6, waiting for transfers between devices, exchange(): lax.all_to_all(hbm(value), 'seq', split_axis=0, concat_axis=0, tiled=True)  88.8 us
    ppermute x4, waiting for transfers between devices, ahead(): lax.ppermute(value, 'section', [(s, (s + 1) % count) for s in range(count)])  51.7 us
    all_to_all x6, starting transfers between devices, exchange(): lax.all_to_all(hbm(value), 'seq', split_axis=0, concat_axis=0, tiled=True)  46.3 us
    pallas_call x9, Pallas kernels, call(): pl.pallas_call(kernel, out_shape=outs, in_specs=scalars + [nearby if n in...  38.5 us
    unnamed x18, local copies, waits for them, and re-layouts  6.67 us
    ppermute x4, starting transfers between devices, ahead(): lax.ppermute(value, 'section', [(s, (s + 1) % count) for s in range(count)])  5.55 us
  transfers between devices with their start and end apart: 12, of which 11 were waited for; matrix products, arithmetic and copies ran while one was open for 0% of the time, Pallas kernels for 5%

profile of v5, /device:TPU:1, one launch (start us, length us, event | category | flops | bytes accessed | tf_op | source)
XLA Modules:
  0.0 246.7 jit_solution(6294520345510796938)
XLA Ops:
  0.6 4.3 %shard_map.96 = bf16[64,8,1536]{2,1,0:T(8,128)(2,1)} custom-call(bf16[512,1536]{1,0:T(8,128)(2,1)} %bitcast.14, f32[1,1536]{1,0:T(1,128)} %gain_ref.1, bf16[2,256,256]{2,1,0:T(8,128)(2,1)} %bitcast.16), custom_call_target="tpu_custom_call" | custom-call | flops 2000000000 | bytes 4000000 | tf_op jit(solution)/shard_map/pallas_call | solution.py:28
  5.0 13.0 %all-to-all-start = ((bf16[64,8,1536]{2,1,0:T(8,128)(2,1)}), bf16[64,8,1536]{2,1,0:T(8,128)(2,1)S(1)}, u32[]{:S(2)}, u32[]{:S(2)}) async-start(bf16[64,8,1536]{2,1,0:T(8,128)(2,1)} %shard_map.96), calls=%async_computation | async-start | bytes 3145728 | tf_op jit(solution)/shard_map/all_to_all | solution.py:397
  18.0 2.7 %shard_map.95 = (bf16[512,512]{1,0:T(8,128)(2,1)S(1)}, bf16[2,512,512]{2,1,0:T(8,128)(2,1)S(1)}) custom-call(bf16[4,128,128]{2,1,0:T(8,128)(2,1)} %bitcast.18), custom_call_target="tpu_custom_call" | custom-call | flops 600000000 | bytes 5000000 | tf_op jit(solution)/shard_map/pallas_call | solution.py:28
  21.6 36.1 %all-to-all-done.r_ref = bf16[64,8,1536]{2,1,0:T(8,128)(2,1)S(1)} async-done(((bf16[64,8,1536]{2,1,0:T(8,128)(2,1)}), bf16[64,8,1536]{2,1,0:T(8,128)(2,1)S(1)}, u32[]{:S(2)}, u32[]{:S(2)}) %all-to-all-start) | async-done | bytes 1572896 | tf_op jit(solution)/shard_map/all_to_all | solution.py:397
  57.7 2.0 shard_map.97
  59.8 6.3 %all-to-all-start.1 = ((bf16[64,8,1536]{2,1,0:T(8,128)(2,1)}), bf16[64,8,1536]{2,1,0:T(8,128)(2,1)S(1)}, u32[]{:S(2)}, u32[]{:S(2)}) async-start(bf16[64,8,1536]{2,1,0:T(8,128)(2,1)} %shard_map.97), calls=%async_computation.1 | async-start | bytes 3145728 | tf_op jit(solution)/shard_map/all_to_all | solution.py:397
  66.1 2.8 %collective-permute-start.1 = (bf16[2,256,256]{2,1,0:T(8,128)(2,1)S(1)}, bf16[2,256,256]{2,1,0:T(8,128)(2,1)S(1)}, u32[]{:S(2)}, u32[]{:S(2)}) collective-permute-start(bf16[2,256,256]{2,1,0:T(8,128)(2,1)S(1)} %bitcast.17), channel_id=1, source_target_pairs={{64,0},{128,64},{192,128},{0,192},{65,1},{129,65},{193,129},{1,193... | collective-permute-start | bytes 786440 | tf_op jit(solution)/shard_map/ppermute | solution.py:415
  69.4 4.9 %collective-permute-done.gain_ref = f32[1,1536]{1,0:T(1,128)S(1)} collective-permute-done((f32[1,1536]{1,0:T(1,128)S(1)}, f32[1,1536]{1,0:T(1,128)S(1)}, u32[]{:S(2)}, u32[]{:S(2)}) %collective-permute-start) | collective-permute-done | bytes 6176 | tf_op jit(solution)/shard_map/ppermute | solution.py:415
  74.3 31.6 %all-to-all-done.1.across_ref = bf16[64,8,1536]{2,1,0:T(8,128)(2,1)S(1)} async-done(((bf16[64,8,1536]{2,1,0:T(8,128)(2,1)}), bf16[64,8,1536]{2,1,0:T(8,128)(2,1)S(1)}, u32[]{:S(2)}, u32[]{:S(2)}) %all-to-all-start.1) | async-done | bytes 1572896 | tf_op jit(solution)/shard_map/all_to_all | solution.py:397
  105.9 11.4 %shard_map.98 = (bf16[512,1536]{1,0:T(8,128)(2,1)}, bf16[512,1536]{1,0:T(8,128)(2,1)}, bf16[512,1536]{1,0:T(8,128)(2,1)}, bf16[256,1536]{1,0:T(8,128)(2,1)}, bf16[64,8,768]{2,1,0:T(8,128)(2,1)}) custom-call(s32[1]{0:T(128)} %bitcast.flag_ref, bf16[512,1536]{1,0:T(8,128)(2,1)} %bitcast.15, bf16[64,8,1536]{2,1,0:T(8,128)(2,1)S(1)} %all-to-all-done.1.across_ref, ...), custom_call_target="tpu_custom_call" | custom-call | flops 7000000000 | bytes 18000000 | tf_op jit(solution)/shard_map/pallas_call | solution.py:28
  117.3 6.4 %all-to-all-start.2 = ((bf16[64,8,768]{2,1,0:T(8,128)(2,1)}), bf16[64,8,768]{2,1,0:T(8,128)(2,1)}, u32[]{:S(2)}, u32[]{:S(2)}) async-start(bf16[64,8,768]{2,1,0:T(8,128)(2,1)} %get-tuple-element.22), calls=%async_computation.2 | async-start | bytes 1572864 | tf_op jit(solution)/shard_map/all_to_all | solution.py:397
  123.8 1.6 collective-permute-start.2
  125.4 1.4 copy-done.3
  126.8 2.3 shard_map.99
  129.1 15.2 %collective-permute-done.2.x_ref = bf16[256,1536]{1,0:T(8,128)(2,1)S(1)} collective-permute-done((bf16[256,1536]{1,0:T(8,128)(2,1)}, bf16[256,1536]{1,0:T(8,128)(2,1)S(1)}, u32[]{:S(2)}, u32[]{:S(2)}) %collective-permute-start.2) | collective-permute-done | bytes 786464 | tf_op jit(solution)/shard_map/ppermute | solution.py:412
  144.3 2.4 all-to-all-done.2
  146.7 1.3 collective-permute-start.5
  148.0 8.0 %all-to-all-start.3 = ((bf16[64,8,768]{2,1,0:T(8,128)(2,1)}), bf16[64,8,768]{2,1,0:T(8,128)(2,1)}, u32[]{:S(2)}, u32[]{:S(2)}) async-start(bf16[64,8,768]{2,1,0:T(8,128)(2,1)} %get-tuple-element.26), calls=%async_computation.3 | async-start | bytes 1572864 | tf_op jit(solution)/shard_map/all_to_all | solution.py:397
  155.9 11.1 %collective-permute-done.5.r_ref = bf16[64,8,768]{2,1,0:T(8,128)(2,1)S(1)} collective-permute-done((bf16[64,8,768]{2,1,0:T(8,128)(2,1)}, bf16[64,8,768]{2,1,0:T(8,128)(2,1)S(1)}, u32[]{:S(2)}, u32[]{:S(2)}) %collective-permute-start.5) | collective-permute-done | bytes 786464 | tf_op jit(solution)/shard_map/ppermute | solution.py:412
  167.1 1.2 copy-done.5
  170.3 8.6 %all-to-all-done.3.other_ref = bf16[64,8,768]{2,1,0:T(8,128)(2,1)} async-done(((bf16[64,8,768]{2,1,0:T(8,128)(2,1)}), bf16[64,8,768]{2,1,0:T(8,128)(2,1)}, u32[]{:S(2)}, u32[]{:S(2)}) %all-to-all-start.3) | async-done | bytes 786464 | tf_op jit(solution)/shard_map/all_to_all | solution.py:397
  178.9 1.3 collective-permute-start.3
  180.2 6.5 %all-to-all-start.4 = ((bf16[64,8,768]{2,1,0:T(8,128)(2,1)}), bf16[64,8,768]{2,1,0:T(8,128)(2,1)S(1)}, u32[]{:S(2)}, u32[]{:S(2)}) async-start(bf16[64,8,768]{2,1,0:T(8,128)(2,1)} %shard_map.102), calls=%async_computation.4 | async-start | bytes 1572864 | tf_op jit(solution)/shard_map/all_to_all | solution.py:397
  186.6 12.4 %collective-permute-done.3.r_ref = bf16[64,8,768]{2,1,0:T(8,128)(2,1)S(1)} collective-permute-done((bf16[64,8,768]{2,1,0:T(8,128)(2,1)}, bf16[64,8,768]{2,1,0:T(8,128)(2,1)S(1)}, u32[]{:S(2)}, u32[]{:S(2)}) %collective-permute-start.3) | collective-permute-done | bytes 786464 | tf_op jit(solution)/shard_map/ppermute | solution.py:412
  199.0 1.2 copy-done.6
  202.2 7.5 %all-to-all-done.4.other_ref.across_ref = bf16[64,8,768]{2,1,0:T(8,128)(2,1)S(1)} async-done(((bf16[64,8,768]{2,1,0:T(8,128)(2,1)}), bf16[64,8,768]{2,1,0:T(8,128)(2,1)S(1)}, u32[]{:S(2)}, u32[]{:S(2)}) %all-to-all-start.4) | async-done | bytes 786464 | tf_op jit(solution)/shard_map/all_to_all | solution.py:397
  209.6 6.2 %all-to-all-start.5 = ((bf16[64,8,768]{2,1,0:T(8,128)(2,1)}), bf16[64,8,768]{2,1,0:T(8,128)(2,1)S(1)}, u32[]{:S(2)}, u32[]{:S(2)}) async-start(bf16[64,8,768]{2,1,0:T(8,128)(2,1)} %shard_map.103), calls=%async_computation.5 | async-start | bytes 1572864 | tf_op jit(solution)/shard_map/all_to_all | solution.py:397
  215.8 1.3 collective-permute-start.4
  217.2 6.0 %shard_map.104.rest_0_ = bf16[256,1536]{1,0:T(8,128)(2,1)} custom-call(bf16[256,1536]{1,0:T(8,128)(2,1)S(1)} %collective-permute-done.2.x_ref, bf16[64,8,768]{2,1,0:T(8,128)(2,1)S(1)} %all-to-all-done.4.other_ref.across_ref, f32[1,1536]{1,0:T(1,128)} %channel_ref.5, bf16[4,384,1024]{2,1,0:T(8,128)(2,1)} %bitcast.9, bf16[4,1024,384]{2,1,0:T(8,128)(2,1)} %bitcast.12), custom_call_target="tpu_custom_call" | custom-call | flops 2500000000 | bytes 10000000 | tf_op jit(solution)/shard_map/pallas_call | solution.py:28
  223.1 13.0 %collective-permute-done.4.x_ref = bf16[256,1536]{1,0:T(8,128)(2,1)} collective-permute-done((bf16[256,1536]{1,0:T(8,128)(2,1)S(1)}, bf16[256,1536]{1,0:T(8,128)(2,1)}, u32[]{:S(2)}, u32[]{:S(2)}) %collective-permute-start.4) | collective-permute-done | bytes 786464 | tf_op jit(solution)/shard_map/ppermute | solution.py:412
  236.1 2.7 %all-to-all-done.5.across_ref = bf16[64,8,768]{2,1,0:T(8,128)(2,1)S(1)} async-done(((bf16[64,8,768]{2,1,0:T(8,128)(2,1)}), bf16[64,8,768]{2,1,0:T(8,128)(2,1)S(1)}, u32[]{:S(2)}, u32[]{:S(2)}) %all-to-all-start.5) | async-done | bytes 786464 | tf_op jit(solution)/shard_map/all_to_all | solution.py:397
  238.8 7.7 %shard_map.105 = bf16[512,1536]{1,0:T(8,128)(2,1)} custom-call(bf16[256,1536]{1,0:T(8,128)(2,1)} %collective-permute-done.4.x_ref, bf16[64,8,768]{2,1,0:T(8,128)(2,1)S(1)} %all-to-all-done.5.across_ref, f32[1,1536]{1,0:T(1,128)} %channel_ref.5, bf16[4,384,1024]{2,1,0:T(8,128)(2,1)} %bitcast.10, bf16[4,1024,384]{2,1,0:T(8,128)(2,1)} %bitcast.13, ...), custom_call_target="tpu_custom_call" | custom-call | flops 3000000000 | bytes 11000000 | tf_op jit(solution)/shard_map/pallas_call | solution.py:28
  (21 shorter events, 5.3 us)
Async XLA Ops:
  5.0 52.8 %all-to-all-start = ((bf16[64,8,1536]{2,1,0:T(8,128)(2,1)}), bf16[64,8,1536]{2,1,0:T(8,128)(2,1)S(1)}, u32[]{:S(2)}, u32[]{:S(2)}) async-start(bf16[64,8,1536]{2,1,0:T(8,128)(2,1)} %shard_map.96), calls=%async_computation | async-start | bytes 3145728 | tf_op jit(solution)/shard_map/all_to_all | solution.py:397
  20.6 1.0 copy-start.4
  59.8 6.3 %copy-start.7 = (bf16[1,2,256,256]{3,2,1,0:T(8,128)(2,1)S(1)}, bf16[1,2,256,256]{3,2,1,0:T(8,128)(2,1)}, u32[]{:S(2)}) copy-start(bf16[1,2,256,256]{3,2,1,0:T(8,128)(2,1)} %param.11) | copy-start | bytes 786436
  59.8 9.1 %copy-start.8 = (f32[1,1536]{1,0:T(1,128)S(1)}, f32[1,1536]{1,0:T(1,128)}, u32[]{:S(2)}) copy-start(f32[1,1536]{1,0:T(1,128)} %gain_ref.1) | copy-start | bytes 18436
  59.8 46.1 %all-to-all-start.1 = ((bf16[64,8,1536]{2,1,0:T(8,128)(2,1)}), bf16[64,8,1536]{2,1,0:T(8,128)(2,1)S(1)}, u32[]{:S(2)}, u32[]{:S(2)}) async-start(bf16[64,8,1536]{2,1,0:T(8,128)(2,1)} %shard_map.97), calls=%async_computation.1 | async-start | bytes 3145728 | tf_op jit(solution)/shard_map/all_to_all | solution.py:397
  66.1 8.2 %collective-permute-start.1 = (bf16[2,256,256]{2,1,0:T(8,128)(2,1)S(1)}, bf16[2,256,256]{2,1,0:T(8,128)(2,1)S(1)}, u32[]{:S(2)}, u32[]{:S(2)}) collective-permute-start(bf16[2,256,256]{2,1,0:T(8,128)(2,1)S(1)} %bitcast.17), channel_id=1, source_target_pairs={{64,0},{128,64},{192,128},{0,192},{65,1},{129,65},{193,129},{1,193... | collective-permute-start | bytes 786440 | tf_op jit(solution)/shard_map/ppermute | solution.py:415
  68.9 5.4 %collective-permute-start = (f32[1,1536]{1,0:T(1,128)S(1)}, f32[1,1536]{1,0:T(1,128)S(1)}, u32[]{:S(2)}, u32[]{:S(2)}) collective-permute-start(f32[1,1536]{1,0:T(1,128)S(1)} %copy-done.8), channel_id=1, source_target_pairs={{64,0},{128,64},{192,128},{0,192},{65,1},{129,65},{193,129},{1,193... | collective-permute-start | bytes 18440 | tf_op jit(solution)/shard_map/ppermute | solution.py:415
  117.3 8.1 %copy-start.2 = (bf16[512,1536]{1,0:T(8,128)(2,1)S(1)}, bf16[512,1536]{1,0:T(8,128)(2,1)}, u32[]{:S(2)}) copy-start(bf16[512,1536]{1,0:T(8,128)(2,1)} %get-tuple-element.19.entering_ref) | copy-start | bytes 4718596
  117.3 29.3 %all-to-all-start.2 = ((bf16[64,8,768]{2,1,0:T(8,128)(2,1)}), bf16[64,8,768]{2,1,0:T(8,128)(2,1)}, u32[]{:S(2)}, u32[]{:S(2)}) async-start(bf16[64,8,768]{2,1,0:T(8,128)(2,1)} %get-tuple-element.22), calls=%async_computation.2 | async-start | bytes 1572864 | tf_op jit(solution)/shard_map/all_to_all | solution.py:397
  123.8 20.6 %collective-permute-start.2 = (bf16[256,1536]{1,0:T(8,128)(2,1)}, bf16[256,1536]{1,0:T(8,128)(2,1)S(1)}, u32[]{:S(2)}, u32[]{:S(2)}) collective-permute-start(bf16[256,1536]{1,0:T(8,128)(2,1)} %get-tuple-element.23), channel_id=1, source_target_pairs={{0,64},{64,128},{128,192},{192,0},{1,65},{65,129},{129,193},{193,1... | collective-permute-start | bytes 2359304 | tf_op jit(solution)/shard_map/ppermute | solution.py:412
  125.4 1.4 copy-start.3
  146.7 20.4 %collective-permute-start.5 = (bf16[64,8,768]{2,1,0:T(8,128)(2,1)}, bf16[64,8,768]{2,1,0:T(8,128)(2,1)S(1)}, u32[]{:S(2)}, u32[]{:S(2)}) collective-permute-start(bf16[64,8,768]{2,1,0:T(8,128)(2,1)} %all-to-all-done.2), channel_id=1, source_target_pairs={{0,64},{64,128},{128,192},{192,0},{1,65},{65,129},{129,193},{193,1... | collective-permute-start | bytes 2359304 | tf_op jit(solution)/shard_map/ppermute | solution.py:412
  148.0 30.9 %all-to-all-start.3 = ((bf16[64,8,768]{2,1,0:T(8,128)(2,1)}), bf16[64,8,768]{2,1,0:T(8,128)(2,1)}, u32[]{:S(2)}, u32[]{:S(2)}) async-start(bf16[64,8,768]{2,1,0:T(8,128)(2,1)} %get-tuple-element.26), calls=%async_computation.3 | async-start | bytes 1572864 | tf_op jit(solution)/shard_map/all_to_all | solution.py:397
  167.1 1.2 copy-start.5
  169.3 0.9 copy-start
  178.9 20.1 %collective-permute-start.3 = (bf16[64,8,768]{2,1,0:T(8,128)(2,1)}, bf16[64,8,768]{2,1,0:T(8,128)(2,1)S(1)}, u32[]{:S(2)}, u32[]{:S(2)}) collective-permute-start(bf16[64,8,768]{2,1,0:T(8,128)(2,1)} %all-to-all-done.3.other_ref), channel_id=1, source_target_pairs={{0,64},{64,128},{128,192},{192,0},{1,65},{65,129},{129,193},{193,1... | collective-permute-start | bytes 2359304 | tf_op jit(solution)/shard_map/ppermute | solution.py:412
  180.2 29.5 %all-to-all-start.4 = ((bf16[64,8,768]{2,1,0:T(8,128)(2,1)}), bf16[64,8,768]{2,1,0:T(8,128)(2,1)S(1)}, u32[]{:S(2)}, u32[]{:S(2)}) async-start(bf16[64,8,768]{2,1,0:T(8,128)(2,1)} %shard_map.102), calls=%async_computation.4 | async-start | bytes 1572864 | tf_op jit(solution)/shard_map/all_to_all | solution.py:397
  199.0 1.2 copy-start.6
  201.3 0.9 copy-start.1
  209.6 29.2 %all-to-all-start.5 = ((bf16[64,8,768]{2,1,0:T(8,128)(2,1)}), bf16[64,8,768]{2,1,0:T(8,128)(2,1)S(1)}, u32[]{:S(2)}, u32[]{:S(2)}) async-start(bf16[64,8,768]{2,1,0:T(8,128)(2,1)} %shard_map.103), calls=%async_computation.5 | async-start | bytes 1572864 | tf_op jit(solution)/shard_map/all_to_all | solution.py:397
  215.8 20.3 %collective-permute-start.4 = (bf16[256,1536]{1,0:T(8,128)(2,1)S(1)}, bf16[256,1536]{1,0:T(8,128)(2,1)}, u32[]{:S(2)}, u32[]{:S(2)}) collective-permute-start(bf16[256,1536]{1,0:T(8,128)(2,1)S(1)} %get-tuple-element.27), channel_id=1, source_target_pairs={{0,64},{64,128},{128,192},{192,0},{1,65},{65,129},{129,193},{193,1... | collective-permute-start | bytes 2359304 | tf_op jit(solution)/shard_map/ppermute | solution.py:412

commit v6 on v5

--- a/solution.py
+++ b/solution.py
@@ -144,46 +144,77 @@
     copies.wait()
 
 
-def spread_kernel(cross_ref, whole_ref, out_ref, cross_buf, whole_buf, out_buf, sems):
-    copies = Copies(sems)
-    copies.start(cross_ref, cross_buf)
-    copies.wait()
+def spread(cross, rows, columns, mask):
     n = 2 * BLK
     row = lax.broadcasted_iota(jnp.int32, (n, n), 0)
     col = lax.broadcasted_iota(jnp.int32, (n, n), 1)
-    cross = cross_buf[...].reshape(n, 128)
-
-    def spread(rows, columns, mask):
-        full = dot(dot(onehot(n, n, rows), cross).astype(BF), onehot(128, n, columns))
-        return jnp.where(((row ^ col) & mask) == 0, full, 0.0).astype(BF)
-
+    full = dot(dot(onehot(n, n, rows), cross).astype(BF), onehot(128, n, columns))
+    return jnp.where(((row ^ col) & mask) == 0, full, 0.0).astype(BF)
+
+
+def spread_part(cross, c):
+    return spread(
+        cross,
+        lambda r, k: k == (2 * c + (r & 1)) * 128 + (r >> 3) * 2 + ((r >> 1) & 1),
+        lambda m, k: m == (k >> 3) * 2 + ((k >> 1) & 1),
+        5,
+    )
+
+
+def spread_own_kernel(cross_ref, whole_ref, part_ref, cross_buf, whole_buf, part_buf, sems):
+    copies = Copies(sems)
+    copies.start(cross_ref, cross_buf)
+    copies.wait()
+    cross = cross_buf[...].reshape(2 * BLK, 128)
     whole_buf[...] = spread(
+        cross,
         lambda r, k: k == (r & 3) * 128 + (r >> 3) * 2 + ((r >> 2) & 1),
         lambda m, k: m == (k >> 3) * 2 + ((k >> 2) & 1),
         3,
     )
     copies.start(whole_buf, whole_ref)
-    for c in range(2):
-        out_buf[c] = spread(
-            lambda r, k: k == (2 * c + (r & 1)) * 128 + (r >> 3) * 2 + ((r >> 1) & 1),
-            lambda m, k: m == (k >> 3) * 2 + ((k >> 1) & 1),
-            5,
-        )
-    copies.start(out_buf, out_ref)
-    copies.wait()
-
-
-def cross_kernel(c, spread_ref, r_ref, out_ref, spread_buf, out_buf, sems):
-    copies = Copies(sems)
-    if c is not None:
-        copies.start(spread_ref.at[c], spread_buf)
-        copies.wait()
-        spread_ref = spread_buf
+    part_buf[...] = spread_part(cross, 1)
+    copies.start(part_buf, part_ref)
+    copies.wait()
+
+
+def spread_next_kernel(cross_ref, part_ref, cross_buf, part_buf, sems):
+    copies = Copies(sems)
+    copies.start(cross_ref, cross_buf)
+    copies.wait()
+    part_buf[...] = spread_part(cross_buf[...].reshape(2 * BLK, 128), 0)
+    copies.start(part_buf, part_ref)
+    copies.wait()
+
+
+def cross_groups(copies, spread_ref, columns, out_ref, out_buf):
     for g in range(out_ref.shape[2] // WIDTH):
         part = columns_of(g)
-        total = dot(spread_ref[...], r_ref[:, :, part].reshape(2 * BLK, WIDTH))
+        total = dot(spread_ref[...], columns(part).reshape(2 * BLK, WIDTH))
         out_buf[:, :, part] = total.astype(BF).reshape(DEV, 8, WIDTH)
         copies.start(out_buf.at[:, :, part], out_ref.at[:, :, part])
+
+
+def cross_whole_kernel(spread_ref, r_ref, out_ref, out_buf, sems):
+    copies = Copies(sems)
+    cross_groups(copies, spread_ref, lambda part: r_ref[:, :, part], out_ref, out_buf)
+    copies.wait()
+
+
+def cross_first_kernel(spread_ref, r_ref, out_ref, other_ref, spread_buf, out_buf, sems):
+    copies = Copies(sems)
+    copies.start(spread_ref, spread_buf)
+    copies.start(r_ref.at[:, 1], other_ref)
+    copies.wait(0)
+    cross_groups(copies, spread_buf, lambda part: r_ref[:, 0, :, part], out_ref, out_buf)
+    copies.wait()
+
+
+def cross_second_kernel(spread_ref, r_ref, out_ref, spread_buf, out_buf, sems):
+    copies = Copies(sems)
+    copies.start(spread_ref, spread_buf)
+    copies.wait()
+    cross_groups(copies, spread_buf, lambda part: r_ref[:, :, part], out_ref, out_buf)
     copies.wait()
 
 
@@ -239,8 +270,6 @@
     factor_ref,
     first_ref,
     entering_ref,
-    mixed_ref,
-    kept_ref,
     out_ref,
     x_buf,
     channel_buf,
@@ -251,8 +280,6 @@
     factor_buf,
     first_buf,
     entering_buf,
-    mixed_buf,
-    kept_buf,
     out_buf,
     sems,
 ):
@@ -270,8 +297,6 @@
         copies.start(queued_ref, queued_buf),
     ]
     unpacks = [onehot(BLK, 2 * BLK, lambda j, r: whole_at(r, j, b)) for b in range(2)]
-    packs = [[pack(0, h, b) for h in range(2)] for b in range(2)]
-    picked = pick(0)
     last = flag_ref[0] == 1
     residuals = [[], []]
     for g in range(GROUPS):
@@ -294,37 +319,22 @@
         entering = jnp.where(last, queued_buf[rows[b], :], first_buf[rows[b], :])
         entering_buf[rows[b], :] = entering
         copies.start(entering_buf.at[rows[b]], entering_ref.at[rows[b]])
-        half = pl.ds(b * (BLK // 2), BLK // 2)
-        kept_buf[half, :] = dot(picked, entering).astype(BF)
         mixed.append(dot(factor_buf[b], normalize(entering.astype(F32), gain_buf[...])).astype(BF))
-        mixed_buf[rows[b], :] = mixed[b]
-        copies.start(mixed_buf.at[rows[b]], mixed_ref.at[rows[b]])
-    copies.start(kept_buf, kept_ref)
-    for n in range(2):
-        part = slice(n * BLK, (n + 1) * BLK)
-        devices = pl.ds(n * (DEV // 2), DEV // 2)
-        out_buf[devices] = packed_part(lambda h, b: packs[b][h][part], mixed)
-        copies.start(out_buf.at[devices], out_ref.at[devices])
-    copies.wait()
-
-
-def remainder_kernel(
-    entering_ref, mixed_ref, kept_ref, out_ref, entering_buf, mixed_buf, kept_buf, out_buf, sems
-):
-    copies = Copies(sems)
-    copies.start(mixed_ref, mixed_buf)
-    copies.start(entering_ref, entering_buf)
-    copies.wait(0)
-    mixed = [mixed_buf[b * BLK : (b + 1) * BLK, :] for b in range(2)]
-    out_buf[...] = packed_part(functools.partial(pack, 1), mixed)
-    copies.start(out_buf, out_ref)
-    copies.wait(1)
-    for b in range(2):
-        rows = pl.ds(b * (BLK // 2), BLK // 2)
-        kept = dot(pick(1), entering_buf[b * BLK : (b + 1) * BLK, :])
-        kept_buf[rows, :] = kept.astype(BF)
-    copies.start(kept_buf, kept_ref)
-    copies.wait()
+    for c in range(2):
+        out_buf[c] = packed_part(functools.partial(pack, c), mixed)
+        copies.start(out_buf.at[c], out_ref.at[:, c])
+    copies.wait()
+
+
+def last_rows(copies, loads, residual_of, across_ref, channel_buf, weights, store):
+    up, down, start = weights
+    compact = [unpack_compact(h) for h in range(2)]
+    copies.wait(*loads)
+    start(2)
+    start(3)
+    packed = across_ref[...].reshape(2 * BLK, HALF)
+    across = jnp.concatenate([dot(compact[h], packed) for h in range(2)], axis=1)
+    channel_rows(residual_of() + across, channel_buf[...], up, down, store)
 
 
 def last_kernel(
@@ -333,41 +343,67 @@
     channel_ref,
     up_ref,
     down_ref,
-    *rest,
+    out_ref,
+    kept_ref,
+    x_buf,
+    channel_buf,
+    up_buf,
+    down_buf,
+    out_buf,
+    kept_buf,
+    sems,
 ):
-    whole = len(rest) > 7
-    if whole:
-        other_ref, out_ref, x_buf, channel_buf, up_buf, down_buf, other_buf, out_buf, sems = rest
-    else:
-        out_ref, x_buf, channel_buf, up_buf, down_buf, out_buf, sems = rest
-    copies = Copies(sems)
-    loads = [
-        copies.start(x_ref, x_buf),
-        copies.start(channel_ref, channel_buf),
-    ]
-    up, down, start = weight_loads(copies, up_ref, down_ref, up_buf, down_buf)
-    if whole:
-        other = copies.start(other_ref, other_buf)
+    copies = Copies(sems)
+    loads = [copies.start(x_ref, x_buf), copies.start(channel_ref, channel_buf)]
+    weights = weight_loads(copies, up_ref, down_ref, up_buf, down_buf)
+
+    def rows_of(c):
+        picked = [dot(pick(c), x_buf[b * BLK : (b + 1) * BLK, :]) for b in range(2)]
+        return jnp.concatenate(picked, axis=0)
 
     def store(g, part, value):
-        if whole:
-            copies.wait(other)
-            for b in range(2):
-                rows = slice(b * (BLK // 2), (b + 1) * (BLK // 2))
-                joined = dot(places[0], other_buf[rows, part]) + dot(places[1], value[rows])
-                out_buf[b * BLK : (b + 1) * BLK, part] = joined.astype(BF)
-        else:
-            out_buf[:, part] = value
+        out_buf[:, part] = value
         copies.start(out_buf.at[:, columns_of(g)], out_ref.at[:, columns_of(g)])
 
-    places = [place(c) for c in range(2)] if whole else None
-    compact = [unpack_compact(h) for h in range(2)]
-    copies.wait(*loads)
-    start(2)
-    start(3)
-    packed = across_ref[...].reshape(2 * BLK, HALF)
-    across = jnp.concatenate([dot(compact[h], packed) for h in range(2)], axis=1)
-    channel_rows(x_buf[...].astype(F32) + across, channel_buf[...], up, down, store)
+    last_rows(copies, loads, lambda: rows_of(0), across_ref, channel_buf, weights, store)
+    kept_buf[...] = rows_of(1).astype(BF)
+    copies.start(kept_buf, kept_ref)
+    copies.wait()
+
+
+def final_kernel(
+    x_ref,
+    across_ref,
+    channel_ref,
+    up_ref,
+    down_ref,
+    other_ref,
+    out_ref,
+    x_buf,
+    channel_buf,
+    up_buf,
+    down_buf,
+    other_buf,
+    out_buf,
+    sems,
+):
+    copies = Copies(sems)
+    loads = [copies.start(x_ref, x_buf), copies.start(channel_ref, channel_buf)]
+    weights = weight_loads(copies, up_ref, down_ref, up_buf, down_buf)
+    other = copies.start(other_ref, other_buf)
+    places = [place(c) for c in range(2)]
+
+    def store(g, part, value):
+        copies.wait(other)
+        for b in range(2):
+            rows = slice(b * (BLK // 2), (b + 1) * (BLK // 2))
+            joined = dot(places[0], other_buf[rows, part]) + dot(places[1], value[rows])
+            out_buf[b * BLK : (b + 1) * BLK, part] = joined.astype(BF)
+        copies.start(out_buf.at[:, columns_of(g)], out_ref.at[:, columns_of(g)])
+
+    last_rows(
+        copies, loads, lambda: x_buf[...].astype(F32), across_ref, channel_buf, weights, store
+    )
     copies.wait()
 
 
@@ -414,12 +450,15 @@
     def behind(value):
         return lax.ppermute(value, "section", [((s + 1) % count, s) for s in range(count)])
 
-    message, both = shape(DEV, 8, HALF), shape(DEV, 8, D)
+    message, both, pair = shape(DEV, 8, HALF), shape(DEV, 8, D), shape(DEV, 2, 8, HALF)
+    square = shape(2 * BLK, 2 * BLK)
     sequence, part_rows = shape(2 * BLK, D), shape(BLK, D)
-    far = pltpu.HBM(sequence.shape, BF)
 
     def buf(value):
         return pltpu.VMEM(value.shape, value.dtype)
+
+    def far(value):
+        return pltpu.HBM(value.shape, value.dtype)
 
     def sems(n):
         return pltpu.SemaphoreType.DMA((n,))
@@ -432,30 +471,35 @@
         (2_000_000_000, 4_000_000, 0),
     )
     columns = exchange(sent)
-    square = shape(2 * BLK, 2 * BLK)
-    whole, spread = call(
-        spread_kernel,
-        (square, shape(2, 2 * BLK, 2 * BLK)),
+    whole, own_part = call(
+        spread_own_kernel,
+        (square, square),
         [cross],
-        [buf(cross), buf(square), buf(shape(2, 2 * BLK, 2 * BLK)), sems(3)],
-        (600_000_000, 5_000_000, 0),
-    )
-    next_gain, next_factor = behind(norm_gain), behind(factor)
-
+        [buf(cross), buf(square), buf(square), sems(3)],
+        (400_000_000, 3_000_000, 0),
+    )
+    next_gain, next_factor, next_cross = behind(norm_gain), behind(factor), behind(cross)
     out = call(
-        functools.partial(cross_kernel, None),
+        cross_whole_kernel,
         both,
         [whole, columns],
-        [buf(square), buf(both), sems(5)],
+        [buf(both), sems(4)],
         (800_000_000, 4_000_000, 0),
         near=(0, 1),
         mib=16,
     )
     across = exchange(out)
-
-    first, entering, mixed, kept0, sent0 = call(
+    next_part = call(
+        spread_next_kernel,
+        square,
+        [next_cross],
+        [buf(cross), buf(square), sems(2)],
+        (200_000_000, 2_000_000, 0),
+    )
+
+    first, entering, sent = call(
         middle_kernel,
-        (sequence, far, far, part_rows, message),
+        (sequence, far(sequence), pair),
         [held_x, across, channel_gain, up, down, queued, next_gain, next_factor],
         [
             buf(x),
@@ -467,59 +511,53 @@
             buf(factor),
             buf(x),
             buf(x),
-            buf(x),
-            buf(part_rows),
-            buf(message),
-            sems(23),
+            buf(shape(2, DEV, 8, HALF)),
+            sems(20),
         ],
         (7_000_000_000, 18_000_000, 2_000_000),
         flags,
         near=(1,),
     )
-    columns0 = exchange(sent0)
-    x0 = ahead(kept0)
-    kept1, sent1 = call(
-        remainder_kernel,
-        (part_rows, message),
-        [entering, mixed],
-        [buf(x), buf(x), buf(part_rows), buf(message), sems(4)],
-        (1_000_000_000, 5_000_000, 0),
-    )
-    columns0, x0 = lax.optimization_barrier((columns0, x0))
-    columns0, sent1 = lax.optimization_barrier((columns0, sent1))
-    columns0 = ahead(columns0)
-    columns1 = exchange(sent1)
-
-    def crossed(c, value):
-        return call(
-            functools.partial(cross_kernel, c),
-            message,
-            [spread, value],
-            [buf(square), buf(message), sems(3)],
-            (LONG, 2_000_000, 0),
-            near=(1,),
-            mib=12,
-        )
-
-    across0 = exchange(after(crossed(0, columns0), columns1))
+    columns = exchange(sent)
+    entered = ahead(entering)
+    entered = after(entered, flags)
+    columns, entered = lax.optimization_barrier((columns, entered))
+    out0, columns1 = call(
+        cross_first_kernel,
+        (message, far(message)),
+        [next_part, columns],
+        [buf(square), buf(message), sems(4)],
+        (400_000_000, 2_000_000, 0),
+        near=(1,),
+        mib=12,
+    )
+    across0 = exchange(out0)
     columns1 = ahead(columns1)
-    kept1, columns1 = lax.optimization_barrier((kept1, columns1))
-    x1 = ahead(kept1)
-    across1 = exchange(after(crossed(1, columns1), across0, True))
-    bufs = [buf(part_rows), buf(channel_gain), buf(up), buf(down)]
-    other = call(
+    out1 = call(
+        cross_second_kernel,
+        message,
+        [own_part, columns1],
+        [buf(square), buf(message), sems(3)],
+        (LONG, 2_000_000, 0),
+        near=(1,),
+        mib=12,
+    )
+    across1 = exchange(after(out1, across0, True))
+    across0 = ahead(across0)
+    bufs = [buf(channel_gain), buf(up), buf(down)]
+    other, kept = call(
         last_kernel,
-        pltpu.HBM(part_rows.shape, BF),
-        [x0, across0, channel_gain, up, down],
-        [*bufs, buf(part_rows), sems(14)],
-        (2_500_000_000, 10_000_000, 1_000_000),
+        (far(part_rows), far(part_rows)),
+        [entered, across0, channel_gain, up, down],
+        [buf(sequence), *bufs, buf(part_rows), buf(part_rows), sems(15)],
+        (LONG, 10_000_000, 1_000_000),
         near=(1,),
     )
     second = call(
-        last_kernel,
+        final_kernel,
         sequence,
-        [hbm(x1), across1, channel_gain, up, down, hbm(other)],
-        [*bufs, buf(part_rows), buf(sequence), sems(15)],
+        [hbm(kept), across1, channel_gain, up, down, hbm(other)],
+        [buf(part_rows), *bufs, buf(part_rows), buf(sequence), sems(15)],
         (3_000_000_000, 11_000_000, 1_000_000),
         near=(1,),
     )

time: 247 us -> 237 us (0.960)
  starting transfers between devices: 55.1 us -> 47.4 us
  local copies, waits for them, and re-layouts: 6.67 us -> 1.54 us
    all_to_all x6 -> x5, starting transfers between devices: 46.3 us -> 38.7 us  [exchange(): lax.all_to_all(hbm(value), 'seq', split_axis=0, concat_axis=0, tiled=True)]
    unnamed x18 -> x10, local copies, waits for them, and re-layouts: 6.67 us -> 1.54 us
    ppermute x4 -> x3, waiting for transfers between devices: 51.7 us -> 47.5 us  [ahead(): lax.ppermute(value, 'section', [(s, (s + 1) % count) for s in range(count)])]
    ppermute x2 -> x3, waiting for transfers between devices: 4.89 us -> 8.25 us  [behind(): lax.ppermute(value, 'section', [((s + 1) % count, s) for s in range(count)])]
    all_to_all x6 -> x5, waiting for transfers between devices: 88.8 us -> 90.8 us  [exchange(): lax.all_to_all(hbm(value), 'seq', split_axis=0, concat_axis=0, tiled=True)]
    ppermute x4 -> x3, starting transfers between devices: 5.55 us -> 3.74 us  [ahead(): lax.ppermute(value, 'section', [(s, (s + 1) % count) for s in range(count)])]
    ppermute x2 -> x3, starting transfers between devices: 3.28 us -> 4.94 us  [behind(): lax.ppermute(value, 'section', [((s + 1) % count, s) for s in range(count)])]
  transfers between devices with their start and end apart: 12 -> 11, of which waited for: 11 -> 10; matrix products, arithmetic and copies ran while one was open for 0% -> 0% of each run, Pallas kernels for 5% -> 5%
where the time goes in v6:
time: 237 us; the launch traced here: 236 us
  waiting for transfers between devices  147 us (62%)
  starting transfers between devices  47.4 us (20%)
  Pallas kernels  39.9 us (17%)
    all_to_all x5, waiting for transfers between devices, exchange(): lax.all_to_all(hbm(value), 'seq', split_axis=0, concat_axis=0, tiled=True)  90.8 us
    ppermute x3, waiting for transfers between devices, ahead(): lax.ppermute(value, 'section', [(s, (s + 1) % count) for s in range(count)])  47.5 us
    pallas_call x9, Pallas kernels, call(): pl.pallas_call(kernel, out_shape=outs, in_specs=scalars + [nearby if n in...  39.9 us
    all_to_all x5, starting transfers between devices, exchange(): lax.all_to_all(hbm(value), 'seq', split_axis=0, concat_axis=0, tiled=True)  38.7 us
    ppermute x3, waiting for transfers between devices, behind(): lax.ppermute(value, 'section', [((s + 1) % count, s) for s in range(count)])  8.25 us
    ppermute x3, starting transfers between devices, behind(): lax.ppermute(value, 'section', [((s + 1) % count, s) for s in range(count)])  4.94 us
  transfers between devices with their start and end apart: 11, of which 10 were waited for; matrix products, arithmetic and copies ran while one was open for 0% of the time, Pallas kernels for 5%

profile of v6, /device:TPU:1, one launch (start us, length us, event | category | flops | bytes accessed | tf_op | source)
XLA Modules:
  0.0 236.3 jit_solution(1183023446166874367)
XLA Ops:
  0.6 4.3 %shard_map.96 = bf16[64,8,1536]{2,1,0:T(8,128)(2,1)} custom-call(bf16[512,1536]{1,0:T(8,128)(2,1)} %bitcast.14, f32[1,1536]{1,0:T(1,128)} %gain_ref.1, bf16[2,256,256]{2,1,0:T(8,128)(2,1)} %bitcast.16), custom_call_target="tpu_custom_call" | custom-call | flops 2000000000 | bytes 4000000 | tf_op jit(solution)/shard_map/pallas_call | solution.py:28
  5.0 13.0 %all-to-all-start = ((bf16[64,8,1536]{2,1,0:T(8,128)(2,1)}), bf16[64,8,1536]{2,1,0:T(8,128)(2,1)S(1)}, u32[]{:S(2)}, u32[]{:S(2)}) async-start(bf16[64,8,1536]{2,1,0:T(8,128)(2,1)} %shard_map.96), calls=%async_computation | async-start | bytes 3145728 | tf_op jit(solution)/shard_map/all_to_all | solution.py:433
  18.0 2.4 shard_map.95
  20.3 37.4 %all-to-all-done.r_ref = bf16[64,8,1536]{2,1,0:T(8,128)(2,1)S(1)} async-done(((bf16[64,8,1536]{2,1,0:T(8,128)(2,1)}), bf16[64,8,1536]{2,1,0:T(8,128)(2,1)S(1)}, u32[]{:S(2)}, u32[]{:S(2)}) %all-to-all-start) | async-done | bytes 1572896 | tf_op jit(solution)/shard_map/all_to_all | solution.py:433
  57.7 2.0 shard_map.97
  59.8 6.3 %all-to-all-start.1 = ((bf16[64,8,1536]{2,1,0:T(8,128)(2,1)}), bf16[64,8,1536]{2,1,0:T(8,128)(2,1)S(1)}, u32[]{:S(2)}, u32[]{:S(2)}) async-start(bf16[64,8,1536]{2,1,0:T(8,128)(2,1)} %shard_map.97), calls=%async_computation.1 | async-start | bytes 3145728 | tf_op jit(solution)/shard_map/all_to_all | solution.py:433
  66.1 2.8 %collective-permute-start.1 = (bf16[2,256,256]{2,1,0:T(8,128)(2,1)S(1)}, bf16[2,256,256]{2,1,0:T(8,128)(2,1)S(1)}, u32[]{:S(2)}, u32[]{:S(2)}) collective-permute-start(bf16[2,256,256]{2,1,0:T(8,128)(2,1)S(1)} %bitcast.17), channel_id=1, source_target_pairs={{64,0},{128,64},{192,128},{0,192},{65,1},{129,65},{193,129},{1,193... | collective-permute-start | bytes 786440 | tf_op jit(solution)/shard_map/ppermute | solution.py:451
  68.9 0.5 collective-permute-start
  69.4 4.9 %collective-permute-done.gain_ref = f32[1,1536]{1,0:T(1,128)S(1)} collective-permute-done((f32[1,1536]{1,0:T(1,128)S(1)}, f32[1,1536]{1,0:T(1,128)S(1)}, u32[]{:S(2)}, u32[]{:S(2)}) %collective-permute-start) | collective-permute-done | bytes 6176 | tf_op jit(solution)/shard_map/ppermute | solution.py:451
  74.3 31.6 %all-to-all-done.1.across_ref = bf16[64,8,1536]{2,1,0:T(8,128)(2,1)S(1)} async-done(((bf16[64,8,1536]{2,1,0:T(8,128)(2,1)}), bf16[64,8,1536]{2,1,0:T(8,128)(2,1)S(1)}, u32[]{:S(2)}, u32[]{:S(2)}) %all-to-all-start.1) | async-done | bytes 1572896 | tf_op jit(solution)/shard_map/all_to_all | solution.py:433
  105.9 12.1 %shard_map.98 = (bf16[512,1536]{1,0:T(8,128)(2,1)}, bf16[512,1536]{1,0:T(8,128)(2,1)}, bf16[64,2,8,768]{3,2,1,0:T(8,128)(2,1)}) custom-call(s32[1]{0:T(128)} %bitcast.flag_ref.other_ref, bf16[512,1536]{1,0:T(8,128)(2,1)} %bitcast.15, bf16[64,8,1536]{2,1,0:T(8,128)(2,1)S(1)} %all-to-all-done.1.across_ref, f32[1,1536]{1,0:T(1,128)} %channel_ref.5, ...), custom_call_target="tpu_custom_call" | custom-call | flops 7000000000 | bytes 18000000 | tf_op jit(solution)/shard_map/pallas_call | solution.py:28
  118.0 1.4 collective-permute-start.2
  119.3 6.5 %all-to-all-start.2 = ((bf16[64,2,8,768]{3,2,1,0:T(8,128)(2,1)}), bf16[64,2,8,768]{3,2,1,0:T(8,128)(2,1)S(1)}, u32[]{:S(2)}, u32[]{:S(2)}) async-start(bf16[64,2,8,768]{3,2,1,0:T(8,128)(2,1)} %get-tuple-element.15), calls=%async_computation.2 | async-start | bytes 3145728 | tf_op jit(solution)/shard_map/all_to_all | solution.py:433
  125.9 1.7 collective-permute-start.3
  127.6 3.4 %collective-permute-done.3.cross_ref = bf16[4,128,128]{2,1,0:T(8,128)(2,1)S(1)} collective-permute-done((bf16[4,128,128]{2,1,0:T(8,128)(2,1)S(1)}, bf16[4,128,128]{2,1,0:T(8,128)(2,1)S(1)}, u32[]{:S(2)}, u32[]{:S(2)}) %collective-permute-start.3) | collective-permute-done | bytes 131104 | tf_op jit(solution)/shard_map/ppermute | solution.py:451
  130.9 0.7 copy-done.3
  131.6 1.6 shard_map.100.spread_ref
  133.2 22.3 %collective-permute-done.2.value_ref = bf16[512,1536]{1,0:T(8,128)(2,1)} collective-permute-done((bf16[512,1536]{1,0:T(8,128)(2,1)}, bf16[512,1536]{1,0:T(8,128)(2,1)}, u32[]{:S(2)}, u32[]{:S(2)}) %collective-permute-start.2) | collective-permute-done | bytes 1572896 | tf_op jit(solution)/shard_map/ppermute | solution.py:448
  155.6 10.1 %all-to-all-done.2.r_ref = bf16[64,2,8,768]{3,2,1,0:T(8,128)(2,1)S(1)} async-done(((bf16[64,2,8,768]{3,2,1,0:T(8,128)(2,1)}), bf16[64,2,8,768]{3,2,1,0:T(8,128)(2,1)S(1)}, u32[]{:S(2)}, u32[]{:S(2)}) %all-to-all-start.2) | async-done | bytes 1572896 | tf_op jit(solution)/shard_map/all_to_all | solution.py:433
  165.7 1.5 shard_map.101
  167.2 1.4 collective-permute-start.5
  168.6 6.4 %all-to-all-start.3 = ((bf16[64,8,768]{2,1,0:T(8,128)(2,1)}), bf16[64,8,768]{2,1,0:T(8,128)(2,1)S(1)}, u32[]{:S(2)}, u32[]{:S(2)}) async-start(bf16[64,8,768]{2,1,0:T(8,128)(2,1)} %get-tuple-element.19), calls=%async_computation.3 | async-start | bytes 1572864 | tf_op jit(solution)/shard_map/all_to_all | solution.py:433
  175.0 12.7 %collective-permute-done.5.r_ref = bf16[64,8,768]{2,1,0:T(8,128)(2,1)S(1)} collective-permute-done((bf16[64,8,768]{2,1,0:T(8,128)(2,1)}, bf16[64,8,768]{2,1,0:T(8,128)(2,1)S(1)}, u32[]{:S(2)}, u32[]{:S(2)}) %collective-permute-start.5) | collective-permute-done | bytes 786464 | tf_op jit(solution)/shard_map/ppermute | solution.py:448
  187.7 1.0 shard_map.103.value_ref
  188.8 0.9 copy-done
  189.6 8.3 %all-to-all-done.3.other_ref = bf16[64,8,768]{2,1,0:T(8,128)(2,1)S(1)} async-done(((bf16[64,8,768]{2,1,0:T(8,128)(2,1)}), bf16[64,8,768]{2,1,0:T(8,128)(2,1)S(1)}, u32[]{:S(2)}, u32[]{:S(2)}) %all-to-all-start.3) | async-done | bytes 786464 | tf_op jit(solution)/shard_map/all_to_all | solution.py:433
  198.0 1.0 collective-permute-start.4
  199.0 6.5 %all-to-all-start.4 = ((bf16[64,8,768]{2,1,0:T(8,128)(2,1)}), bf16[64,8,768]{2,1,0:T(8,128)(2,1)S(1)}, u32[]{:S(2)}, u32[]{:S(2)}) async-start(bf16[64,8,768]{2,1,0:T(8,128)(2,1)} %shard_map.104), calls=%async_computation.4 | async-start | bytes 1572864 | tf_op jit(solution)/shard_map/all_to_all | solution.py:433
  205.5 12.4 %collective-permute-done.4.across_ref = bf16[64,8,768]{2,1,0:T(8,128)(2,1)S(1)} collective-permute-done((bf16[64,8,768]{2,1,0:T(8,128)(2,1)S(1)}, bf16[64,8,768]{2,1,0:T(8,128)(2,1)S(1)}, u32[]{:S(2)}, u32[]{:S(2)}) %collective-permute-start.4) | collective-permute-done | bytes 786464 | tf_op jit(solution)/shard_map/ppermute | solution.py:448
  217.9 7.2 %shard_map.102 = (bf16[256,1536]{1,0:T(8,128)(2,1)}, bf16[256,1536]{1,0:T(8,128)(2,1)}) custom-call(bf16[512,1536]{1,0:T(8,128)(2,1)} %shard_map.99.x_ref, bf16[64,8,768]{2,1,0:T(8,128)(2,1)S(1)} %collective-permute-done.4.across_ref, f32[1,1536]{1,0:T(1,128)} %channel_ref.5, bf16[4,384,1024]{2,1,0:T(8,128)(2,1)} %bitcast.9, bf16[4,1024,384]{2,1,0:T(8,128)(2,1)} %bitcast.12), custom_call_target="tpu_custom_call" | custom-call | flops 20000000000 | bytes 10000000 | tf_op jit(solution)/shard_map/pallas_call | solution.py:28
  225.1 3.3 %all-to-all-done.4.across_ref = bf16[64,8,768]{2,1,0:T(8,128)(2,1)S(1)} async-done(((bf16[64,8,768]{2,1,0:T(8,128)(2,1)}), bf16[64,8,768]{2,1,0:T(8,128)(2,1)S(1)}, u32[]{:S(2)}, u32[]{:S(2)}) %all-to-all-start.4) | async-done | bytes 786464 | tf_op jit(solution)/shard_map/all_to_all | solution.py:433
  228.4 7.7 %shard_map.105 = bf16[512,1536]{1,0:T(8,128)(2,1)} custom-call(bf16[256,1536]{1,0:T(8,128)(2,1)} %get-tuple-element.20.x_ref, bf16[64,8,768]{2,1,0:T(8,128)(2,1)S(1)} %all-to-all-done.4.across_ref, f32[1,1536]{1,0:T(1,128)} %channel_ref.5, bf16[4,384,1024]{2,1,0:T(8,128)(2,1)} %bitcast.10, bf16[4,1024,384]{2,1,0:T(8,128)(2,1)} %bitcast.13, ...), custom_call_target="tpu_custom_call" | custom-call | flops 3000000000 | bytes 11000000 | tf_op jit(solution)/shard_map/pallas_call | solution.py:28
  (11 shorter events, 0.0 us)
Async XLA Ops:
  5.0 52.8 %all-to-all-start = ((bf16[64,8,1536]{2,1,0:T(8,128)(2,1)}), bf16[64,8,1536]{2,1,0:T(8,128)(2,1)S(1)}, u32[]{:S(2)}, u32[]{:S(2)}) async-start(bf16[64,8,1536]{2,1,0:T(8,128)(2,1)} %shard_map.96), calls=%async_computation | async-start | bytes 3145728 | tf_op jit(solution)/shard_map/all_to_all | solution.py:433
  59.8 6.3 %copy-start.1 = (bf16[1,2,256,256]{3,2,1,0:T(8,128)(2,1)S(1)}, bf16[1,2,256,256]{3,2,1,0:T(8,128)(2,1)}, u32[]{:S(2)}) copy-start(bf16[1,2,256,256]{3,2,1,0:T(8,128)(2,1)} %param.11) | copy-start | bytes 786436
  59.8 9.1 %copy-start.4 = (f32[1,1536]{1,0:T(1,128)S(1)}, f32[1,1536]{1,0:T(1,128)}, u32[]{:S(2)}) copy-start(f32[1,1536]{1,0:T(1,128)} %gain_ref.1) | copy-start | bytes 18436
  59.8 46.1 %all-to-all-start.1 = ((bf16[64,8,1536]{2,1,0:T(8,128)(2,1)}), bf16[64,8,1536]{2,1,0:T(8,128)(2,1)S(1)}, u32[]{:S(2)}, u32[]{:S(2)}) async-start(bf16[64,8,1536]{2,1,0:T(8,128)(2,1)} %shard_map.97), calls=%async_computation.1 | async-start | bytes 3145728 | tf_op jit(solution)/shard_map/all_to_all | solution.py:433
  66.1 8.2 %collective-permute-start.1 = (bf16[2,256,256]{2,1,0:T(8,128)(2,1)S(1)}, bf16[2,256,256]{2,1,0:T(8,128)(2,1)S(1)}, u32[]{:S(2)}, u32[]{:S(2)}) collective-permute-start(bf16[2,256,256]{2,1,0:T(8,128)(2,1)S(1)} %bitcast.17), channel_id=1, source_target_pairs={{64,0},{128,64},{192,128},{0,192},{65,1},{129,65},{193,129},{1,193... | collective-permute-start | bytes 786440 | tf_op jit(solution)/shard_map/ppermute | solution.py:451
  68.9 5.4 %collective-permute-start = (f32[1,1536]{1,0:T(1,128)S(1)}, f32[1,1536]{1,0:T(1,128)S(1)}, u32[]{:S(2)}, u32[]{:S(2)}) collective-permute-start(f32[1,1536]{1,0:T(1,128)S(1)} %copy-done.4), channel_id=1, source_target_pairs={{64,0},{128,64},{192,128},{0,192},{65,1},{129,65},{193,129},{1,193... | collective-permute-start | bytes 18440 | tf_op jit(solution)/shard_map/ppermute | solution.py:451
  118.0 37.6 %collective-permute-start.2 = (bf16[512,1536]{1,0:T(8,128)(2,1)}, bf16[512,1536]{1,0:T(8,128)(2,1)}, u32[]{:S(2)}, u32[]{:S(2)}) collective-permute-start(bf16[512,1536]{1,0:T(8,128)(2,1)} %get-tuple-element.16), channel_id=1, source_target_pairs={{0,64},{64,128},{128,192},{192,0},{1,65},{65,129},{129,193},{193,1... | collective-permute-start | bytes 4718600 | tf_op jit(solution)/shard_map/ppermute | solution.py:448
  119.3 6.5 %copy-start.2 = (bf16[1,4,128,128]{3,2,1,0:T(8,128)(2,1)S(1)}, bf16[1,4,128,128]{3,2,1,0:T(8,128)(2,1)}, u32[]{:S(2)}) copy-start(bf16[1,4,128,128]{3,2,1,0:T(8,128)(2,1)} %param.12) | copy-start | bytes 393220
  119.3 46.3 %all-to-all-start.2 = ((bf16[64,2,8,768]{3,2,1,0:T(8,128)(2,1)}), bf16[64,2,8,768]{3,2,1,0:T(8,128)(2,1)S(1)}, u32[]{:S(2)}, u32[]{:S(2)}) async-start(bf16[64,2,8,768]{3,2,1,0:T(8,128)(2,1)} %get-tuple-element.15), calls=%async_computation.2 | async-start | bytes 3145728 | tf_op jit(solution)/shard_map/all_to_all | solution.py:433
  125.9 5.0 %collective-permute-start.3 = (bf16[4,128,128]{2,1,0:T(8,128)(2,1)S(1)}, bf16[4,128,128]{2,1,0:T(8,128)(2,1)S(1)}, u32[]{:S(2)}, u32[]{:S(2)}) collective-permute-start(bf16[4,128,128]{2,1,0:T(8,128)(2,1)S(1)} %bitcast.19), channel_id=1, source_target_pairs={{64,0},{128,64},{192,128},{0,192},{65,1},{129,65},{193,129},{1,193... | collective-permute-start | bytes 393224 | tf_op jit(solution)/shard_map/ppermute | solution.py:451
  130.9 0.7 copy-start.3
  167.2 20.5 %collective-permute-start.5 = (bf16[64,8,768]{2,1,0:T(8,128)(2,1)}, bf16[64,8,768]{2,1,0:T(8,128)(2,1)S(1)}, u32[]{:S(2)}, u32[]{:S(2)}) collective-permute-start(bf16[64,8,768]{2,1,0:T(8,128)(2,1)} %get-tuple-element.22), channel_id=1, source_target_pairs={{0,64},{64,128},{128,192},{192,0},{1,65},{65,129},{129,193},{193,1... | collective-permute-start | bytes 2359304 | tf_op jit(solution)/shard_map/ppermute | solution.py:448
  168.6 29.4 %all-to-all-start.3 = ((bf16[64,8,768]{2,1,0:T(8,128)(2,1)}), bf16[64,8,768]{2,1,0:T(8,128)(2,1)S(1)}, u32[]{:S(2)}, u32[]{:S(2)}) async-start(bf16[64,8,768]{2,1,0:T(8,128)(2,1)} %get-tuple-element.19), calls=%async_computation.3 | async-start | bytes 1572864 | tf_op jit(solution)/shard_map/all_to_all | solution.py:433
  188.7 0.9 copy-start
  198.0 19.9 %collective-permute-start.4 = (bf16[64,8,768]{2,1,0:T(8,128)(2,1)S(1)}, bf16[64,8,768]{2,1,0:T(8,128)(2,1)S(1)}, u32[]{:S(2)}, u32[]{:S(2)}) collective-permute-start(bf16[64,8,768]{2,1,0:T(8,128)(2,1)S(1)} %all-to-all-done.3.other_ref), channel_id=1, source_target_pairs={{0,64},{64,128},{128,192},{192,0},{1,65},{65,129},{129,193},{193,1... | collective-permute-start | bytes 2359304 | tf_op jit(solution)/shard_map/ppermute | solution.py:448
  199.0 29.5 %all-to-all-start.4 = ((bf16[64,8,768]{2,1,0:T(8,128)(2,1)}), bf16[64,8,768]{2,1,0:T(8,128)(2,1)S(1)}, u32[]{:S(2)}, u32[]{:S(2)}) async-start(bf16[64,8,768]{2,1,0:T(8,128)(2,1)} %shard_map.104), calls=%async_computation.4 | async-start | bytes 1572864 | tf_op jit(solution)/shard_map/all_to_all | solution.py:433

commit v7 on v6

--- a/solution.py
+++ b/solution.py
@@ -80,44 +80,13 @@
     return jnp.where(hit(r, c), 1.0, 0.0).astype(BF)
 
 
-def packed_at(r, j, c, h, b):
-    return (((r >> 3) * 4 + 2 * c + (r & 1)) == j) & (((r >> 1) & 3) == 2 * h + b)
-
-
-def pack(c, h, b):
-    return onehot(2 * BLK, BLK, lambda r, j: packed_at(r, j, c, h, b))
-
-
-def whole_at(r, j, b):
-    return (((r >> 3) * 4 + (r & 3)) == j) & (((r >> 2) & 1) == b)
-
-
-def unpack_compact(h):
-    return onehot(
-        BLK, 2 * BLK, lambda q, r: r == ((q & 127) >> 1) * 8 + 4 * h + 2 * (q >> 7) + (q & 1)
-    )
-
-
-def pick(c):
-    return onehot(BLK // 2, BLK, lambda q, j: j == (q >> 1) * 4 + 2 * c + (q & 1))
-
-
-def place(c):
-    return onehot(BLK, BLK // 2, lambda j, q: j == (q >> 1) * 4 + 2 * c + (q & 1))
+def offsets_of(rows, c):
+    return rows.reshape(DEV, 4, -1)[:, 2 * c : 2 * c + 2].reshape(BLK // 2, -1)
 
 
 def normalize(values, gain):
     scale = lax.rsqrt(jnp.mean(values * values, axis=-1, keepdims=True) + EPS)
     return (values * scale * gain).astype(BF)
-
-
-def packed_part(packs, mixed):
-    total = None
-    for b in range(2):
-        for h in range(2):
-            term = dot(packs(h, b), mixed[b][:, h * HALF : (h + 1) * HALF])
-            total = term if total is None else total + term
-    return total.astype(BF).reshape(-1, 8, HALF)
 
 
 def first_kernel(x_ref, gain_ref, factor_ref, out_ref, x_buf, gain_buf, factor_buf, out_buf, sems):
@@ -129,18 +98,12 @@
         copies.start(factor_ref, factor_buf),
         copies.start(x_ref.at[rows[1]], x_buf.at[rows[1]]),
     ]
-    packs = [onehot(2 * BLK, BLK, lambda r, j: whole_at(r, j, b)) for b in range(2)]
-    mixed = []
     for b in range(2):
         copies.wait(loads[3 * b], loads[1], loads[2])
         normed = normalize(x_buf[rows[b], :].astype(F32), gain_buf[...])
-        mixed.append(dot(factor_buf[b], normed).astype(BF))
-    for g in range(GROUPS):
-        part = columns_of(g)
-        at = slice(g * WIDTH, (g + 1) * WIDTH)
-        total = dot(packs[0], mixed[0][:, at]) + dot(packs[1], mixed[1][:, at])
-        out_buf[:, :, part] = total.astype(BF).reshape(DEV, 8, WIDTH)
-        copies.start(out_buf.at[:, :, part], out_ref.at[:, :, part])
+        mixed = dot(factor_buf[b], normed).astype(BF)
+        out_buf[:, b] = mixed.reshape(DEV, 4, D)
+        copies.start(out_buf.at[:, b], out_ref.at[:, b])
     copies.wait()
 
 
@@ -188,16 +151,16 @@
 
 
 def cross_groups(copies, spread_ref, columns, out_ref, out_buf):
-    for g in range(out_ref.shape[2] // WIDTH):
-        part = columns_of(g)
+    for g in range(out_ref.shape[-1] // WIDTH):
+        part = (slice(None),) * (len(out_ref.shape) - 1) + (columns_of(g),)
         total = dot(spread_ref[...], columns(part).reshape(2 * BLK, WIDTH))
-        out_buf[:, :, part] = total.astype(BF).reshape(DEV, 8, WIDTH)
-        copies.start(out_buf.at[:, :, part], out_ref.at[:, :, part])
+        out_buf[part] = total.astype(BF).reshape(out_ref.shape[:-1] + (WIDTH,))
+        copies.start(out_buf.at[part], out_ref.at[part])
 
 
 def cross_whole_kernel(spread_ref, r_ref, out_ref, out_buf, sems):
     copies = Copies(sems)
-    cross_groups(copies, spread_ref, lambda part: r_ref[:, :, part], out_ref, out_buf)
+    cross_groups(copies, spread_ref, lambda part: r_ref[part], out_ref, out_buf)
     copies.wait()
 
 
@@ -206,7 +169,7 @@
     copies.start(spread_ref, spread_buf)
     copies.start(r_ref.at[:, 1], other_ref)
     copies.wait(0)
-    cross_groups(copies, spread_buf, lambda part: r_ref[:, 0, :, part], out_ref, out_buf)
+    cross_groups(copies, spread_buf, lambda part: r_ref[:, 0, :, part[-1]], out_ref, out_buf)
     copies.wait()
 
 
@@ -214,7 +177,7 @@
     copies = Copies(sems)
     copies.start(spread_ref, spread_buf)
     copies.wait()
-    cross_groups(copies, spread_buf, lambda part: r_ref[:, :, part], out_ref, out_buf)
+    cross_groups(copies, spread_buf, lambda part: r_ref[part], out_ref, out_buf)
     copies.wait()
 
 
@@ -296,13 +259,7 @@
         copies.start(factor_ref, factor_buf),
         copies.start(queued_ref, queued_buf),
     ]
-    unpacks = [onehot(BLK, 2 * BLK, lambda j, r: whole_at(r, j, b)) for b in range(2)]
     last = flag_ref[0] == 1
-    residuals = [[], []]
-    for g in range(GROUPS):
-        packed = across_ref[:, :, columns_of(g)].reshape(2 * BLK, WIDTH)
-        for b in range(2):
-            residuals[b].append(dot(unpacks[b], packed))
     copies.wait(channel_load)
     mixed = []
     for b in range(2):
@@ -311,7 +268,7 @@
             first_buf[rows[b], part] = value
 
         copies.wait(x_loads[b])
-        residual = x_buf[rows[b], :].astype(F32) + jnp.concatenate(residuals[b], axis=1)
+        residual = x_buf[rows[b], :].astype(F32) + across_ref[:, b].reshape(BLK, D).astype(F32)
         channel_rows(residual, channel_buf[...], up, down, store)
         if b == 0:
             copies.wait(*late)
@@ -321,20 +278,30 @@
         copies.start(entering_buf.at[rows[b]], entering_ref.at[rows[b]])
         mixed.append(dot(factor_buf[b], normalize(entering.astype(F32), gain_buf[...])).astype(BF))
     for c in range(2):
-        out_buf[c] = packed_part(functools.partial(pack, c), mixed)
+        for b in range(2):
+            rows_c = mixed[b].reshape(DEV, 4, D)[:, 2 * c : 2 * c + 2]
+            for h in range(2):
+                first_row = 4 * h + 2 * b
+                half = slice(h * HALF, (h + 1) * HALF)
+                out_buf[c, :, first_row : first_row + 2, :] = rows_c[:, :, half]
         copies.start(out_buf.at[c], out_ref.at[:, c])
     copies.wait()
 
 
 def last_rows(copies, loads, residual_of, across_ref, channel_buf, weights, store):
     up, down, start = weights
-    compact = [unpack_compact(h) for h in range(2)]
     copies.wait(*loads)
     start(2)
     start(3)
-    packed = across_ref[...].reshape(2 * BLK, HALF)
-    across = jnp.concatenate([dot(compact[h], packed) for h in range(2)], axis=1)
-    channel_rows(residual_of() + across, channel_buf[...], up, down, store)
+    halves = [
+        [
+            across_ref[:, 4 * h + 2 * b : 4 * h + 2 * b + 2, :].reshape(BLK // 2, HALF)
+            for h in range(2)
+        ]
+        for b in range(2)
+    ]
+    across = jnp.concatenate([jnp.concatenate(halves[b], axis=1) for b in range(2)], axis=0)
+    channel_rows(residual_of() + across.astype(F32), channel_buf[...], up, down, store)
 
 
 def last_kernel(
@@ -358,15 +325,15 @@
     weights = weight_loads(copies, up_ref, down_ref, up_buf, down_buf)
 
     def rows_of(c):
-        picked = [dot(pick(c), x_buf[b * BLK : (b + 1) * BLK, :]) for b in range(2)]
+        picked = [offsets_of(x_buf[b * BLK : (b + 1) * BLK, :], c) for b in range(2)]
         return jnp.concatenate(picked, axis=0)
 
     def store(g, part, value):
         out_buf[:, part] = value
         copies.start(out_buf.at[:, columns_of(g)], out_ref.at[:, columns_of(g)])
 
-    last_rows(copies, loads, lambda: rows_of(0), across_ref, channel_buf, weights, store)
-    kept_buf[...] = rows_of(1).astype(BF)
+    last_rows(copies, loads, lambda: rows_of(0).astype(F32), across_ref, channel_buf, weights, store)
+    kept_buf[...] = rows_of(1)
     copies.start(kept_buf, kept_ref)
     copies.wait()
 
@@ -391,14 +358,14 @@
     loads = [copies.start(x_ref, x_buf), copies.start(channel_ref, channel_buf)]
     weights = weight_loads(copies, up_ref, down_ref, up_buf, down_buf)
     other = copies.start(other_ref, other_buf)
-    places = [place(c) for c in range(2)]
 
     def store(g, part, value):
         copies.wait(other)
         for b in range(2):
             rows = slice(b * (BLK // 2), (b + 1) * (BLK // 2))
-            joined = dot(places[0], other_buf[rows, part]) + dot(places[1], value[rows])
-            out_buf[b * BLK : (b + 1) * BLK, part] = joined.astype(BF)
+            both = [v.reshape(DEV, 2, WIDTH) for v in (other_buf[rows, part], value[rows])]
+            joined = jnp.concatenate(both, axis=1).reshape(BLK, WIDTH)
+            out_buf[b * BLK : (b + 1) * BLK, part] = joined
         copies.start(out_buf.at[:, columns_of(g)], out_ref.at[:, columns_of(g)])
 
     last_rows(
@@ -450,7 +417,7 @@
     def behind(value):
         return lax.ppermute(value, "section", [((s + 1) % count, s) for s in range(count)])
 
-    message, both, pair = shape(DEV, 8, HALF), shape(DEV, 8, D), shape(DEV, 2, 8, HALF)
+    message, both, pair = shape(DEV, 8, HALF), shape(DEV, 2, 4, D), shape(DEV, 2, 8, HALF)
     square = shape(2 * BLK, 2 * BLK)
     sequence, part_rows = shape(2 * BLK, D), shape(BLK, D)
 
@@ -467,7 +434,7 @@
         first_kernel,
         both,
         [held_x, held_gain, held_factor],
-        [buf(x), buf(norm_gain), buf(factor), buf(both), sems(8)],
+        [buf(x), buf(norm_gain), buf(factor), buf(both), sems(6)],
         (2_000_000_000, 4_000_000, 0),
     )
     columns = exchange(sent)

time: 237 us -> 235 us (level)
  no operation moved by 1% of the time
where the time goes in v7:
time: 235 us; the launch traced here: 234 us
  waiting for transfers between devices  146 us (62%)
  starting transfers between devices  47.2 us (20%)
  Pallas kernels  38.2 us (16%)
    all_to_all x5, waiting for transfers between devices, exchange(): lax.all_to_all(hbm(value), 'seq', split_axis=0, concat_axis=0, tiled=True)  90.5 us
    ppermute x3, waiting for transfers between devices, ahead(): lax.ppermute(value, 'section', [(s, (s + 1) % count) for s in range(count)])  47.7 us
    all_to_all x5, starting transfers between devices, exchange(): lax.all_to_all(hbm(value), 'seq', split_axis=0, concat_axis=0, tiled=True)  38.7 us
    pallas_call x9, Pallas kernels, call(): pl.pallas_call(kernel, out_shape=outs, in_specs=scalars + [nearby if n in...  38.2 us
    ppermute x3, waiting for transfers between devices, behind(): lax.ppermute(value, 'section', [((s + 1) % count, s) for s in range(count)])  8.21 us
    ppermute x3, starting transfers between devices, behind(): lax.ppermute(value, 'section', [((s + 1) % count, s) for s in range(count)])  4.75 us
  transfers between devices with their start and end apart: 11, of which 10 were waited for; matrix products, arithmetic and copies ran while one was open for 0% of the time, Pallas kernels for 5%

profile of v7, /device:TPU:1, one launch (start us, length us, event | category | flops | bytes accessed | tf_op | source)
XLA Modules:
  0.0 234.3 jit_solution(6597379462536174521)
XLA Ops:
  0.6 3.4 %shard_map.96 = bf16[64,2,4,1536]{3,2,1,0:T(4,128)(2,1)} custom-call(bf16[512,1536]{1,0:T(8,128)(2,1)} %bitcast.14, f32[1,1536]{1,0:T(1,128)} %gain_ref.1, bf16[2,256,256]{2,1,0:T(8,128)(2,1)} %bitcast.16), custom_call_target="tpu_custom_call" | custom-call | flops 2000000000 | bytes 4000000 | tf_op jit(solution)/shard_map/pallas_call | solution.py:28
  4.0 13.0 %all-to-all-start = ((bf16[64,2,4,1536]{3,2,1,0:T(4,128)(2,1)}), bf16[64,2,4,1536]{3,2,1,0:T(4,128)(2,1)S(1)}, u32[]{:S(2)}, u32[]{:S(2)}) async-start(bf16[64,2,4,1536]{3,2,1,0:T(4,128)(2,1)} %shard_map.96), calls=%async_computation | async-start | bytes 3145728 | tf_op jit(solution)/shard_map/all_to_all | solution.py:400
  17.0 2.4 %shard_map.95 = (bf16[512,512]{1,0:T(8,128)(2,1)S(1)}, bf16[512,512]{1,0:T(8,128)(2,1)S(1)}) custom-call(bf16[4,128,128]{2,1,0:T(8,128)(2,1)} %bitcast.18), custom_call_target="tpu_custom_call" | custom-call | flops 400000000 | bytes 3000000 | tf_op jit(solution)/shard_map/pallas_call | solution.py:28
  19.4 37.4 %all-to-all-done.r_ref = bf16[64,2,4,1536]{3,2,1,0:T(4,128)(2,1)S(1)} async-done(((bf16[64,2,4,1536]{3,2,1,0:T(4,128)(2,1)}), bf16[64,2,4,1536]{3,2,1,0:T(4,128)(2,1)S(1)}, u32[]{:S(2)}, u32[]{:S(2)}) %all-to-all-start) | async-done | bytes 1572896 | tf_op jit(solution)/shard_map/all_to_all | solution.py:400
  56.8 2.0 shard_map.97
  58.9 6.3 %all-to-all-start.1 = ((bf16[64,2,4,1536]{3,2,1,0:T(4,128)(2,1)}), bf16[64,2,4,1536]{3,2,1,0:T(4,128)(2,1)S(1)}, u32[]{:S(2)}, u32[]{:S(2)}) async-start(bf16[64,2,4,1536]{3,2,1,0:T(4,128)(2,1)} %shard_map.97), calls=%async_computation.1 | async-start | bytes 3145728 | tf_op jit(solution)/shard_map/all_to_all | solution.py:400
  65.2 2.8 %collective-permute-start.1 = (bf16[2,256,256]{2,1,0:T(8,128)(2,1)S(1)}, bf16[2,256,256]{2,1,0:T(8,128)(2,1)S(1)}, u32[]{:S(2)}, u32[]{:S(2)}) collective-permute-start(bf16[2,256,256]{2,1,0:T(8,128)(2,1)S(1)} %bitcast.17), channel_id=1, source_target_pairs={{64,0},{128,64},{192,128},{0,192},{65,1},{129,65},{193,129},{1,193... | collective-permute-start | bytes 786440 | tf_op jit(solution)/shard_map/ppermute | solution.py:418
  68.0 0.5 collective-permute-start
  68.4 4.9 %collective-permute-done.gain_ref = f32[1,1536]{1,0:T(1,128)S(1)} collective-permute-done((f32[1,1536]{1,0:T(1,128)S(1)}, f32[1,1536]{1,0:T(1,128)S(1)}, u32[]{:S(2)}, u32[]{:S(2)}) %collective-permute-start) | collective-permute-done | bytes 6176 | tf_op jit(solution)/shard_map/ppermute | solution.py:418
  73.3 31.6 %all-to-all-done.1.across_ref = bf16[64,2,4,1536]{3,2,1,0:T(4,128)(2,1)S(1)} async-done(((bf16[64,2,4,1536]{3,2,1,0:T(4,128)(2,1)}), bf16[64,2,4,1536]{3,2,1,0:T(4,128)(2,1)S(1)}, u32[]{:S(2)}, u32[]{:S(2)}) %all-to-all-start.1) | async-done | bytes 1572896 | tf_op jit(solution)/shard_map/all_to_all | solution.py:400
  104.9 10.8 %shard_map.98 = (bf16[512,1536]{1,0:T(8,128)(2,1)}, bf16[512,1536]{1,0:T(8,128)(2,1)}, bf16[64,2,8,768]{3,2,1,0:T(8,128)(2,1)}) custom-call(s32[1]{0:T(128)} %bitcast.flag_ref.other_ref, bf16[512,1536]{1,0:T(8,128)(2,1)} %bitcast.15, bf16[64,2,4,1536]{3,2,1,0:T(4,128)(2,1)S(1)} %all-to-all-done.1.across_ref, f32[1,1536]{1,0:T(1,128)} %channel_ref.5, ...), custom_call_target="tpu_custom_call" | custom-call | flops 7000000000 | bytes 18000000 | tf_op jit(solution)/shard_map/pallas_call | solution.py:28
  115.8 1.4 collective-permute-start.2
  117.2 6.5 %all-to-all-start.2 = ((bf16[64,2,8,768]{3,2,1,0:T(8,128)(2,1)}), bf16[64,2,8,768]{3,2,1,0:T(8,128)(2,1)S(1)}, u32[]{:S(2)}, u32[]{:S(2)}) async-start(bf16[64,2,8,768]{3,2,1,0:T(8,128)(2,1)} %get-tuple-element.15), calls=%async_computation.2 | async-start | bytes 3145728 | tf_op jit(solution)/shard_map/all_to_all | solution.py:400
  123.7 1.5 collective-permute-start.3
  125.2 3.3 %collective-permute-done.3.cross_ref = bf16[4,128,128]{2,1,0:T(8,128)(2,1)S(1)} collective-permute-done((bf16[4,128,128]{2,1,0:T(8,128)(2,1)S(1)}, bf16[4,128,128]{2,1,0:T(8,128)(2,1)S(1)}, u32[]{:S(2)}, u32[]{:S(2)}) %collective-permute-start.3) | collective-permute-done | bytes 131104 | tf_op jit(solution)/shard_map/ppermute | solution.py:418
  128.5 0.7 copy-done.3
  129.1 1.6 shard_map.100.spread_ref
  130.8 22.6 %collective-permute-done.2.value_ref = bf16[512,1536]{1,0:T(8,128)(2,1)} collective-permute-done((bf16[512,1536]{1,0:T(8,128)(2,1)}, bf16[512,1536]{1,0:T(8,128)(2,1)}, u32[]{:S(2)}, u32[]{:S(2)}) %collective-permute-start.2) | collective-permute-done | bytes 1572896 | tf_op jit(solution)/shard_map/ppermute | solution.py:415
  153.4 10.1 %all-to-all-done.2.r_ref = bf16[64,2,8,768]{3,2,1,0:T(8,128)(2,1)S(1)} async-done(((bf16[64,2,8,768]{3,2,1,0:T(8,128)(2,1)}), bf16[64,2,8,768]{3,2,1,0:T(8,128)(2,1)S(1)}, u32[]{:S(2)}, u32[]{:S(2)}) %all-to-all-start.2) | async-done | bytes 1572896 | tf_op jit(solution)/shard_map/all_to_all | solution.py:400
  163.5 1.5 shard_map.101
  165.0 1.4 collective-permute-start.5
  166.4 6.4 %all-to-all-start.3 = ((bf16[64,8,768]{2,1,0:T(8,128)(2,1)}), bf16[64,8,768]{2,1,0:T(8,128)(2,1)S(1)}, u32[]{:S(2)}, u32[]{:S(2)}) async-start(bf16[64,8,768]{2,1,0:T(8,128)(2,1)} %get-tuple-element.19), calls=%async_computation.3 | async-start | bytes 1572864 | tf_op jit(solution)/shard_map/all_to_all | solution.py:400
  172.8 12.7 %collective-permute-done.5.r_ref = bf16[64,8,768]{2,1,0:T(8,128)(2,1)S(1)} collective-permute-done((bf16[64,8,768]{2,1,0:T(8,128)(2,1)}, bf16[64,8,768]{2,1,0:T(8,128)(2,1)S(1)}, u32[]{:S(2)}, u32[]{:S(2)}) %collective-permute-start.5) | collective-permute-done | bytes 786464 | tf_op jit(solution)/shard_map/ppermute | solution.py:415
  185.5 1.0 shard_map.103.value_ref
  186.6 0.9 copy-done
  187.4 8.4 %all-to-all-done.3.other_ref = bf16[64,8,768]{2,1,0:T(8,128)(2,1)S(1)} async-done(((bf16[64,8,768]{2,1,0:T(8,128)(2,1)}), bf16[64,8,768]{2,1,0:T(8,128)(2,1)S(1)}, u32[]{:S(2)}, u32[]{:S(2)}) %all-to-all-start.3) | async-done | bytes 786464 | tf_op jit(solution)/shard_map/all_to_all | solution.py:400
  195.8 1.0 collective-permute-start.4
  196.8 6.5 %all-to-all-start.4 = ((bf16[64,8,768]{2,1,0:T(8,128)(2,1)}), bf16[64,8,768]{2,1,0:T(8,128)(2,1)S(1)}, u32[]{:S(2)}, u32[]{:S(2)}) async-start(bf16[64,8,768]{2,1,0:T(8,128)(2,1)} %shard_map.104), calls=%async_computation.4 | async-start | bytes 1572864 | tf_op jit(solution)/shard_map/all_to_all | solution.py:400
  203.3 12.5 %collective-permute-done.4.across_ref = bf16[64,8,768]{2,1,0:T(8,128)(2,1)S(1)} collective-permute-done((bf16[64,8,768]{2,1,0:T(8,128)(2,1)S(1)}, bf16[64,8,768]{2,1,0:T(8,128)(2,1)S(1)}, u32[]{:S(2)}, u32[]{:S(2)}) %collective-permute-start.4) | collective-permute-done | bytes 786464 | tf_op jit(solution)/shard_map/ppermute | solution.py:415
  215.7 7.6 %shard_map.102 = (bf16[256,1536]{1,0:T(8,128)(2,1)}, bf16[256,1536]{1,0:T(8,128)(2,1)}) custom-call(bf16[512,1536]{1,0:T(8,128)(2,1)} %shard_map.99.x_ref, bf16[64,8,768]{2,1,0:T(8,128)(2,1)S(1)} %collective-permute-done.4.across_ref, f32[1,1536]{1,0:T(1,128)} %channel_ref.5, bf16[4,384,1024]{2,1,0:T(8,128)(2,1)} %bitcast.9, bf16[4,1024,384]{2,1,0:T(8,128)(2,1)} %bitcast.12), custom_call_target="tpu_custom_call" | custom-call | flops 20000000000 | bytes 10000000 | tf_op jit(solution)/shard_map/pallas_call | solution.py:28
  223.3 3.0 %all-to-all-done.4.across_ref = bf16[64,8,768]{2,1,0:T(8,128)(2,1)S(1)} async-done(((bf16[64,8,768]{2,1,0:T(8,128)(2,1)}), bf16[64,8,768]{2,1,0:T(8,128)(2,1)S(1)}, u32[]{:S(2)}, u32[]{:S(2)}) %all-to-all-start.4) | async-done | bytes 786464 | tf_op jit(solution)/shard_map/all_to_all | solution.py:400
  226.2 7.8 %shard_map.105 = bf16[512,1536]{1,0:T(8,128)(2,1)} custom-call(bf16[256,1536]{1,0:T(8,128)(2,1)} %get-tuple-element.20.x_ref, bf16[64,8,768]{2,1,0:T(8,128)(2,1)S(1)} %all-to-all-done.4.across_ref, f32[1,1536]{1,0:T(1,128)} %channel_ref.5, bf16[4,384,1024]{2,1,0:T(8,128)(2,1)} %bitcast.10, bf16[4,1024,384]{2,1,0:T(8,128)(2,1)} %bitcast.13, ...), custom_call_target="tpu_custom_call" | custom-call | flops 3000000000 | bytes 11000000 | tf_op jit(solution)/shard_map/pallas_call | solution.py:28
  (11 shorter events, 0.0 us)
Async XLA Ops:
  4.0 52.8 %all-to-all-start = ((bf16[64,2,4,1536]{3,2,1,0:T(4,128)(2,1)}), bf16[64,2,4,1536]{3,2,1,0:T(4,128)(2,1)S(1)}, u32[]{:S(2)}, u32[]{:S(2)}) async-start(bf16[64,2,4,1536]{3,2,1,0:T(4,128)(2,1)} %shard_map.96), calls=%async_computation | async-start | bytes 3145728 | tf_op jit(solution)/shard_map/all_to_all | solution.py:400
  58.8 6.3 %copy-start.1 = (bf16[1,2,256,256]{3,2,1,0:T(8,128)(2,1)S(1)}, bf16[1,2,256,256]{3,2,1,0:T(8,128)(2,1)}, u32[]{:S(2)}) copy-start(bf16[1,2,256,256]{3,2,1,0:T(8,128)(2,1)} %param.11) | copy-start | bytes 786436
  58.9 9.1 %copy-start.4 = (f32[1,1536]{1,0:T(1,128)S(1)}, f32[1,1536]{1,0:T(1,128)}, u32[]{:S(2)}) copy-start(f32[1,1536]{1,0:T(1,128)} %gain_ref.1) | copy-start | bytes 18436
  58.9 46.1 %all-to-all-start.1 = ((bf16[64,2,4,1536]{3,2,1,0:T(4,128)(2,1)}), bf16[64,2,4,1536]{3,2,1,0:T(4,128)(2,1)S(1)}, u32[]{:S(2)}, u32[]{:S(2)}) async-start(bf16[64,2,4,1536]{3,2,1,0:T(4,128)(2,1)} %shard_map.97), calls=%async_computation.1 | async-start | bytes 3145728 | tf_op jit(solution)/shard_map/all_to_all | solution.py:400
  65.2 8.2 %collective-permute-start.1 = (bf16[2,256,256]{2,1,0:T(8,128)(2,1)S(1)}, bf16[2,256,256]{2,1,0:T(8,128)(2,1)S(1)}, u32[]{:S(2)}, u32[]{:S(2)}) collective-permute-start(bf16[2,256,256]{2,1,0:T(8,128)(2,1)S(1)} %bitcast.17), channel_id=1, source_target_pairs={{64,0},{128,64},{192,128},{0,192},{65,1},{129,65},{193,129},{1,193... | collective-permute-start | bytes 786440 | tf_op jit(solution)/shard_map/ppermute | solution.py:418
  68.0 5.4 %collective-permute-start = (f32[1,1536]{1,0:T(1,128)S(1)}, f32[1,1536]{1,0:T(1,128)S(1)}, u32[]{:S(2)}, u32[]{:S(2)}) collective-permute-start(f32[1,1536]{1,0:T(1,128)S(1)} %copy-done.4), channel_id=1, source_target_pairs={{64,0},{128,64},{192,128},{0,192},{65,1},{129,65},{193,129},{1,193... | collective-permute-start | bytes 18440 | tf_op jit(solution)/shard_map/ppermute | solution.py:418
  115.8 37.6 %collective-permute-start.2 = (bf16[512,1536]{1,0:T(8,128)(2,1)}, bf16[512,1536]{1,0:T(8,128)(2,1)}, u32[]{:S(2)}, u32[]{:S(2)}) collective-permute-start(bf16[512,1536]{1,0:T(8,128)(2,1)} %get-tuple-element.16), channel_id=1, source_target_pairs={{0,64},{64,128},{128,192},{192,0},{1,65},{65,129},{129,193},{193,1... | collective-permute-start | bytes 4718600 | tf_op jit(solution)/shard_map/ppermute | solution.py:415
  117.1 6.5 %copy-start.2 = (bf16[1,4,128,128]{3,2,1,0:T(8,128)(2,1)S(1)}, bf16[1,4,128,128]{3,2,1,0:T(8,128)(2,1)}, u32[]{:S(2)}) copy-start(bf16[1,4,128,128]{3,2,1,0:T(8,128)(2,1)} %param.12) | copy-start | bytes 393220
  117.2 46.3 %all-to-all-start.2 = ((bf16[64,2,8,768]{3,2,1,0:T(8,128)(2,1)}), bf16[64,2,8,768]{3,2,1,0:T(8,128)(2,1)S(1)}, u32[]{:S(2)}, u32[]{:S(2)}) async-start(bf16[64,2,8,768]{3,2,1,0:T(8,128)(2,1)} %get-tuple-element.15), calls=%async_computation.2 | async-start | bytes 3145728 | tf_op jit(solution)/shard_map/all_to_all | solution.py:400
  123.7 4.8 %collective-permute-start.3 = (bf16[4,128,128]{2,1,0:T(8,128)(2,1)S(1)}, bf16[4,128,128]{2,1,0:T(8,128)(2,1)S(1)}, u32[]{:S(2)}, u32[]{:S(2)}) collective-permute-start(bf16[4,128,128]{2,1,0:T(8,128)(2,1)S(1)} %bitcast.19), channel_id=1, source_target_pairs={{64,0},{128,64},{192,128},{0,192},{65,1},{129,65},{193,129},{1,193... | collective-permute-start | bytes 393224 | tf_op jit(solution)/shard_map/ppermute | solution.py:418
  128.5 0.7 copy-start.3
  165.0 20.5 %collective-permute-start.5 = (bf16[64,8,768]{2,1,0:T(8,128)(2,1)}, bf16[64,8,768]{2,1,0:T(8,128)(2,1)S(1)}, u32[]{:S(2)}, u32[]{:S(2)}) collective-permute-start(bf16[64,8,768]{2,1,0:T(8,128)(2,1)} %get-tuple-element.22), channel_id=1, source_target_pairs={{0,64},{64,128},{128,192},{192,0},{1,65},{65,129},{129,193},{193,1... | collective-permute-start | bytes 2359304 | tf_op jit(solution)/shard_map/ppermute | solution.py:415
  166.4 29.4 %all-to-all-start.3 = ((bf16[64,8,768]{2,1,0:T(8,128)(2,1)}), bf16[64,8,768]{2,1,0:T(8,128)(2,1)S(1)}, u32[]{:S(2)}, u32[]{:S(2)}) async-start(bf16[64,8,768]{2,1,0:T(8,128)(2,1)} %get-tuple-element.19), calls=%async_computation.3 | async-start | bytes 1572864 | tf_op jit(solution)/shard_map/all_to_all | solution.py:400
  186.5 0.9 copy-start
  195.8 19.9 %collective-permute-start.4 = (bf16[64,8,768]{2,1,0:T(8,128)(2,1)S(1)}, bf16[64,8,768]{2,1,0:T(8,128)(2,1)S(1)}, u32[]{:S(2)}, u32[]{:S(2)}) collective-permute-start(bf16[64,8,768]{2,1,0:T(8,128)(2,1)S(1)} %all-to-all-done.3.other_ref), channel_id=1, source_target_pairs={{0,64},{64,128},{128,192},{192,0},{1,65},{65,129},{129,193},{193,1... | collective-permute-start | bytes 2359304 | tf_op jit(solution)/shard_map/ppermute | solution.py:415
  196.8 29.5 %all-to-all-start.4 = ((bf16[64,8,768]{2,1,0:T(8,128)(2,1)}), bf16[64,8,768]{2,1,0:T(8,128)(2,1)S(1)}, u32[]{:S(2)}, u32[]{:S(2)}) async-start(bf16[64,8,768]{2,1,0:T(8,128)(2,1)} %shard_map.104), calls=%async_computation.4 | async-start | bytes 1572864 | tf_op jit(solution)/shard_map/all_to_all | solution.py:400

commit v8 on v7

--- a/solution.py
+++ b/solution.py
@@ -346,30 +346,26 @@
     down_ref,
     other_ref,
     out_ref,
-    x_buf,
     channel_buf,
     up_buf,
     down_buf,
-    other_buf,
     out_buf,
     sems,
 ):
     copies = Copies(sems)
-    loads = [copies.start(x_ref, x_buf), copies.start(channel_ref, channel_buf)]
+    loads = [copies.start(channel_ref, channel_buf)]
     weights = weight_loads(copies, up_ref, down_ref, up_buf, down_buf)
-    other = copies.start(other_ref, other_buf)
 
     def store(g, part, value):
-        copies.wait(other)
         for b in range(2):
             rows = slice(b * (BLK // 2), (b + 1) * (BLK // 2))
-            both = [v.reshape(DEV, 2, WIDTH) for v in (other_buf[rows, part], value[rows])]
+            both = [v.reshape(DEV, 2, WIDTH) for v in (other_ref[rows, part], value[rows])]
             joined = jnp.concatenate(both, axis=1).reshape(BLK, WIDTH)
             out_buf[b * BLK : (b + 1) * BLK, part] = joined
         copies.start(out_buf.at[:, columns_of(g)], out_ref.at[:, columns_of(g)])
 
     last_rows(
-        copies, loads, lambda: x_buf[...].astype(F32), across_ref, channel_buf, weights, store
+        copies, loads, lambda: x_ref[...].astype(F32), across_ref, channel_buf, weights, store
     )
     copies.wait()
 
@@ -514,7 +510,7 @@
     bufs = [buf(channel_gain), buf(up), buf(down)]
     other, kept = call(
         last_kernel,
-        (far(part_rows), far(part_rows)),
+        (part_rows, part_rows),
         [entered, across0, channel_gain, up, down],
         [buf(sequence), *bufs, buf(part_rows), buf(part_rows), sems(15)],
         (LONG, 10_000_000, 1_000_000),
@@ -523,10 +519,10 @@
     second = call(
         final_kernel,
         sequence,
-        [hbm(kept), across1, channel_gain, up, down, hbm(other)],
-        [buf(part_rows), *bufs, buf(part_rows), buf(sequence), sems(15)],
+        [kept, across1, channel_gain, up, down, other],
+        [*bufs, buf(sequence), sems(13)],
         (3_000_000_000, 11_000_000, 1_000_000),
-        near=(1,),
+        near=(0, 1, 5),
     )
     return first.reshape(1, *x.shape), second.reshape(1, *x.shape)
 

time: 235 us -> 234 us (level)
  no operation moved by 1% of the time
where the time goes in v8:
time: 234 us
  waiting for transfers between devices  147 us (63%)
  starting transfers between devices  47.2 us (20%)
  Pallas kernels  36.8 us (16%)
    all_to_all x5, waiting for transfers between devices, exchange(): lax.all_to_all(hbm(value), 'seq', split_axis=0, concat_axis=0, tiled=True)  91.3 us
    ppermute x3, waiting for transfers between devices, ahead(): lax.ppermute(value, 'section', [(s, (s + 1) % count) for s in range(count)])  47.7 us
    all_to_all x5, starting transfers between devices, exchange(): lax.all_to_all(hbm(value), 'seq', split_axis=0, concat_axis=0, tiled=True)  38.7 us
    pallas_call x9, Pallas kernels, call(): pl.pallas_call(kernel, out_shape=outs, in_specs=scalars + [nearby if n in...  36.8 us
    ppermute x3, waiting for transfers between devices, behind(): lax.ppermute(value, 'section', [((s + 1) % count, s) for s in range(count)])  8.21 us
    ppermute x3, starting transfers between devices, behind(): lax.ppermute(value, 'section', [((s + 1) % count, s) for s in range(count)])  4.75 us
  transfers between devices with their start and end apart: 11, of which 10 were waited for; matrix products, arithmetic and copies ran while one was open for 0% of the time, Pallas kernels for 5%

profile of v8, /device:TPU:1, one launch (start us, length us, event | category | flops | bytes accessed | tf_op | source)
XLA Modules:
  0.0 233.7 jit_solution(5579727913995099708)
XLA Ops:
  0.6 3.4 %shard_map.96 = bf16[64,2,4,1536]{3,2,1,0:T(4,128)(2,1)} custom-call(bf16[512,1536]{1,0:T(8,128)(2,1)} %bitcast.14, f32[1,1536]{1,0:T(1,128)} %gain_ref.1, bf16[2,256,256]{2,1,0:T(8,128)(2,1)} %bitcast.16), custom_call_target="tpu_custom_call" | custom-call | flops 2000000000 | bytes 4000000 | tf_op jit(solution)/shard_map/pallas_call | solution.py:28
  4.0 13.0 %all-to-all-start = ((bf16[64,2,4,1536]{3,2,1,0:T(4,128)(2,1)}), bf16[64,2,4,1536]{3,2,1,0:T(4,128)(2,1)S(1)}, u32[]{:S(2)}, u32[]{:S(2)}) async-start(bf16[64,2,4,1536]{3,2,1,0:T(4,128)(2,1)} %shard_map.96), calls=%async_computation | async-start | bytes 3145728 | tf_op jit(solution)/shard_map/all_to_all | solution.py:396
  17.0 2.4 %shard_map.95 = (bf16[512,512]{1,0:T(8,128)(2,1)S(1)}, bf16[512,512]{1,0:T(8,128)(2,1)S(1)}) custom-call(bf16[4,128,128]{2,1,0:T(8,128)(2,1)} %bitcast.18), custom_call_target="tpu_custom_call" | custom-call | flops 400000000 | bytes 3000000 | tf_op jit(solution)/shard_map/pallas_call | solution.py:28
  19.4 37.4 %all-to-all-done.r_ref = bf16[64,2,4,1536]{3,2,1,0:T(4,128)(2,1)S(1)} async-done(((bf16[64,2,4,1536]{3,2,1,0:T(4,128)(2,1)}), bf16[64,2,4,1536]{3,2,1,0:T(4,128)(2,1)S(1)}, u32[]{:S(2)}, u32[]{:S(2)}) %all-to-all-start) | async-done | bytes 1572896 | tf_op jit(solution)/shard_map/all_to_all | solution.py:396
  56.8 2.0 shard_map.97
  58.9 6.3 %all-to-all-start.1 = ((bf16[64,2,4,1536]{3,2,1,0:T(4,128)(2,1)}), bf16[64,2,4,1536]{3,2,1,0:T(4,128)(2,1)S(1)}, u32[]{:S(2)}, u32[]{:S(2)}) async-start(bf16[64,2,4,1536]{3,2,1,0:T(4,128)(2,1)} %shard_map.97), calls=%async_computation.1 | async-start | bytes 3145728 | tf_op jit(solution)/shard_map/all_to_all | solution.py:396
  65.2 2.8 %collective-permute-start.1 = (bf16[2,256,256]{2,1,0:T(8,128)(2,1)S(1)}, bf16[2,256,256]{2,1,0:T(8,128)(2,1)S(1)}, u32[]{:S(2)}, u32[]{:S(2)}) collective-permute-start(bf16[2,256,256]{2,1,0:T(8,128)(2,1)S(1)} %bitcast.17), channel_id=1, source_target_pairs={{64,0},{128,64},{192,128},{0,192},{65,1},{129,65},{193,129},{1,193... | collective-permute-start | bytes 786440 | tf_op jit(solution)/shard_map/ppermute | solution.py:414
  68.0 0.5 collective-permute-start
  68.4 4.9 %collective-permute-done.gain_ref = f32[1,1536]{1,0:T(1,128)S(1)} collective-permute-done((f32[1,1536]{1,0:T(1,128)S(1)}, f32[1,1536]{1,0:T(1,128)S(1)}, u32[]{:S(2)}, u32[]{:S(2)}) %collective-permute-start) | collective-permute-done | bytes 6176 | tf_op jit(solution)/shard_map/ppermute | solution.py:414
  73.3 31.6 %all-to-all-done.1.across_ref = bf16[64,2,4,1536]{3,2,1,0:T(4,128)(2,1)S(1)} async-done(((bf16[64,2,4,1536]{3,2,1,0:T(4,128)(2,1)}), bf16[64,2,4,1536]{3,2,1,0:T(4,128)(2,1)S(1)}, u32[]{:S(2)}, u32[]{:S(2)}) %all-to-all-start.1) | async-done | bytes 1572896 | tf_op jit(solution)/shard_map/all_to_all | solution.py:396
  104.9 10.8 %shard_map.98 = (bf16[512,1536]{1,0:T(8,128)(2,1)}, bf16[512,1536]{1,0:T(8,128)(2,1)}, bf16[64,2,8,768]{3,2,1,0:T(8,128)(2,1)}) custom-call(s32[1]{0:T(128)} %bitcast.flag_ref.other_ref, bf16[512,1536]{1,0:T(8,128)(2,1)} %bitcast.15, bf16[64,2,4,1536]{3,2,1,0:T(4,128)(2,1)S(1)} %all-to-all-done.1.across_ref, f32[1,1536]{1,0:T(1,128)} %channel_ref.5, ...), custom_call_target="tpu_custom_call" | custom-call | flops 7000000000 | bytes 18000000 | tf_op jit(solution)/shard_map/pallas_call | solution.py:28
  115.8 1.4 collective-permute-start.2
  117.2 6.5 %all-to-all-start.2 = ((bf16[64,2,8,768]{3,2,1,0:T(8,128)(2,1)}), bf16[64,2,8,768]{3,2,1,0:T(8,128)(2,1)S(1)}, u32[]{:S(2)}, u32[]{:S(2)}) async-start(bf16[64,2,8,768]{3,2,1,0:T(8,128)(2,1)} %get-tuple-element.15), calls=%async_computation.2 | async-start | bytes 3145728 | tf_op jit(solution)/shard_map/all_to_all | solution.py:396
  123.7 1.5 collective-permute-start.3
  125.2 3.3 %collective-permute-done.3.cross_ref = bf16[4,128,128]{2,1,0:T(8,128)(2,1)S(1)} collective-permute-done((bf16[4,128,128]{2,1,0:T(8,128)(2,1)S(1)}, bf16[4,128,128]{2,1,0:T(8,128)(2,1)S(1)}, u32[]{:S(2)}, u32[]{:S(2)}) %collective-permute-start.3) | collective-permute-done | bytes 131104 | tf_op jit(solution)/shard_map/ppermute | solution.py:414
  128.5 0.7 copy-done.3
  129.1 1.6 shard_map.100.spread_ref
  130.8 22.6 %collective-permute-done.2.value_ref = bf16[512,1536]{1,0:T(8,128)(2,1)} collective-permute-done((bf16[512,1536]{1,0:T(8,128)(2,1)}, bf16[512,1536]{1,0:T(8,128)(2,1)}, u32[]{:S(2)}, u32[]{:S(2)}) %collective-permute-start.2) | collective-permute-done | bytes 1572896 | tf_op jit(solution)/shard_map/ppermute | solution.py:411
  153.4 10.1 %all-to-all-done.2.r_ref = bf16[64,2,8,768]{3,2,1,0:T(8,128)(2,1)S(1)} async-done(((bf16[64,2,8,768]{3,2,1,0:T(8,128)(2,1)}), bf16[64,2,8,768]{3,2,1,0:T(8,128)(2,1)S(1)}, u32[]{:S(2)}, u32[]{:S(2)}) %all-to-all-start.2) | async-done | bytes 1572896 | tf_op jit(solution)/shard_map/all_to_all | solution.py:396
  163.5 1.5 shard_map.101
  165.0 1.4 collective-permute-start.5
  166.4 6.4 %all-to-all-start.3 = ((bf16[64,8,768]{2,1,0:T(8,128)(2,1)}), bf16[64,8,768]{2,1,0:T(8,128)(2,1)S(1)}, u32[]{:S(2)}, u32[]{:S(2)}) async-start(bf16[64,8,768]{2,1,0:T(8,128)(2,1)} %get-tuple-element.19), calls=%async_computation.3 | async-start | bytes 1572864 | tf_op jit(solution)/shard_map/all_to_all | solution.py:396
  172.8 12.7 %collective-permute-done.5.r_ref = bf16[64,8,768]{2,1,0:T(8,128)(2,1)S(1)} collective-permute-done((bf16[64,8,768]{2,1,0:T(8,128)(2,1)}, bf16[64,8,768]{2,1,0:T(8,128)(2,1)S(1)}, u32[]{:S(2)}, u32[]{:S(2)}) %collective-permute-start.5) | collective-permute-done | bytes 786464 | tf_op jit(solution)/shard_map/ppermute | solution.py:411
  185.5 1.0 shard_map.103.value_ref
  186.6 0.9 copy-done
  187.4 8.4 %all-to-all-done.3.other_ref = bf16[64,8,768]{2,1,0:T(8,128)(2,1)S(1)} async-done(((bf16[64,8,768]{2,1,0:T(8,128)(2,1)}), bf16[64,8,768]{2,1,0:T(8,128)(2,1)S(1)}, u32[]{:S(2)}, u32[]{:S(2)}) %all-to-all-start.3) | async-done | bytes 786464 | tf_op jit(solution)/shard_map/all_to_all | solution.py:396
  195.8 1.0 collective-permute-start.4
  196.8 6.5 %all-to-all-start.4 = ((bf16[64,8,768]{2,1,0:T(8,128)(2,1)}), bf16[64,8,768]{2,1,0:T(8,128)(2,1)S(1)}, u32[]{:S(2)}, u32[]{:S(2)}) async-start(bf16[64,8,768]{2,1,0:T(8,128)(2,1)} %shard_map.104), calls=%async_computation.4 | async-start | bytes 1572864 | tf_op jit(solution)/shard_map/all_to_all | solution.py:396
  203.3 12.5 %collective-permute-done.4.across_ref = bf16[64,8,768]{2,1,0:T(8,128)(2,1)S(1)} collective-permute-done((bf16[64,8,768]{2,1,0:T(8,128)(2,1)S(1)}, bf16[64,8,768]{2,1,0:T(8,128)(2,1)S(1)}, u32[]{:S(2)}, u32[]{:S(2)}) %collective-permute-start.4) | collective-permute-done | bytes 786464 | tf_op jit(solution)/shard_map/ppermute | solution.py:411
  215.7 6.7 %shard_map.102 = (bf16[256,1536]{1,0:T(8,128)(2,1)S(1)}, bf16[256,1536]{1,0:T(8,128)(2,1)S(1)}) custom-call(bf16[512,1536]{1,0:T(8,128)(2,1)} %shard_map.99.x_ref, bf16[64,8,768]{2,1,0:T(8,128)(2,1)S(1)} %collective-permute-done.4.across_ref, f32[1,1536]{1,0:T(1,128)} %channel_ref.5, bf16[4,384,1024]{2,1,0:T(8,128)(2,1)} %bitcast.9, ...), custom_call_target="tpu_custom_call" | custom-call | flops 20000000000 | bytes 10000000 | tf_op jit(solution)/shard_map/pallas_call | solution.py:28
  222.5 3.8 %all-to-all-done.4.across_ref = bf16[64,8,768]{2,1,0:T(8,128)(2,1)S(1)} async-done(((bf16[64,8,768]{2,1,0:T(8,128)(2,1)}), bf16[64,8,768]{2,1,0:T(8,128)(2,1)S(1)}, u32[]{:S(2)}, u32[]{:S(2)}) %all-to-all-start.4) | async-done | bytes 786464 | tf_op jit(solution)/shard_map/all_to_all | solution.py:396
  226.2 7.3 %shard_map.105 = bf16[512,1536]{1,0:T(8,128)(2,1)} custom-call(bf16[256,1536]{1,0:T(8,128)(2,1)S(1)} %get-tuple-element.20.x_ref, bf16[64,8,768]{2,1,0:T(8,128)(2,1)S(1)} %all-to-all-done.4.across_ref, f32[1,1536]{1,0:T(1,128)} %channel_ref.5, bf16[4,384,1024]{2,1,0:T(8,128)(2,1)} %bitcast.10, bf16[4,1024,384]{2,1,0:T(8,128)(2,1)} %bitcast.13, ...), custom_call_target="tpu_custom_call" | custom-call | flops 3000000000 | bytes 11000000 | tf_op jit(solution)/shard_map/pallas_call | solution.py:28
  (11 shorter events, 0.0 us)
Async XLA Ops:
  4.0 52.8 %all-to-all-start = ((bf16[64,2,4,1536]{3,2,1,0:T(4,128)(2,1)}), bf16[64,2,4,1536]{3,2,1,0:T(4,128)(2,1)S(1)}, u32[]{:S(2)}, u32[]{:S(2)}) async-start(bf16[64,2,4,1536]{3,2,1,0:T(4,128)(2,1)} %shard_map.96), calls=%async_computation | async-start | bytes 3145728 | tf_op jit(solution)/shard_map/all_to_all | solution.py:396
  58.8 6.3 %copy-start.1 = (bf16[1,2,256,256]{3,2,1,0:T(8,128)(2,1)S(1)}, bf16[1,2,256,256]{3,2,1,0:T(8,128)(2,1)}, u32[]{:S(2)}) copy-start(bf16[1,2,256,256]{3,2,1,0:T(8,128)(2,1)} %param.11) | copy-start | bytes 786436
  58.9 9.1 %copy-start.4 = (f32[1,1536]{1,0:T(1,128)S(1)}, f32[1,1536]{1,0:T(1,128)}, u32[]{:S(2)}) copy-start(f32[1,1536]{1,0:T(1,128)} %gain_ref.1) | copy-start | bytes 18436
  58.9 46.1 %all-to-all-start.1 = ((bf16[64,2,4,1536]{3,2,1,0:T(4,128)(2,1)}), bf16[64,2,4,1536]{3,2,1,0:T(4,128)(2,1)S(1)}, u32[]{:S(2)}, u32[]{:S(2)}) async-start(bf16[64,2,4,1536]{3,2,1,0:T(4,128)(2,1)} %shard_map.97), calls=%async_computation.1 | async-start | bytes 3145728 | tf_op jit(solution)/shard_map/all_to_all | solution.py:396
  65.2 8.2 %collective-permute-start.1 = (bf16[2,256,256]{2,1,0:T(8,128)(2,1)S(1)}, bf16[2,256,256]{2,1,0:T(8,128)(2,1)S(1)}, u32[]{:S(2)}, u32[]{:S(2)}) collective-permute-start(bf16[2,256,256]{2,1,0:T(8,128)(2,1)S(1)} %bitcast.17), channel_id=1, source_target_pairs={{64,0},{128,64},{192,128},{0,192},{65,1},{129,65},{193,129},{1,193... | collective-permute-start | bytes 786440 | tf_op jit(solution)/shard_map/ppermute | solution.py:414
  68.0 5.4 %collective-permute-start = (f32[1,1536]{1,0:T(1,128)S(1)}, f32[1,1536]{1,0:T(1,128)S(1)}, u32[]{:S(2)}, u32[]{:S(2)}) collective-permute-start(f32[1,1536]{1,0:T(1,128)S(1)} %copy-done.4), channel_id=1, source_target_pairs={{64,0},{128,64},{192,128},{0,192},{65,1},{129,65},{193,129},{1,193... | collective-permute-start | bytes 18440 | tf_op jit(solution)/shard_map/ppermute | solution.py:414
  115.8 37.6 %collective-permute-start.2 = (bf16[512,1536]{1,0:T(8,128)(2,1)}, bf16[512,1536]{1,0:T(8,128)(2,1)}, u32[]{:S(2)}, u32[]{:S(2)}) collective-permute-start(bf16[512,1536]{1,0:T(8,128)(2,1)} %get-tuple-element.16), channel_id=1, source_target_pairs={{0,64},{64,128},{128,192},{192,0},{1,65},{65,129},{129,193},{193,1... | collective-permute-start | bytes 4718600 | tf_op jit(solution)/shard_map/ppermute | solution.py:411
  117.1 6.5 %copy-start.2 = (bf16[1,4,128,128]{3,2,1,0:T(8,128)(2,1)S(1)}, bf16[1,4,128,128]{3,2,1,0:T(8,128)(2,1)}, u32[]{:S(2)}) copy-start(bf16[1,4,128,128]{3,2,1,0:T(8,128)(2,1)} %param.12) | copy-start | bytes 393220
  117.2 46.3 %all-to-all-start.2 = ((bf16[64,2,8,768]{3,2,1,0:T(8,128)(2,1)}), bf16[64,2,8,768]{3,2,1,0:T(8,128)(2,1)S(1)}, u32[]{:S(2)}, u32[]{:S(2)}) async-start(bf16[64,2,8,768]{3,2,1,0:T(8,128)(2,1)} %get-tuple-element.15), calls=%async_computation.2 | async-start | bytes 3145728 | tf_op jit(solution)/shard_map/all_to_all | solution.py:396
  123.7 4.8 %collective-permute-start.3 = (bf16[4,128,128]{2,1,0:T(8,128)(2,1)S(1)}, bf16[4,128,128]{2,1,0:T(8,128)(2,1)S(1)}, u32[]{:S(2)}, u32[]{:S(2)}) collective-permute-start(bf16[4,128,128]{2,1,0:T(8,128)(2,1)S(1)} %bitcast.19), channel_id=1, source_target_pairs={{64,0},{128,64},{192,128},{0,192},{65,1},{129,65},{193,129},{1,193... | collective-permute-start | bytes 393224 | tf_op jit(solution)/shard_map/ppermute | solution.py:414
  128.5 0.7 copy-start.3
  165.0 20.5 %collective-permute-start.5 = (bf16[64,8,768]{2,1,0:T(8,128)(2,1)}, bf16[64,8,768]{2,1,0:T(8,128)(2,1)S(1)}, u32[]{:S(2)}, u32[]{:S(2)}) collective-permute-start(bf16[64,8,768]{2,1,0:T(8,128)(2,1)} %get-tuple-element.22), channel_id=1, source_target_pairs={{0,64},{64,128},{128,192},{192,0},{1,65},{65,129},{129,193},{193,1... | collective-permute-start | bytes 2359304 | tf_op jit(solution)/shard_map/ppermute | solution.py:411
  166.4 29.4 %all-to-all-start.3 = ((bf16[64,8,768]{2,1,0:T(8,128)(2,1)}), bf16[64,8,768]{2,1,0:T(8,128)(2,1)S(1)}, u32[]{:S(2)}, u32[]{:S(2)}) async-start(bf16[64,8,768]{2,1,0:T(8,128)(2,1)} %get-tuple-element.19), calls=%async_computation.3 | async-start | bytes 1572864 | tf_op jit(solution)/shard_map/all_to_all | solution.py:396
  186.5 0.9 copy-start
  195.8 19.9 %collective-permute-start.4 = (bf16[64,8,768]{2,1,0:T(8,128)(2,1)S(1)}, bf16[64,8,768]{2,1,0:T(8,128)(2,1)S(1)}, u32[]{:S(2)}, u32[]{:S(2)}) collective-permute-start(bf16[64,8,768]{2,1,0:T(8,128)(2,1)S(1)} %all-to-all-done.3.other_ref), channel_id=1, source_target_pairs={{0,64},{64,128},{128,192},{192,0},{1,65},{65,129},{129,193},{193,1... | collective-permute-start | bytes 2359304 | tf_op jit(solution)/shard_map/ppermute | solution.py:411
  196.8 29.5 %all-to-all-start.4 = ((bf16[64,8,768]{2,1,0:T(8,128)(2,1)}), bf16[64,8,768]{2,1,0:T(8,128)(2,1)S(1)}, u32[]{:S(2)}, u32[]{:S(2)}) async-start(bf16[64,8,768]{2,1,0:T(8,128)(2,1)} %shard_map.104), calls=%async_computation.4 | async-start | bytes 1572864 | tf_op jit(solution)/shard_map/all_to_all | solution.py:396

commit v9 on v8

--- a/solution.py
+++ b/solution.py
@@ -19,7 +19,7 @@
 F32 = jnp.float32
 
 
-def call(kernel, out_shape, inputs, scratch, cost, flags=None, near=(), mib=32):
+def call(kernel, out_shape, inputs, scratch, cost, flags=None, near=(), near_out=(), mib=32):
     outs = out_shape if isinstance(out_shape, tuple) else (out_shape,)
     held = pl.BlockSpec(memory_space=pl.ANY)
     nearby = pl.BlockSpec(memory_space=pltpu.VMEM)
@@ -29,7 +29,7 @@
         kernel,
         out_shape=outs,
         in_specs=scalars + [nearby if n in near else held for n in range(len(inputs))],
-        out_specs=[held] * len(outs),
+        out_specs=[nearby if n in near_out else held for n in range(len(outs))],
         scratch_shapes=scratch,
         cost_estimate=pl.CostEstimate(
             flops=flops, bytes_accessed=bytes_accessed, transcendentals=transcendentals
@@ -124,7 +124,7 @@
     )
 
 
-def spread_own_kernel(cross_ref, whole_ref, part_ref, cross_buf, whole_buf, part_buf, sems):
+def spread_own_kernel(cross_ref, whole_ref, cross_buf, whole_buf, sems):
     copies = Copies(sems)
     copies.start(cross_ref, cross_buf)
     copies.wait()
@@ -136,17 +136,24 @@
         3,
     )
     copies.start(whole_buf, whole_ref)
-    part_buf[...] = spread_part(cross, 1)
-    copies.start(part_buf, part_ref)
-    copies.wait()
-
-
-def spread_next_kernel(cross_ref, part_ref, cross_buf, part_buf, sems):
-    copies = Copies(sems)
-    copies.start(cross_ref, cross_buf)
-    copies.wait()
-    part_buf[...] = spread_part(cross_buf[...].reshape(2 * BLK, 128), 0)
-    copies.start(part_buf, part_ref)
+    copies.wait()
+
+
+def spread_parts_kernel(next_ref, own_ref, part0_ref, part1_ref, cross_buf, part_buf, sems):
+    copies = Copies(sems)
+    copies.start(next_ref, cross_buf.at[0])
+    copies.start(own_ref, cross_buf.at[1])
+    copies.wait()
+    for c, part_ref in enumerate((part0_ref, part1_ref)):
+        part_buf[c] = spread_part(cross_buf[c].reshape(2 * BLK, 128), c)
+        copies.start(part_buf.at[c], part_ref)
+    copies.wait()
+
+
+def bring_kernel(x_ref, gain_ref, x_out, gain_out, sems):
+    copies = Copies(sems)
+    copies.start(x_ref, x_out)
+    copies.start(gain_ref, gain_out)
     copies.wait()
 
 
@@ -234,8 +241,6 @@
     first_ref,
     entering_ref,
     out_ref,
-    x_buf,
-    channel_buf,
     up_buf,
     down_buf,
     queued_buf,
@@ -248,10 +253,7 @@
 ):
     copies = Copies(sems)
     rows = [pl.ds(b * BLK, BLK) for b in range(2)]
-    x_loads = [copies.start(x_ref.at[rows[0]], x_buf.at[rows[0]])]
-    channel_load = copies.start(channel_ref, channel_buf)
     up, down, start = weight_loads(copies, up_ref, down_ref, up_buf, down_buf)
-    x_loads.append(copies.start(x_ref.at[rows[1]], x_buf.at[rows[1]]))
     for g in range(2, GROUPS):
         start(g)
     late = [
@@ -260,16 +262,14 @@
         copies.start(queued_ref, queued_buf),
     ]
     last = flag_ref[0] == 1
-    copies.wait(channel_load)
     mixed = []
     for b in range(2):
 
         def store(g, part, value):
             first_buf[rows[b], part] = value
 
-        copies.wait(x_loads[b])
-        residual = x_buf[rows[b], :].astype(F32) + across_ref[:, b].reshape(BLK, D).astype(F32)
-        channel_rows(residual, channel_buf[...], up, down, store)
+        residual = x_ref[rows[b], :].astype(F32) + across_ref[:, b].reshape(BLK, D).astype(F32)
+        channel_rows(residual, channel_ref[...], up, down, store)
         if b == 0:
             copies.wait(*late)
         copies.start(first_buf.at[rows[b]], first_ref.at[rows[b]])
@@ -434,12 +434,12 @@
         (2_000_000_000, 4_000_000, 0),
     )
     columns = exchange(sent)
-    whole, own_part = call(
+    whole = call(
         spread_own_kernel,
-        (square, square),
+        square,
         [cross],
-        [buf(cross), buf(square), buf(square), sems(3)],
-        (400_000_000, 3_000_000, 0),
+        [buf(cross), buf(square), sems(2)],
+        (200_000_000, 2_000_000, 0),
     )
     next_gain, next_factor, next_cross = behind(norm_gain), behind(factor), behind(cross)
     out = call(
@@ -452,21 +452,21 @@
         mib=16,
     )
     across = exchange(out)
-    next_part = call(
-        spread_next_kernel,
-        square,
-        [next_cross],
-        [buf(cross), buf(square), sems(2)],
-        (200_000_000, 2_000_000, 0),
+    near_x, near_gain = call(
+        bring_kernel,
+        (sequence, jax.ShapeDtypeStruct(channel_gain.shape, F32)),
+        [held_x, channel_gain],
+        [sems(2)],
+        (LONG, 3_000_000, 0),
+        near_out=(0, 1),
+        mib=2,
     )
 
     first, entering, sent = call(
         middle_kernel,
         (sequence, far(sequence), pair),
-        [held_x, across, channel_gain, up, down, queued, next_gain, next_factor],
+        [near_x, across, near_gain, up, down, queued, next_gain, next_factor],
         [
-            buf(x),
-            buf(channel_gain),
             buf(up),
             buf(down),
             buf(x),
@@ -475,20 +475,25 @@
             buf(x),
             buf(x),
             buf(shape(2, DEV, 8, HALF)),
-            sems(20),
+            sems(17),
         ],
         (7_000_000_000, 18_000_000, 2_000_000),
         flags,
-        near=(1,),
+        near=(0, 1, 2),
     )
     columns = exchange(sent)
+    parts = call(
+        spread_parts_kernel,
+        (square, square),
+        [next_cross, cross],
+        [buf(shape(2, *cross.shape)), buf(shape(2, 2 * BLK, 2 * BLK)), sems(4)],
+        (400_000_000, 2_000_000, 0),
+    )
     entered = ahead(entering)
-    entered = after(entered, flags)
-    columns, entered = lax.optimization_barrier((columns, entered))
     out0, columns1 = call(
         cross_first_kernel,
         (message, far(message)),
-        [next_part, columns],
+        [parts[0], columns],
         [buf(square), buf(message), sems(4)],
         (400_000_000, 2_000_000, 0),
         near=(1,),
@@ -496,10 +501,11 @@
     )
     across0 = exchange(out0)
     columns1 = ahead(columns1)
+    columns1, entered = lax.optimization_barrier((columns1, entered))
     out1 = call(
         cross_second_kernel,
         message,
-        [own_part, columns1],
+        [parts[1], columns1],
         [buf(square), buf(message), sems(3)],
         (LONG, 2_000_000, 0),
         near=(1,),

time: 234 us -> 232 us (level)
  waiting for transfers between devices: 147 us -> 144 us
    ppermute x3, waiting for transfers between devices: 47.7 us -> 25 us  [ahead(): lax.ppermute(value, 'section', [(s, (s + 1) % count) for s in range(count)])]
    all_to_all x5, waiting for transfers between devices: 91.3 us -> 113 us  [exchange(): lax.all_to_all(hbm(value), 'seq', split_axis=0, concat_axis=0, tiled=True)]
    pallas_call x9 -> x10, Pallas kernels: 36.8 us -> 37.5 us  [call(): pl.pallas_call(kernel, out_shape=outs, in_specs=scalars + [nearby if n in...]
  transfers between devices with their start and end apart: 11 -> 11, of which waited for: 10 -> 9; matrix products, arithmetic and copies ran while one was open for 0% -> 0% of each run, Pallas kernels for 5% -> 6%
where the time goes in v9:
time: 232 us; the launch traced here: 231 us
  waiting for transfers between devices  144 us (62%)
  starting transfers between devices  47.1 us (20%)
  Pallas kernels  37.5 us (16%)
    all_to_all x5, waiting for transfers between devices, exchange(): lax.all_to_all(hbm(value), 'seq', split_axis=0, concat_axis=0, tiled=True)  113 us
    all_to_all x5, starting transfers between devices, exchange(): lax.all_to_all(hbm(value), 'seq', split_axis=0, concat_axis=0, tiled=True)  38.3 us
    pallas_call x10, Pallas kernels, call(): pl.pallas_call(kernel, out_shape=outs, in_specs=scalars + [nearby if n in...  37.5 us
    ppermute x3, waiting for transfers between devices, ahead(): lax.ppermute(value, 'section', [(s, (s + 1) % count) for s in range(count)])  25 us
    ppermute x3, waiting for transfers between devices, behind(): lax.ppermute(value, 'section', [((s + 1) % count, s) for s in range(count)])  6.52 us
    ppermute x3, starting transfers between devices, behind(): lax.ppermute(value, 'section', [((s + 1) % count, s) for s in range(count)])  4.82 us
  transfers between devices with their start and end apart: 11, of which 9 were waited for; matrix products, arithmetic and copies ran while one was open for 0% of the time, Pallas kernels for 6%

profile of v9, /device:TPU:1, one launch (start us, length us, event | category | flops | bytes accessed | tf_op | source)
XLA Modules:
  0.0 231.4 jit_solution(2610124621025374226)
XLA Ops:
  0.6 3.4 %shard_map.97 = bf16[64,2,4,1536]{3,2,1,0:T(4,128)(2,1)} custom-call(bf16[512,1536]{1,0:T(8,128)(2,1)} %bitcast.14, f32[1,1536]{1,0:T(1,128)} %gain_ref.3, bf16[2,256,256]{2,1,0:T(8,128)(2,1)} %bitcast.3.factor_ref), custom_call_target="tpu_custom_call" | custom-call | flops 2000000000 | bytes 4000000 | tf_op jit(solution)/shard_map/pallas_call | solution.py:28
  4.0 13.0 %all-to-all-start = ((bf16[64,2,4,1536]{3,2,1,0:T(4,128)(2,1)}), bf16[64,2,4,1536]{3,2,1,0:T(4,128)(2,1)S(1)}, u32[]{:S(2)}, u32[]{:S(2)}) async-start(bf16[64,2,4,1536]{3,2,1,0:T(4,128)(2,1)} %shard_map.97), calls=%async_computation | async-start | bytes 3145728 | tf_op jit(solution)/shard_map/all_to_all | solution.py:396
  17.0 1.6 shard_map.96.spread_ref
  18.6 38.1 %all-to-all-done.r_ref = bf16[64,2,4,1536]{3,2,1,0:T(4,128)(2,1)S(1)} async-done(((bf16[64,2,4,1536]{3,2,1,0:T(4,128)(2,1)}), bf16[64,2,4,1536]{3,2,1,0:T(4,128)(2,1)S(1)}, u32[]{:S(2)}, u32[]{:S(2)}) %all-to-all-start) | async-done | bytes 1572896 | tf_op jit(solution)/shard_map/all_to_all | solution.py:396
  56.8 2.0 shard_map.98
  58.9 6.1 %all-to-all-start.1 = ((bf16[64,2,4,1536]{3,2,1,0:T(4,128)(2,1)}), bf16[64,2,4,1536]{3,2,1,0:T(4,128)(2,1)S(1)}, u32[]{:S(2)}, u32[]{:S(2)}) async-start(bf16[64,2,4,1536]{3,2,1,0:T(4,128)(2,1)} %shard_map.98), calls=%async_computation.1 | async-start | bytes 3145728 | tf_op jit(solution)/shard_map/all_to_all | solution.py:396
  65.0 2.8 %collective-permute-start.1 = (bf16[2,256,256]{2,1,0:T(8,128)(2,1)}, bf16[2,256,256]{2,1,0:T(8,128)(2,1)S(1)}, u32[]{:S(2)}, u32[]{:S(2)}) collective-permute-start(bf16[2,256,256]{2,1,0:T(8,128)(2,1)} %bitcast.3.factor_ref), channel_id=1, source_target_pairs={{64,0},{128,64},{192,128},{0,192},{65,1},{129,65},{193,129},{1,193... | collective-permute-start | bytes 786440 | tf_op jit(solution)/shard_map/ppermute | solution.py:414
  67.8 0.5 collective-permute-start
  68.3 1.4 shard_map.95
  69.7 3.7 %collective-permute-done.gain_ref = f32[1,1536]{1,0:T(1,128)S(1)} collective-permute-done((f32[1,1536]{1,0:T(1,128)S(1)}, f32[1,1536]{1,0:T(1,128)S(1)}, u32[]{:S(2)}, u32[]{:S(2)}) %collective-permute-start) | collective-permute-done | bytes 6176 | tf_op jit(solution)/shard_map/ppermute | solution.py:414
  73.4 31.4 %all-to-all-done.1.across_ref = bf16[64,2,4,1536]{3,2,1,0:T(4,128)(2,1)S(1)} async-done(((bf16[64,2,4,1536]{3,2,1,0:T(4,128)(2,1)}), bf16[64,2,4,1536]{3,2,1,0:T(4,128)(2,1)S(1)}, u32[]{:S(2)}, u32[]{:S(2)}) %all-to-all-start.1) | async-done | bytes 1572896 | tf_op jit(solution)/shard_map/all_to_all | solution.py:396
  104.8 9.9 %shard_map.99 = (bf16[512,1536]{1,0:T(8,128)(2,1)}, bf16[512,1536]{1,0:T(8,128)(2,1)}, bf16[64,2,8,768]{3,2,1,0:T(8,128)(2,1)}) custom-call(s32[1]{0:T(128)} %bitcast.flag_ref, bf16[512,1536]{1,0:T(8,128)(2,1)S(1)} %get-tuple-element.15.x_ref, bf16[64,2,4,1536]{3,2,1,0:T(4,128)(2,1)S(1)} %all-to-all-done.1.across_ref, ...), custom_call_target="tpu_custom_call" | custom-call | flops 7000000000 | bytes 18000000 | tf_op jit(solution)/shard_map/pallas_call | solution.py:28
  114.8 6.3 %all-to-all-start.2 = ((bf16[64,2,8,768]{3,2,1,0:T(8,128)(2,1)}), bf16[64,2,8,768]{3,2,1,0:T(8,128)(2,1)S(1)}, u32[]{:S(2)}, u32[]{:S(2)}) async-start(bf16[64,2,8,768]{3,2,1,0:T(8,128)(2,1)} %get-tuple-element.19), calls=%async_computation.2 | async-start | bytes 3145728 | tf_op jit(solution)/shard_map/all_to_all | solution.py:396
  121.0 1.4 collective-permute-start.4
  122.4 1.5 collective-permute-start.2
  123.9 2.9 %collective-permute-done.2.next_ref = bf16[4,128,128]{2,1,0:T(8,128)(2,1)S(1)} collective-permute-done((bf16[4,128,128]{2,1,0:T(8,128)(2,1)S(1)}, bf16[4,128,128]{2,1,0:T(8,128)(2,1)S(1)}, u32[]{:S(2)}, u32[]{:S(2)}) %collective-permute-start.2) | collective-permute-done | bytes 131104 | tf_op jit(solution)/shard_map/ppermute | solution.py:414
  126.8 0.7 copy-done.2
  127.5 2.4 %shard_map.100 = (bf16[512,512]{1,0:T(8,128)(2,1)S(1)}, bf16[512,512]{1,0:T(8,128)(2,1)S(1)}) custom-call(bf16[4,128,128]{2,1,0:T(8,128)(2,1)} %copy-done.2, bf16[4,128,128]{2,1,0:T(8,128)(2,1)} %bitcast.17), custom_call_target="tpu_custom_call" | custom-call | flops 400000000 | bytes 2000000 | tf_op jit(solution)/shard_map/pallas_call | solution.py:28
  129.9 30.9 %all-to-all-done.2.r_ref = bf16[64,2,8,768]{3,2,1,0:T(8,128)(2,1)S(1)} async-done(((bf16[64,2,8,768]{3,2,1,0:T(8,128)(2,1)}), bf16[64,2,8,768]{3,2,1,0:T(8,128)(2,1)S(1)}, u32[]{:S(2)}, u32[]{:S(2)}) %all-to-all-start.2) | async-done | bytes 1572896 | tf_op jit(solution)/shard_map/all_to_all | solution.py:396
  160.8 1.6 shard_map.101
  162.4 1.4 collective-permute-start.3
  163.8 6.4 %all-to-all-start.3 = ((bf16[64,8,768]{2,1,0:T(8,128)(2,1)}), bf16[64,8,768]{2,1,0:T(8,128)(2,1)S(1)}, u32[]{:S(2)}, u32[]{:S(2)}) async-start(bf16[64,8,768]{2,1,0:T(8,128)(2,1)} %get-tuple-element.23), calls=%async_computation.3 | async-start | bytes 1572864 | tf_op jit(solution)/shard_map/all_to_all | solution.py:396
  170.2 12.9 %collective-permute-done.3.r_ref = bf16[64,8,768]{2,1,0:T(8,128)(2,1)S(1)} collective-permute-done((bf16[64,8,768]{2,1,0:T(8,128)(2,1)}, bf16[64,8,768]{2,1,0:T(8,128)(2,1)S(1)}, u32[]{:S(2)}, u32[]{:S(2)}) %collective-permute-start.3) | collective-permute-done | bytes 786464 | tf_op jit(solution)/shard_map/ppermute | solution.py:411
  183.0 1.0 shard_map.103.value_ref
  184.1 0.9 copy-done
  185.0 8.2 %all-to-all-done.3.other_ref = bf16[64,8,768]{2,1,0:T(8,128)(2,1)S(1)} async-done(((bf16[64,8,768]{2,1,0:T(8,128)(2,1)}), bf16[64,8,768]{2,1,0:T(8,128)(2,1)S(1)}, u32[]{:S(2)}, u32[]{:S(2)}) %all-to-all-start.3) | async-done | bytes 786464 | tf_op jit(solution)/shard_map/all_to_all | solution.py:396
  193.2 1.3 collective-permute-start.5
  194.5 6.5 %all-to-all-start.4 = ((bf16[64,8,768]{2,1,0:T(8,128)(2,1)}), bf16[64,8,768]{2,1,0:T(8,128)(2,1)S(1)}, u32[]{:S(2)}, u32[]{:S(2)}) async-start(bf16[64,8,768]{2,1,0:T(8,128)(2,1)} %shard_map.104), calls=%async_computation.4 | async-start | bytes 1572864 | tf_op jit(solution)/shard_map/all_to_all | solution.py:396
  201.0 12.1 %collective-permute-done.5.across_ref = bf16[64,8,768]{2,1,0:T(8,128)(2,1)S(1)} collective-permute-done((bf16[64,8,768]{2,1,0:T(8,128)(2,1)S(1)}, bf16[64,8,768]{2,1,0:T(8,128)(2,1)S(1)}, u32[]{:S(2)}, u32[]{:S(2)}) %collective-permute-start.5) | collective-permute-done | bytes 786464 | tf_op jit(solution)/shard_map/ppermute | solution.py:411
  213.1 6.7 %shard_map.102 = (bf16[256,1536]{1,0:T(8,128)(2,1)S(1)}, bf16[256,1536]{1,0:T(8,128)(2,1)S(1)}) custom-call(bf16[512,1536]{1,0:T(8,128)(2,1)} %collective-permute-done.4.x_ref, bf16[64,8,768]{2,1,0:T(8,128)(2,1)S(1)} %collective-permute-done.5.across_ref, f32[1,1536]{1,0:T(1,128)} %channel_ref.3, bf16[4,384,1024]{2,1,0:T(8,128)(2,1)} %bitcast.9, ...), custom_call_target="tpu_custom_call" | custom-call | flops 20000000000 | bytes 10000000 | tf_op jit(solution)/shard_map/pallas_call | solution.py:28
  219.8 4.1 %all-to-all-done.4.across_ref = bf16[64,8,768]{2,1,0:T(8,128)(2,1)S(1)} async-done(((bf16[64,8,768]{2,1,0:T(8,128)(2,1)}), bf16[64,8,768]{2,1,0:T(8,128)(2,1)S(1)}, u32[]{:S(2)}, u32[]{:S(2)}) %all-to-all-start.4) | async-done | bytes 786464 | tf_op jit(solution)/shard_map/all_to_all | solution.py:396
  223.9 7.3 %shard_map.105 = bf16[512,1536]{1,0:T(8,128)(2,1)} custom-call(bf16[256,1536]{1,0:T(8,128)(2,1)S(1)} %get-tuple-element.24.x_ref, bf16[64,8,768]{2,1,0:T(8,128)(2,1)S(1)} %all-to-all-done.4.across_ref, f32[1,1536]{1,0:T(1,128)} %channel_ref.3, bf16[4,384,1024]{2,1,0:T(8,128)(2,1)} %bitcast.10, bf16[4,1024,384]{2,1,0:T(8,128)(2,1)} %bitcast.13, ...), custom_call_target="tpu_custom_call" | custom-call | flops 3000000000 | bytes 11000000 | tf_op jit(solution)/shard_map/pallas_call | solution.py:28
  (9 shorter events, 0.0 us)
Async XLA Ops:
  4.0 52.8 %all-to-all-start = ((bf16[64,2,4,1536]{3,2,1,0:T(4,128)(2,1)}), bf16[64,2,4,1536]{3,2,1,0:T(4,128)(2,1)S(1)}, u32[]{:S(2)}, u32[]{:S(2)}) async-start(bf16[64,2,4,1536]{3,2,1,0:T(4,128)(2,1)} %shard_map.97), calls=%async_computation | async-start | bytes 3145728 | tf_op jit(solution)/shard_map/all_to_all | solution.py:396
  58.8 9.0 %copy-start.3 = (f32[1,1536]{1,0:T(1,128)S(1)}, f32[1,1536]{1,0:T(1,128)}, u32[]{:S(2)}) copy-start(f32[1,1536]{1,0:T(1,128)} %gain_ref.3) | copy-start | bytes 18436
  58.9 45.9 %all-to-all-start.1 = ((bf16[64,2,4,1536]{3,2,1,0:T(4,128)(2,1)}), bf16[64,2,4,1536]{3,2,1,0:T(4,128)(2,1)S(1)}, u32[]{:S(2)}, u32[]{:S(2)}) async-start(bf16[64,2,4,1536]{3,2,1,0:T(4,128)(2,1)} %shard_map.98), calls=%async_computation.1 | async-start | bytes 3145728 | tf_op jit(solution)/shard_map/all_to_all | solution.py:396
  65.0 8.4 %collective-permute-start.1 = (bf16[2,256,256]{2,1,0:T(8,128)(2,1)}, bf16[2,256,256]{2,1,0:T(8,128)(2,1)S(1)}, u32[]{:S(2)}, u32[]{:S(2)}) collective-permute-start(bf16[2,256,256]{2,1,0:T(8,128)(2,1)} %bitcast.3.factor_ref), channel_id=1, source_target_pairs={{64,0},{128,64},{192,128},{0,192},{65,1},{129,65},{193,129},{1,193... | collective-permute-start | bytes 786440 | tf_op jit(solution)/shard_map/ppermute | solution.py:414
  67.8 5.6 %collective-permute-start = (f32[1,1536]{1,0:T(1,128)S(1)}, f32[1,1536]{1,0:T(1,128)S(1)}, u32[]{:S(2)}, u32[]{:S(2)}) collective-permute-start(f32[1,1536]{1,0:T(1,128)S(1)} %copy-done.3), channel_id=1, source_target_pairs={{64,0},{128,64},{192,128},{0,192},{65,1},{129,65},{193,129},{1,193... | collective-permute-start | bytes 18440 | tf_op jit(solution)/shard_map/ppermute | solution.py:414
  114.7 7.7 %copy-start.1 = (bf16[1,4,128,128]{3,2,1,0:T(8,128)(2,1)S(1)}, bf16[1,4,128,128]{3,2,1,0:T(8,128)(2,1)}, u32[]{:S(2)}) copy-start(bf16[1,4,128,128]{3,2,1,0:T(8,128)(2,1)} %param.12) | copy-start | bytes 393220
  114.8 46.1 %all-to-all-start.2 = ((bf16[64,2,8,768]{3,2,1,0:T(8,128)(2,1)}), bf16[64,2,8,768]{3,2,1,0:T(8,128)(2,1)S(1)}, u32[]{:S(2)}, u32[]{:S(2)}) async-start(bf16[64,2,8,768]{3,2,1,0:T(8,128)(2,1)} %get-tuple-element.19), calls=%async_computation.2 | async-start | bytes 3145728 | tf_op jit(solution)/shard_map/all_to_all | solution.py:396
  121.0 49.2 %collective-permute-start.4 = (bf16[512,1536]{1,0:T(8,128)(2,1)}, bf16[512,1536]{1,0:T(8,128)(2,1)}, u32[]{:S(2)}, u32[]{:S(2)}) collective-permute-start(bf16[512,1536]{1,0:T(8,128)(2,1)} %get-tuple-element.21), channel_id=1, source_target_pairs={{0,64},{64,128},{128,192},{192,0},{1,65},{65,129},{129,193},{193,1... | collective-permute-start | bytes 4718600 | tf_op jit(solution)/shard_map/ppermute | solution.py:411
  122.4 4.4 %collective-permute-start.2 = (bf16[4,128,128]{2,1,0:T(8,128)(2,1)S(1)}, bf16[4,128,128]{2,1,0:T(8,128)(2,1)S(1)}, u32[]{:S(2)}, u32[]{:S(2)}) collective-permute-start(bf16[4,128,128]{2,1,0:T(8,128)(2,1)S(1)} %bitcast.18), channel_id=1, source_target_pairs={{64,0},{128,64},{192,128},{0,192},{65,1},{129,65},{193,129},{1,193... | collective-permute-start | bytes 393224 | tf_op jit(solution)/shard_map/ppermute | solution.py:414
  126.8 0.7 copy-start.2
  162.4 20.6 %collective-permute-start.3 = (bf16[64,8,768]{2,1,0:T(8,128)(2,1)}, bf16[64,8,768]{2,1,0:T(8,128)(2,1)S(1)}, u32[]{:S(2)}, u32[]{:S(2)}) collective-permute-start(bf16[64,8,768]{2,1,0:T(8,128)(2,1)} %get-tuple-element.20), channel_id=1, source_target_pairs={{0,64},{64,128},{128,192},{192,0},{1,65},{65,129},{129,193},{193,1... | collective-permute-start | bytes 2359304 | tf_op jit(solution)/shard_map/ppermute | solution.py:411
  163.8 29.4 %all-to-all-start.3 = ((bf16[64,8,768]{2,1,0:T(8,128)(2,1)}), bf16[64,8,768]{2,1,0:T(8,128)(2,1)S(1)}, u32[]{:S(2)}, u32[]{:S(2)}) async-start(bf16[64,8,768]{2,1,0:T(8,128)(2,1)} %get-tuple-element.23), calls=%async_computation.3 | async-start | bytes 1572864 | tf_op jit(solution)/shard_map/all_to_all | solution.py:396
  184.1 0.9 copy-start
  193.2 19.9 %collective-permute-start.5 = (bf16[64,8,768]{2,1,0:T(8,128)(2,1)S(1)}, bf16[64,8,768]{2,1,0:T(8,128)(2,1)S(1)}, u32[]{:S(2)}, u32[]{:S(2)}) collective-permute-start(bf16[64,8,768]{2,1,0:T(8,128)(2,1)S(1)} %all-to-all-done.3.other_ref), channel_id=1, source_target_pairs={{0,64},{64,128},{128,192},{192,0},{1,65},{65,129},{129,193},{193,1... | collective-permute-start | bytes 2359304 | tf_op jit(solution)/shard_map/ppermute | solution.py:411
  194.5 29.5 %all-to-all-start.4 = ((bf16[64,8,768]{2,1,0:T(8,128)(2,1)}), bf16[64,8,768]{2,1,0:T(8,128)(2,1)S(1)}, u32[]{:S(2)}, u32[]{:S(2)}) async-start(bf16[64,8,768]{2,1,0:T(8,128)(2,1)} %shard_map.104), calls=%async_computation.4 | async-start | bytes 1572864 | tf_op jit(solution)/shard_map/all_to_all | solution.py:396

commit v10 on v9

--- a/solution.py
+++ b/solution.py
@@ -80,8 +80,8 @@
     return jnp.where(hit(r, c), 1.0, 0.0).astype(BF)
 
 
-def offsets_of(rows, c):
-    return rows.reshape(DEV, 4, -1)[:, 2 * c : 2 * c + 2].reshape(BLK // 2, -1)
+def part_of(c):
+    return slice(c * (BLK // 2), (c + 1) * (BLK // 2))
 
 
 def normalize(values, gain):
@@ -102,7 +102,8 @@
         copies.wait(loads[3 * b], loads[1], loads[2])
         normed = normalize(x_buf[rows[b], :].astype(F32), gain_buf[...])
         mixed = dot(factor_buf[b], normed).astype(BF)
-        out_buf[:, b] = mixed.reshape(DEV, 4, D)
+        for c in range(2):
+            out_buf[:, b, 2 * c : 2 * c + 2] = mixed[part_of(c)].reshape(DEV, 2, D)
         copies.start(out_buf.at[:, b], out_ref.at[:, b])
     copies.wait()
 
@@ -268,7 +269,9 @@
         def store(g, part, value):
             first_buf[rows[b], part] = value
 
-        residual = x_ref[rows[b], :].astype(F32) + across_ref[:, b].reshape(BLK, D).astype(F32)
+        across = [across_ref[:, b, 2 * c : 2 * c + 2].reshape(BLK // 2, D) for c in range(2)]
+        across = jnp.concatenate(across, axis=0).astype(F32)
+        residual = x_ref[rows[b], :].astype(F32) + across
         channel_rows(residual, channel_ref[...], up, down, store)
         if b == 0:
             copies.wait(*late)
@@ -279,7 +282,7 @@
         mixed.append(dot(factor_buf[b], normalize(entering.astype(F32), gain_buf[...])).astype(BF))
     for c in range(2):
         for b in range(2):
-            rows_c = mixed[b].reshape(DEV, 4, D)[:, 2 * c : 2 * c + 2]
+            rows_c = mixed[b][part_of(c)].reshape(DEV, 2, D)
             for h in range(2):
                 first_row = 4 * h + 2 * b
                 half = slice(h * HALF, (h + 1) * HALF)
@@ -325,7 +328,7 @@
     weights = weight_loads(copies, up_ref, down_ref, up_buf, down_buf)
 
     def rows_of(c):
-        picked = [offsets_of(x_buf[b * BLK : (b + 1) * BLK, :], c) for b in range(2)]
+        picked = [x_buf[b * BLK : (b + 1) * BLK, :][part_of(c)] for b in range(2)]
         return jnp.concatenate(picked, axis=0)
 
     def store(g, part, value):
@@ -355,14 +358,17 @@
     copies = Copies(sems)
     loads = [copies.start(channel_ref, channel_buf)]
     weights = weight_loads(copies, up_ref, down_ref, up_buf, down_buf)
+    rows = BLK // 2
 
     def store(g, part, value):
+        if g == 0:
+            for b in range(2):
+                target = out_ref.at[pl.ds(b * BLK, rows)]
+                copies.start(other_ref.at[pl.ds(b * rows, rows)], target)
+        out_buf[:, part] = value
         for b in range(2):
-            rows = slice(b * (BLK // 2), (b + 1) * (BLK // 2))
-            both = [v.reshape(DEV, 2, WIDTH) for v in (other_ref[rows, part], value[rows])]
-            joined = jnp.concatenate(both, axis=1).reshape(BLK, WIDTH)
-            out_buf[b * BLK : (b + 1) * BLK, part] = joined
-        copies.start(out_buf.at[:, columns_of(g)], out_ref.at[:, columns_of(g)])
+            target = out_ref.at[pl.ds(b * BLK + rows, rows), columns_of(g)]
+            copies.start(out_buf.at[pl.ds(b * rows, rows), columns_of(g)], target)
 
     last_rows(
         copies, loads, lambda: x_ref[...].astype(F32), across_ref, channel_buf, weights, store
@@ -396,16 +402,30 @@
     return lax.all_to_all(hbm(value), "seq", split_axis=0, concat_axis=0, tiled=True)
 
 
+def redistributed(cross):
+    device, count = lax.axis_index("seq"), lax.axis_size("seq")
+    half = count // 2
+    lower = device < half
+    first, second = cross[:2], cross[2:]
+    to_even = [(s, 2 * s) if s < half else (s, 2 * (s - half) + 1) for s in range(count)]
+    to_odd = [(s, 2 * s + 1) if s < half else (s, 2 * (s - half)) for s in range(count)]
+    straight = lax.ppermute(jnp.where(lower, first, second), "seq", to_even)
+    turned = lax.ppermute(jnp.where(lower, second, first), "seq", to_odd)
+    even = device % 2 == 0
+    part0 = jnp.where(even, straight, turned)
+    part1 = jnp.where(even, turned, straight)
+    return jnp.concatenate([part0, part1], axis=0)
+
+
 def per_device(arriving, queued, norm_gain, block_factor, cross_factor, channel_gain, up, down):
     section = lax.axis_index("section")
     count = lax.axis_size("section")
     flags = jnp.full((1,), section == count - 1, jnp.int32)
     x = arriving[0]
     factor, cross, up, down = block_factor[0], cross_factor[0], up[0], down[0]
+    cross = hbm(redistributed(cross))
     held_x, held_factor, held_gain = hbm(x), hbm(factor), hbm(norm_gain)
-    cross, up, down, queued, channel_gain = (
-        hbm(v) for v in (cross, up, down, queued, channel_gain)
-    )
+    up, down, queued, channel_gain = (hbm(v) for v in (up, down, queued, channel_gain))
 
     def ahead(value):
         return lax.ppermute(value, "section", [(s, (s + 1) % count) for s in range(count)])
@@ -526,7 +546,7 @@
         final_kernel,
         sequence,
         [kept, across1, channel_gain, up, down, other],
-        [*bufs, buf(sequence), sems(13)],
+        [*bufs, buf(part_rows), sems(19)],
         (3_000_000_000, 11_000_000, 1_000_000),
         near=(0, 1, 5),
     )

time: 232 us -> 238 us (1.026)
  starting transfers between devices: 47.1 us -> 58.5 us
  waiting for transfers between devices: 144 us -> 140 us
    all_to_all x5, waiting for transfers between devices: 113 us -> 79 us  [exchange(): lax.all_to_all(hbm(value), 'seq', split_axis=0, concat_axis=0, tiled=True)]
    ppermute x0 -> x2, waiting for transfers between devices: none -> 29.3 us  [the longest x1 27.8 us: redistributed(): straight = lax.ppermute(jnp.where(lower, first, second), 'seq', to_even)]
    ppermute x0 -> x2, starting transfers between devices: none -> 5.71 us  [the longest x1 3.54 us: redistributed(): straight = lax.ppermute(jnp.where(lower, first, second), 'seq', to_even)]
    all_to_all x5, starting transfers between devices: 38.3 us -> 43.7 us  [exchange(): lax.all_to_all(hbm(value), 'seq', split_axis=0, concat_axis=0, tiled=True)]
  transfers between devices with their start and end apart: 11 -> 13, of which waited for: 9 -> 11; matrix products, arithmetic and copies ran while one was open for 0% -> 0% of each run, Pallas kernels for 6% -> 6%
where the time goes in v10:
time: 238 us
  waiting for transfers between devices  140 us (59%)
  starting transfers between devices  58.5 us (25%)
  Pallas kernels  36.3 us (15%)
    all_to_all x5, waiting for transfers between devices, exchange(): lax.all_to_all(hbm(value), 'seq', split_axis=0, concat_axis=0, tiled=True)  79 us
    all_to_all x5, starting transfers between devices, exchange(): lax.all_to_all(hbm(value), 'seq', split_axis=0, concat_axis=0, tiled=True)  43.7 us
    pallas_call x10, Pallas kernels, call(): pl.pallas_call(kernel, out_shape=outs, in_specs=scalars + [nearby if n in...  36.3 us
    ppermute x1, waiting for transfers between devices, redistributed(): straight = lax.ppermute(jnp.where(lower, first, second), 'seq', to_even)  27.8 us
    ppermute x3, waiting for transfers between devices, ahead(): lax.ppermute(value, 'section', [(s, (s + 1) % count) for s in range(count)])  25 us
    ppermute x3, waiting for transfers between devices, behind(): lax.ppermute(value, 'section', [((s + 1) % count, s) for s in range(count)])  6.3 us
    ppermute x3, starting transfers between devices, behind(): lax.ppermute(value, 'section', [((s + 1) % count, s) for s in range(count)])  5.04 us
  transfers between devices with their start and end apart: 13, of which 11 were waited for; matrix products, arithmetic and copies ran while one was open for 0% of the time, Pallas kernels for 6%

profile of v10, /device:TPU:1, one launch (start us, length us, event | category | flops | bytes accessed | tf_op | source)
XLA Modules:
  0.0 237.5 jit_solution(14354553073502669563)
XLA Ops:
  0.6 3.4 %shard_map.97 = bf16[64,2,4,1536]{3,2,1,0:T(4,128)(2,1)} custom-call(bf16[512,1536]{1,0:T(8,128)(2,1)} %bitcast.17, f32[1,1536]{1,0:T(1,128)} %gain_ref.3, bf16[2,256,256]{2,1,0:T(8,128)(2,1)} %bitcast.4.factor_ref), custom_call_target="tpu_custom_call" | custom-call | flops 2000000000 | bytes 4000000 | tf_op jit(solution)/shard_map/pallas_call | solution.py:28
  4.1 13.1 %all-to-all-start = ((bf16[64,2,4,1536]{3,2,1,0:T(4,128)(2,1)}), bf16[64,2,4,1536]{3,2,1,0:T(4,128)(2,1)S(1)}, u32[]{:S(2)}, u32[]{:S(2)}) async-start(bf16[64,2,4,1536]{3,2,1,0:T(4,128)(2,1)} %shard_map.97), calls=%async_computation | async-start | bytes 3145728 | tf_op jit(solution)/shard_map/all_to_all | solution.py:402
  17.3 3.5 %collective-permute-start = (bf16[2,128,128]{2,1,0:T(8,128)(2,1)S(1)}, bf16[2,128,128]{2,1,0:T(8,128)(2,1)S(1)}, u32[]{:S(2)}, u32[]{:S(2)}) collective-permute-start(bf16[2,128,128]{2,1,0:T(8,128)(2,1)S(1)} %get-tuple-element.30), channel_id=1, source_target_pairs={{0,0},{1,2},{2,4},{3,6},{4,8},{5,10},{6,12},{7,14},{8,16},{9,18},{... | collective-permute-start | bytes 196616 | tf_op jit(solution)/shard_map/ppermute | solution.py:412
  20.8 2.2 collective-permute-start.1
  23.0 27.8 %collective-permute-done = bf16[2,128,128]{2,1,0:T(8,128)(2,1)S(1)} collective-permute-done((bf16[2,128,128]{2,1,0:T(8,128)(2,1)S(1)}, bf16[2,128,128]{2,1,0:T(8,128)(2,1)S(1)}, u32[]{:S(2)}, u32[]{:S(2)}) %collective-permute-start) | collective-permute-done | bytes 65568 | tf_op jit(solution)/shard_map/ppermute | solution.py:412
  50.8 1.5 collective-permute-done.1
  52.9 1.6 shard_map.96.spread_ref
  54.6 3.9 %all-to-all-done.r_ref = bf16[64,2,4,1536]{3,2,1,0:T(4,128)(2,1)S(1)} async-done(((bf16[64,2,4,1536]{3,2,1,0:T(4,128)(2,1)}), bf16[64,2,4,1536]{3,2,1,0:T(4,128)(2,1)S(1)}, u32[]{:S(2)}, u32[]{:S(2)}) %all-to-all-start) | async-done | bytes 1572896 | tf_op jit(solution)/shard_map/all_to_all | solution.py:402
  58.5 2.0 shard_map.98
  60.5 11.4 %all-to-all-start.1 = ((bf16[64,2,4,1536]{3,2,1,0:T(4,128)(2,1)}), bf16[64,2,4,1536]{3,2,1,0:T(4,128)(2,1)S(1)}, u32[]{:S(2)}, u32[]{:S(2)}) async-start(bf16[64,2,4,1536]{3,2,1,0:T(4,128)(2,1)} %shard_map.98), calls=%async_computation.1 | async-start | bytes 3145728 | tf_op jit(solution)/shard_map/all_to_all | solution.py:402
  71.9 2.8 %collective-permute-start.3 = (bf16[2,256,256]{2,1,0:T(8,128)(2,1)}, bf16[2,256,256]{2,1,0:T(8,128)(2,1)S(1)}, u32[]{:S(2)}, u32[]{:S(2)}) collective-permute-start(bf16[2,256,256]{2,1,0:T(8,128)(2,1)} %bitcast.4.factor_ref), channel_id=1, source_target_pairs={{64,0},{128,64},{192,128},{0,192},{65,1},{129,65},{193,129},{1,193... | collective-permute-start | bytes 786440 | tf_op jit(solution)/shard_map/ppermute | solution.py:434
  75.2 1.4 shard_map.95
  76.7 3.7 %collective-permute-done.2.gain_ref = f32[1,1536]{1,0:T(1,128)S(1)} collective-permute-done((f32[1,1536]{1,0:T(1,128)S(1)}, f32[1,1536]{1,0:T(1,128)S(1)}, u32[]{:S(2)}, u32[]{:S(2)}) %collective-permute-start.2) | collective-permute-done | bytes 6176 | tf_op jit(solution)/shard_map/ppermute | solution.py:434
  80.3 31.4 %all-to-all-done.1.across_ref = bf16[64,2,4,1536]{3,2,1,0:T(4,128)(2,1)S(1)} async-done(((bf16[64,2,4,1536]{3,2,1,0:T(4,128)(2,1)}), bf16[64,2,4,1536]{3,2,1,0:T(4,128)(2,1)S(1)}, u32[]{:S(2)}, u32[]{:S(2)}) %all-to-all-start.1) | async-done | bytes 1572896 | tf_op jit(solution)/shard_map/all_to_all | solution.py:402
  111.7 10.3 %shard_map.99 = (bf16[512,1536]{1,0:T(8,128)(2,1)}, bf16[512,1536]{1,0:T(8,128)(2,1)}, bf16[64,2,8,768]{3,2,1,0:T(8,128)(2,1)}) custom-call(s32[1]{0:T(128)} %bitcast.flag_ref, bf16[512,1536]{1,0:T(8,128)(2,1)S(1)} %get-tuple-element.15.x_ref, bf16[64,2,4,1536]{3,2,1,0:T(4,128)(2,1)S(1)} %all-to-all-done.1.across_ref, ...), custom_call_target="tpu_custom_call" | custom-call | flops 7000000000 | bytes 18000000 | tf_op jit(solution)/shard_map/pallas_call | solution.py:28
  122.1 6.3 %all-to-all-start.2 = ((bf16[64,2,8,768]{3,2,1,0:T(8,128)(2,1)}), bf16[64,2,8,768]{3,2,1,0:T(8,128)(2,1)S(1)}, u32[]{:S(2)}, u32[]{:S(2)}) async-start(bf16[64,2,8,768]{3,2,1,0:T(8,128)(2,1)} %get-tuple-element.19), calls=%async_computation.2 | async-start | bytes 3145728 | tf_op jit(solution)/shard_map/all_to_all | solution.py:402
  128.3 1.4 collective-permute-start.6
  129.7 1.8 collective-permute-start.4
  131.5 2.6 %collective-permute-done.4.next_ref = bf16[4,128,128]{2,1,0:T(8,128)(2,1)S(1)} collective-permute-done((bf16[4,128,128]{2,1,0:T(8,128)(2,1)S(1)}, bf16[4,128,128]{2,1,0:T(8,128)(2,1)S(1)}, u32[]{:S(2)}, u32[]{:S(2)}) %collective-permute-start.4) | collective-permute-done | bytes 131104 | tf_op jit(solution)/shard_map/ppermute | solution.py:434
  134.8 2.4 %shard_map.100 = (bf16[512,512]{1,0:T(8,128)(2,1)S(1)}, bf16[512,512]{1,0:T(8,128)(2,1)S(1)}) custom-call(bf16[4,128,128]{2,1,0:T(8,128)(2,1)} %copy-done.3, bf16[4,128,128]{2,1,0:T(8,128)(2,1)} %pad_maximum_fusion.cross_ref.own_ref), custom_call_target="tpu_custom_call" | custom-call | flops 400000000 | bytes 2000000 | tf_op jit(solution)/shard_map/pallas_call | solution.py:28
  137.2 30.9 %all-to-all-done.2.r_ref = bf16[64,2,8,768]{3,2,1,0:T(8,128)(2,1)S(1)} async-done(((bf16[64,2,8,768]{3,2,1,0:T(8,128)(2,1)}), bf16[64,2,8,768]{3,2,1,0:T(8,128)(2,1)S(1)}, u32[]{:S(2)}, u32[]{:S(2)}) %all-to-all-start.2) | async-done | bytes 1572896 | tf_op jit(solution)/shard_map/all_to_all | solution.py:402
  168.1 1.5 shard_map.101
  169.7 1.4 collective-permute-start.5
  171.1 6.4 %all-to-all-start.3 = ((bf16[64,8,768]{2,1,0:T(8,128)(2,1)}), bf16[64,8,768]{2,1,0:T(8,128)(2,1)S(1)}, u32[]{:S(2)}, u32[]{:S(2)}) async-start(bf16[64,8,768]{2,1,0:T(8,128)(2,1)} %get-tuple-element.23), calls=%async_computation.3 | async-start | bytes 1572864 | tf_op jit(solution)/shard_map/all_to_all | solution.py:402
  177.5 12.9 %collective-permute-done.5.r_ref = bf16[64,8,768]{2,1,0:T(8,128)(2,1)S(1)} collective-permute-done((bf16[64,8,768]{2,1,0:T(8,128)(2,1)}, bf16[64,8,768]{2,1,0:T(8,128)(2,1)S(1)}, u32[]{:S(2)}, u32[]{:S(2)}) %collective-permute-start.5) | collective-permute-done | bytes 786464 | tf_op jit(solution)/shard_map/ppermute | solution.py:431
  192.2 8.2 %all-to-all-done.3.other_ref = bf16[64,8,768]{2,1,0:T(8,128)(2,1)S(1)} async-done(((bf16[64,8,768]{2,1,0:T(8,128)(2,1)}), bf16[64,8,768]{2,1,0:T(8,128)(2,1)S(1)}, u32[]{:S(2)}, u32[]{:S(2)}) %all-to-all-start.3) | async-done | bytes 786464 | tf_op jit(solution)/shard_map/all_to_all | solution.py:402
  200.4 1.3 collective-permute-start.7
  201.7 6.5 %all-to-all-start.4 = ((bf16[64,8,768]{2,1,0:T(8,128)(2,1)}), bf16[64,8,768]{2,1,0:T(8,128)(2,1)S(1)}, u32[]{:S(2)}, u32[]{:S(2)}) async-start(bf16[64,8,768]{2,1,0:T(8,128)(2,1)} %shard_map.104), calls=%async_computation.4 | async-start | bytes 1572864 | tf_op jit(solution)/shard_map/all_to_all | solution.py:402
  208.2 12.1 %collective-permute-done.7.across_ref = bf16[64,8,768]{2,1,0:T(8,128)(2,1)S(1)} collective-permute-done((bf16[64,8,768]{2,1,0:T(8,128)(2,1)S(1)}, bf16[64,8,768]{2,1,0:T(8,128)(2,1)S(1)}, u32[]{:S(2)}, u32[]{:S(2)}) %collective-permute-start.7) | collective-permute-done | bytes 786464 | tf_op jit(solution)/shard_map/ppermute | solution.py:431
  220.4 6.3 %shard_map.102 = (bf16[256,1536]{1,0:T(8,128)(2,1)S(1)}, bf16[256,1536]{1,0:T(8,128)(2,1)S(1)}) custom-call(bf16[512,1536]{1,0:T(8,128)(2,1)} %collective-permute-done.6.x_ref, bf16[64,8,768]{2,1,0:T(8,128)(2,1)S(1)} %collective-permute-done.7.across_ref, f32[1,1536]{1,0:T(1,128)} %channel_ref.3, bf16[4,384,1024]{2,1,0:T(8,128)(2,1)} %bitcast.12, ...), custom_call_target="tpu_custom_call" | custom-call | flops 20000000000 | bytes 10000000 | tf_op jit(solution)/shard_map/pallas_call | solution.py:28
  226.7 4.5 %all-to-all-done.4.across_ref = bf16[64,8,768]{2,1,0:T(8,128)(2,1)S(1)} async-done(((bf16[64,8,768]{2,1,0:T(8,128)(2,1)}), bf16[64,8,768]{2,1,0:T(8,128)(2,1)S(1)}, u32[]{:S(2)}, u32[]{:S(2)}) %all-to-all-start.4) | async-done | bytes 786464 | tf_op jit(solution)/shard_map/all_to_all | solution.py:402
  231.2 6.1 %shard_map.105 = bf16[512,1536]{1,0:T(8,128)(2,1)} custom-call(bf16[256,1536]{1,0:T(8,128)(2,1)S(1)} %get-tuple-element.24.x_ref, bf16[64,8,768]{2,1,0:T(8,128)(2,1)S(1)} %all-to-all-done.4.across_ref, f32[1,1536]{1,0:T(1,128)} %channel_ref.3, bf16[4,384,1024]{2,1,0:T(8,128)(2,1)} %bitcast.13, bf16[4,1024,384]{2,1,0:T(8,128)(2,1)} %bitcast.16, ...), custom_call_target="tpu_custom_call" | custom-call | flops 3000000000 | bytes 11000000 | tf_op jit(solution)/shard_map/pallas_call | solution.py:28
  (18 shorter events, 3.7 us)
Async XLA Ops:
  4.1 13.2 %copy-start.1 = (bf16[1,4,128,128]{3,2,1,0:T(8,128)(2,1)S(1)}, bf16[1,4,128,128]{3,2,1,0:T(8,128)(2,1)}, u32[]{:S(2)}) copy-start(bf16[1,4,128,128]{3,2,1,0:T(8,128)(2,1)} %param.12) | copy-start | bytes 393220
  4.1 54.4 %all-to-all-start = ((bf16[64,2,4,1536]{3,2,1,0:T(4,128)(2,1)}), bf16[64,2,4,1536]{3,2,1,0:T(4,128)(2,1)S(1)}, u32[]{:S(2)}, u32[]{:S(2)}) async-start(bf16[64,2,4,1536]{3,2,1,0:T(4,128)(2,1)} %shard_map.97), calls=%async_computation | async-start | bytes 3145728 | tf_op jit(solution)/shard_map/all_to_all | solution.py:402
  17.3 33.5 %collective-permute-start = (bf16[2,128,128]{2,1,0:T(8,128)(2,1)S(1)}, bf16[2,128,128]{2,1,0:T(8,128)(2,1)S(1)}, u32[]{:S(2)}, u32[]{:S(2)}) collective-permute-start(bf16[2,128,128]{2,1,0:T(8,128)(2,1)S(1)} %get-tuple-element.30), channel_id=1, source_target_pairs={{0,0},{1,2},{2,4},{3,6},{4,8},{5,10},{6,12},{7,14},{8,16},{9,18},{... | collective-permute-start | bytes 196616 | tf_op jit(solution)/shard_map/ppermute | solution.py:412
  20.8 31.4 %collective-permute-start.1 = (bf16[2,128,128]{2,1,0:T(8,128)(2,1)S(1)}, bf16[2,128,128]{2,1,0:T(8,128)(2,1)S(1)}, u32[]{:S(2)}, u32[]{:S(2)}) collective-permute-start(bf16[2,128,128]{2,1,0:T(8,128)(2,1)S(1)} %get-tuple-element.31), channel_id=1, source_target_pairs={{0,1},{1,3},{2,5},{3,7},{4,9},{5,11},{6,13},{7,15},{8,17},{9,19},{... | collective-permute-start | bytes 196616 | tf_op jit(solution)/shard_map/ppermute | solution.py:413
  60.5 14.2 %copy-start.4 = (f32[1,1536]{1,0:T(1,128)S(1)}, f32[1,1536]{1,0:T(1,128)}, u32[]{:S(2)}) copy-start(f32[1,1536]{1,0:T(1,128)} %gain_ref.3) | copy-start | bytes 18436
  60.5 51.2 %all-to-all-start.1 = ((bf16[64,2,4,1536]{3,2,1,0:T(4,128)(2,1)}), bf16[64,2,4,1536]{3,2,1,0:T(4,128)(2,1)S(1)}, u32[]{:S(2)}, u32[]{:S(2)}) async-start(bf16[64,2,4,1536]{3,2,1,0:T(4,128)(2,1)} %shard_map.98), calls=%async_computation.1 | async-start | bytes 3145728 | tf_op jit(solution)/shard_map/all_to_all | solution.py:402
  71.9 8.4 %collective-permute-start.3 = (bf16[2,256,256]{2,1,0:T(8,128)(2,1)}, bf16[2,256,256]{2,1,0:T(8,128)(2,1)S(1)}, u32[]{:S(2)}, u32[]{:S(2)}) collective-permute-start(bf16[2,256,256]{2,1,0:T(8,128)(2,1)} %bitcast.4.factor_ref), channel_id=1, source_target_pairs={{64,0},{128,64},{192,128},{0,192},{65,1},{129,65},{193,129},{1,193... | collective-permute-start | bytes 786440 | tf_op jit(solution)/shard_map/ppermute | solution.py:434
  74.8 5.6 %collective-permute-start.2 = (f32[1,1536]{1,0:T(1,128)S(1)}, f32[1,1536]{1,0:T(1,128)S(1)}, u32[]{:S(2)}, u32[]{:S(2)}) collective-permute-start(f32[1,1536]{1,0:T(1,128)S(1)} %copy-done.4), channel_id=1, source_target_pairs={{64,0},{128,64},{192,128},{0,192},{65,1},{129,65},{193,129},{1,193... | collective-permute-start | bytes 18440 | tf_op jit(solution)/shard_map/ppermute | solution.py:434
  122.1 7.6 %copy-start.2 = (bf16[4,128,128]{2,1,0:T(8,128)(2,1)S(1)}, bf16[4,128,128]{2,1,0:T(8,128)(2,1)}, u32[]{:S(2)}) copy-start(bf16[4,128,128]{2,1,0:T(8,128)(2,1)} %pad_maximum_fusion.cross_ref.own_ref) | copy-start | bytes 393220
  122.1 46.1 %all-to-all-start.2 = ((bf16[64,2,8,768]{3,2,1,0:T(8,128)(2,1)}), bf16[64,2,8,768]{3,2,1,0:T(8,128)(2,1)S(1)}, u32[]{:S(2)}, u32[]{:S(2)}) async-start(bf16[64,2,8,768]{3,2,1,0:T(8,128)(2,1)} %get-tuple-element.19), calls=%async_computation.2 | async-start | bytes 3145728 | tf_op jit(solution)/shard_map/all_to_all | solution.py:402
  128.3 49.1 %collective-permute-start.6 = (bf16[512,1536]{1,0:T(8,128)(2,1)}, bf16[512,1536]{1,0:T(8,128)(2,1)}, u32[]{:S(2)}, u32[]{:S(2)}) collective-permute-start(bf16[512,1536]{1,0:T(8,128)(2,1)} %get-tuple-element.21), channel_id=1, source_target_pairs={{0,64},{64,128},{128,192},{192,0},{1,65},{65,129},{129,193},{193,1... | collective-permute-start | bytes 4718600 | tf_op jit(solution)/shard_map/ppermute | solution.py:431
  129.7 4.4 %collective-permute-start.4 = (bf16[4,128,128]{2,1,0:T(8,128)(2,1)S(1)}, bf16[4,128,128]{2,1,0:T(8,128)(2,1)S(1)}, u32[]{:S(2)}, u32[]{:S(2)}) collective-permute-start(bf16[4,128,128]{2,1,0:T(8,128)(2,1)S(1)} %copy-done.2), channel_id=1, source_target_pairs={{64,0},{128,64},{192,128},{0,192},{65,1},{129,65},{193,129},{1,193... | collective-permute-start | bytes 393224 | tf_op jit(solution)/shard_map/ppermute | solution.py:434
  134.1 0.7 copy-start.3
  169.7 20.6 %collective-permute-start.5 = (bf16[64,8,768]{2,1,0:T(8,128)(2,1)}, bf16[64,8,768]{2,1,0:T(8,128)(2,1)S(1)}, u32[]{:S(2)}, u32[]{:S(2)}) collective-permute-start(bf16[64,8,768]{2,1,0:T(8,128)(2,1)} %get-tuple-element.20), channel_id=1, source_target_pairs={{0,64},{64,128},{128,192},{192,0},{1,65},{65,129},{129,193},{193,1... | collective-permute-start | bytes 2359304 | tf_op jit(solution)/shard_map/ppermute | solution.py:431
  171.1 29.4 %all-to-all-start.3 = ((bf16[64,8,768]{2,1,0:T(8,128)(2,1)}), bf16[64,8,768]{2,1,0:T(8,128)(2,1)S(1)}, u32[]{:S(2)}, u32[]{:S(2)}) async-start(bf16[64,8,768]{2,1,0:T(8,128)(2,1)} %get-tuple-element.23), calls=%async_computation.3 | async-start | bytes 1572864 | tf_op jit(solution)/shard_map/all_to_all | solution.py:402
  191.4 0.9 copy-start
  200.4 19.9 %collective-permute-start.7 = (bf16[64,8,768]{2,1,0:T(8,128)(2,1)S(1)}, bf16[64,8,768]{2,1,0:T(8,128)(2,1)S(1)}, u32[]{:S(2)}, u32[]{:S(2)}) collective-permute-start(bf16[64,8,768]{2,1,0:T(8,128)(2,1)S(1)} %all-to-all-done.3.other_ref), channel_id=1, source_target_pairs={{0,64},{64,128},{128,192},{192,0},{1,65},{65,129},{129,193},{193,1... | collective-permute-start | bytes 2359304 | tf_op jit(solution)/shard_map/ppermute | solution.py:431
  201.7 29.5 %all-to-all-start.4 = ((bf16[64,8,768]{2,1,0:T(8,128)(2,1)}), bf16[64,8,768]{2,1,0:T(8,128)(2,1)S(1)}, u32[]{:S(2)}, u32[]{:S(2)}) async-start(bf16[64,8,768]{2,1,0:T(8,128)(2,1)} %shard_map.104), calls=%async_computation.4 | async-start | bytes 1572864 | tf_op jit(solution)/shard_map/all_to_all | solution.py:402

commit v11 on v9

--- a/solution.py
+++ b/solution.py
@@ -225,7 +225,7 @@
         copies.wait(loads[g][1])
         return down_buf[g]
 
-    return up, down, start
+    return up, down
 
 
 def middle_kernel(
@@ -253,20 +253,18 @@
 ):
     copies = Copies(sems)
     rows = [pl.ds(b * BLK, BLK) for b in range(2)]
-    up, down, start = weight_loads(copies, up_ref, down_ref, up_buf, down_buf)
-    for g in range(2, GROUPS):
-        start(g)
-    late = [
-        copies.start(gain_ref, gain_buf),
-        copies.start(factor_ref, factor_buf),
-        copies.start(queued_ref, queued_buf),
-    ]
+    up, down = weight_loads(copies, up_ref, down_ref, up_buf, down_buf)
+    late = []
     last = flag_ref[0] == 1
     mixed = []
     for b in range(2):
 
         def store(g, part, value):
             first_buf[rows[b], part] = value
+            if b == 0 and g == 1:
+                late.append(copies.start(gain_ref, gain_buf))
+                late.append(copies.start(factor_ref, factor_buf))
+                late.append(copies.start(queued_ref, queued_buf))
 
         residual = x_ref[rows[b], :].astype(F32) + across_ref[:, b].reshape(BLK, D).astype(F32)
         channel_rows(residual, channel_ref[...], up, down, store)
@@ -289,10 +287,8 @@
 
 
 def last_rows(copies, loads, residual_of, across_ref, channel_buf, weights, store):
-    up, down, start = weights
+    up, down = weights
     copies.wait(*loads)
-    start(2)
-    start(3)
     halves = [
         [
             across_ref[:, 4 * h + 2 * b : 4 * h + 2 * b + 2, :].reshape(BLK // 2, HALF)
@@ -356,13 +352,18 @@
     loads = [copies.start(channel_ref, channel_buf)]
     weights = weight_loads(copies, up_ref, down_ref, up_buf, down_buf)
 
+    def put(c, rows, part):
+        for b in range(2):
+            pairs = rows[b * (BLK // 2) : (b + 1) * (BLK // 2)].reshape(DEV // 2, 4, -1)
+            for d in range(2):
+                row = 4 * d + 2 * c
+                out_buf[b, :, row : row + 2, part] = pairs[:, 2 * d : 2 * d + 2]
+
     def store(g, part, value):
-        for b in range(2):
-            rows = slice(b * (BLK // 2), (b + 1) * (BLK // 2))
-            both = [v.reshape(DEV, 2, WIDTH) for v in (other_ref[rows, part], value[rows])]
-            joined = jnp.concatenate(both, axis=1).reshape(BLK, WIDTH)
-            out_buf[b * BLK : (b + 1) * BLK, part] = joined
-        copies.start(out_buf.at[:, columns_of(g)], out_ref.at[:, columns_of(g)])
+        put(0, other_ref[:, part], part)
+        put(1, value, part)
+        columns = columns_of(g)
+        copies.start(out_buf.at[:, :, :, columns], out_ref.at[:, :, :, columns])
 
     last_rows(
         copies, loads, lambda: x_ref[...].astype(F32), across_ref, channel_buf, weights, store
@@ -522,11 +523,12 @@
         (LONG, 10_000_000, 1_000_000),
         near=(1,),
     )
+    paired = shape(2, DEV // 2, 8, D)
     second = call(
         final_kernel,
-        sequence,
+        paired,
         [kept, across1, channel_gain, up, down, other],
-        [*bufs, buf(sequence), sems(13)],
+        [*bufs, buf(paired), sems(13)],
         (3_000_000_000, 11_000_000, 1_000_000),
         near=(0, 1, 5),
     )

time: 232 us -> 232 us (level)
  no operation moved by 1% of the time
where the time goes in v11:
time: 232 us; the launch traced here: 231 us
  waiting for transfers between devices  144 us (62%)
  starting transfers between devices  47.3 us (20%)
  Pallas kernels  36.9 us (16%)
    all_to_all x5, waiting for transfers between devices, exchange(): lax.all_to_all(hbm(value), 'seq', split_axis=0, concat_axis=0, tiled=True)  113 us
    all_to_all x5, starting transfers between devices, exchange(): lax.all_to_all(hbm(value), 'seq', split_axis=0, concat_axis=0, tiled=True)  38.3 us
    pallas_call x10, Pallas kernels, call(): pl.pallas_call(kernel, out_shape=outs, in_specs=scalars + [nearby if n in...  36.9 us
    ppermute x3, waiting for transfers between devices, ahead(): lax.ppermute(value, 'section', [(s, (s + 1) % count) for s in range(count)])  25 us
    ppermute x3, waiting for transfers between devices, behind(): lax.ppermute(value, 'section', [((s + 1) % count, s) for s in range(count)])  6.52 us
    ppermute x3, starting transfers between devices, behind(): lax.ppermute(value, 'section', [((s + 1) % count, s) for s in range(count)])  4.82 us
  transfers between devices with their start and end apart: 11, of which 9 were waited for; matrix products, arithmetic and copies ran while one was open for 0% of the time, Pallas kernels for 6%

profile of v11, /device:TPU:1, one launch (start us, length us, event | category | flops | bytes accessed | tf_op | source)
XLA Modules:
  0.0 231.1 jit_solution(11097194525236843848)
XLA Ops:
  0.6 3.4 %shard_map.97 = bf16[64,2,4,1536]{3,2,1,0:T(4,128)(2,1)} custom-call(bf16[512,1536]{1,0:T(8,128)(2,1)} %bitcast.14, f32[1,1536]{1,0:T(1,128)} %gain_ref.3, bf16[2,256,256]{2,1,0:T(8,128)(2,1)} %bitcast.3.factor_ref), custom_call_target="tpu_custom_call" | custom-call | flops 2000000000 | bytes 4000000 | tf_op jit(solution)/shard_map/pallas_call | solution.py:28
  4.0 13.0 %all-to-all-start = ((bf16[64,2,4,1536]{3,2,1,0:T(4,128)(2,1)}), bf16[64,2,4,1536]{3,2,1,0:T(4,128)(2,1)S(1)}, u32[]{:S(2)}, u32[]{:S(2)}) async-start(bf16[64,2,4,1536]{3,2,1,0:T(4,128)(2,1)} %shard_map.97), calls=%async_computation | async-start | bytes 3145728 | tf_op jit(solution)/shard_map/all_to_all | solution.py:397
  17.0 1.6 shard_map.96.spread_ref
  18.6 38.1 %all-to-all-done.r_ref = bf16[64,2,4,1536]{3,2,1,0:T(4,128)(2,1)S(1)} async-done(((bf16[64,2,4,1536]{3,2,1,0:T(4,128)(2,1)}), bf16[64,2,4,1536]{3,2,1,0:T(4,128)(2,1)S(1)}, u32[]{:S(2)}, u32[]{:S(2)}) %all-to-all-start) | async-done | bytes 1572896 | tf_op jit(solution)/shard_map/all_to_all | solution.py:397
  56.8 2.0 shard_map.98
  58.9 6.1 %all-to-all-start.1 = ((bf16[64,2,4,1536]{3,2,1,0:T(4,128)(2,1)}), bf16[64,2,4,1536]{3,2,1,0:T(4,128)(2,1)S(1)}, u32[]{:S(2)}, u32[]{:S(2)}) async-start(bf16[64,2,4,1536]{3,2,1,0:T(4,128)(2,1)} %shard_map.98), calls=%async_computation.1 | async-start | bytes 3145728 | tf_op jit(solution)/shard_map/all_to_all | solution.py:397
  65.0 2.8 %collective-permute-start.1 = (bf16[2,256,256]{2,1,0:T(8,128)(2,1)}, bf16[2,256,256]{2,1,0:T(8,128)(2,1)S(1)}, u32[]{:S(2)}, u32[]{:S(2)}) collective-permute-start(bf16[2,256,256]{2,1,0:T(8,128)(2,1)} %bitcast.3.factor_ref), channel_id=1, source_target_pairs={{64,0},{128,64},{192,128},{0,192},{65,1},{129,65},{193,129},{1,193... | collective-permute-start | bytes 786440 | tf_op jit(solution)/shard_map/ppermute | solution.py:415
  67.8 0.5 collective-permute-start
  68.3 1.4 shard_map.95
  69.7 3.7 %collective-permute-done.gain_ref = f32[1,1536]{1,0:T(1,128)S(1)} collective-permute-done((f32[1,1536]{1,0:T(1,128)S(1)}, f32[1,1536]{1,0:T(1,128)S(1)}, u32[]{:S(2)}, u32[]{:S(2)}) %collective-permute-start) | collective-permute-done | bytes 6176 | tf_op jit(solution)/shard_map/ppermute | solution.py:415
  73.4 31.4 %all-to-all-done.1.across_ref = bf16[64,2,4,1536]{3,2,1,0:T(4,128)(2,1)S(1)} async-done(((bf16[64,2,4,1536]{3,2,1,0:T(4,128)(2,1)}), bf16[64,2,4,1536]{3,2,1,0:T(4,128)(2,1)S(1)}, u32[]{:S(2)}, u32[]{:S(2)}) %all-to-all-start.1) | async-done | bytes 1572896 | tf_op jit(solution)/shard_map/all_to_all | solution.py:397
  104.8 10.0 %shard_map.99 = (bf16[512,1536]{1,0:T(8,128)(2,1)}, bf16[512,1536]{1,0:T(8,128)(2,1)}, bf16[64,2,8,768]{3,2,1,0:T(8,128)(2,1)}) custom-call(s32[1]{0:T(128)} %bitcast.flag_ref, bf16[512,1536]{1,0:T(8,128)(2,1)S(1)} %get-tuple-element.15.x_ref, bf16[64,2,4,1536]{3,2,1,0:T(4,128)(2,1)S(1)} %all-to-all-done.1.across_ref, ...), custom_call_target="tpu_custom_call" | custom-call | flops 7000000000 | bytes 18000000 | tf_op jit(solution)/shard_map/pallas_call | solution.py:28
  114.8 6.3 %all-to-all-start.2 = ((bf16[64,2,8,768]{3,2,1,0:T(8,128)(2,1)}), bf16[64,2,8,768]{3,2,1,0:T(8,128)(2,1)S(1)}, u32[]{:S(2)}, u32[]{:S(2)}) async-start(bf16[64,2,8,768]{3,2,1,0:T(8,128)(2,1)} %get-tuple-element.19), calls=%async_computation.2 | async-start | bytes 3145728 | tf_op jit(solution)/shard_map/all_to_all | solution.py:397
  121.0 1.4 collective-permute-start.4
  122.4 1.5 collective-permute-start.2
  124.0 2.9 %collective-permute-done.2.next_ref = bf16[4,128,128]{2,1,0:T(8,128)(2,1)S(1)} collective-permute-done((bf16[4,128,128]{2,1,0:T(8,128)(2,1)S(1)}, bf16[4,128,128]{2,1,0:T(8,128)(2,1)S(1)}, u32[]{:S(2)}, u32[]{:S(2)}) %collective-permute-start.2) | collective-permute-done | bytes 131104 | tf_op jit(solution)/shard_map/ppermute | solution.py:415
  126.8 0.7 copy-done.2
  127.5 2.4 %shard_map.100 = (bf16[512,512]{1,0:T(8,128)(2,1)S(1)}, bf16[512,512]{1,0:T(8,128)(2,1)S(1)}) custom-call(bf16[4,128,128]{2,1,0:T(8,128)(2,1)} %copy-done.2, bf16[4,128,128]{2,1,0:T(8,128)(2,1)} %bitcast.17), custom_call_target="tpu_custom_call" | custom-call | flops 400000000 | bytes 2000000 | tf_op jit(solution)/shard_map/pallas_call | solution.py:28
  129.9 30.9 %all-to-all-done.2.r_ref = bf16[64,2,8,768]{3,2,1,0:T(8,128)(2,1)S(1)} async-done(((bf16[64,2,8,768]{3,2,1,0:T(8,128)(2,1)}), bf16[64,2,8,768]{3,2,1,0:T(8,128)(2,1)S(1)}, u32[]{:S(2)}, u32[]{:S(2)}) %all-to-all-start.2) | async-done | bytes 1572896 | tf_op jit(solution)/shard_map/all_to_all | solution.py:397
  160.8 1.6 shard_map.101
  162.4 1.6 collective-permute-start.3
  164.0 6.4 %all-to-all-start.3 = ((bf16[64,8,768]{2,1,0:T(8,128)(2,1)}), bf16[64,8,768]{2,1,0:T(8,128)(2,1)S(1)}, u32[]{:S(2)}, u32[]{:S(2)}) async-start(bf16[64,8,768]{2,1,0:T(8,128)(2,1)} %get-tuple-element.23), calls=%async_computation.3 | async-start | bytes 1572864 | tf_op jit(solution)/shard_map/all_to_all | solution.py:397
  170.4 12.8 %collective-permute-done.3.r_ref = bf16[64,8,768]{2,1,0:T(8,128)(2,1)S(1)} collective-permute-done((bf16[64,8,768]{2,1,0:T(8,128)(2,1)}, bf16[64,8,768]{2,1,0:T(8,128)(2,1)S(1)}, u32[]{:S(2)}, u32[]{:S(2)}) %collective-permute-start.3) | collective-permute-done | bytes 786464 | tf_op jit(solution)/shard_map/ppermute | solution.py:412
  183.3 1.0 shard_map.103.value_ref
  184.3 0.9 copy-done
  185.2 8.2 %all-to-all-done.3.other_ref = bf16[64,8,768]{2,1,0:T(8,128)(2,1)S(1)} async-done(((bf16[64,8,768]{2,1,0:T(8,128)(2,1)}), bf16[64,8,768]{2,1,0:T(8,128)(2,1)S(1)}, u32[]{:S(2)}, u32[]{:S(2)}) %all-to-all-start.3) | async-done | bytes 786464 | tf_op jit(solution)/shard_map/all_to_all | solution.py:397
  193.4 1.3 collective-permute-start.5
  194.7 6.5 %all-to-all-start.4 = ((bf16[64,8,768]{2,1,0:T(8,128)(2,1)}), bf16[64,8,768]{2,1,0:T(8,128)(2,1)S(1)}, u32[]{:S(2)}, u32[]{:S(2)}) async-start(bf16[64,8,768]{2,1,0:T(8,128)(2,1)} %shard_map.104), calls=%async_computation.4 | async-start | bytes 1572864 | tf_op jit(solution)/shard_map/all_to_all | solution.py:397
  201.2 12.1 %collective-permute-done.5.across_ref = bf16[64,8,768]{2,1,0:T(8,128)(2,1)S(1)} collective-permute-done((bf16[64,8,768]{2,1,0:T(8,128)(2,1)S(1)}, bf16[64,8,768]{2,1,0:T(8,128)(2,1)S(1)}, u32[]{:S(2)}, u32[]{:S(2)}) %collective-permute-start.5) | collective-permute-done | bytes 786464 | tf_op jit(solution)/shard_map/ppermute | solution.py:412
  213.3 6.7 %shard_map.102 = (bf16[256,1536]{1,0:T(8,128)(2,1)S(1)}, bf16[256,1536]{1,0:T(8,128)(2,1)S(1)}) custom-call(bf16[512,1536]{1,0:T(8,128)(2,1)} %collective-permute-done.4.x_ref, bf16[64,8,768]{2,1,0:T(8,128)(2,1)S(1)} %collective-permute-done.5.across_ref, f32[1,1536]{1,0:T(1,128)} %channel_ref.3, bf16[4,384,1024]{2,1,0:T(8,128)(2,1)} %bitcast.9, ...), custom_call_target="tpu_custom_call" | custom-call | flops 20000000000 | bytes 10000000 | tf_op jit(solution)/shard_map/pallas_call | solution.py:28
  220.0 4.1 %all-to-all-done.4.across_ref = bf16[64,8,768]{2,1,0:T(8,128)(2,1)S(1)} async-done(((bf16[64,8,768]{2,1,0:T(8,128)(2,1)}), bf16[64,8,768]{2,1,0:T(8,128)(2,1)S(1)}, u32[]{:S(2)}, u32[]{:S(2)}) %all-to-all-start.4) | async-done | bytes 786464 | tf_op jit(solution)/shard_map/all_to_all | solution.py:397
  224.2 6.7 %shard_map.105 = bf16[2,32,8,1536]{3,2,1,0:T(8,128)(2,1)} custom-call(bf16[256,1536]{1,0:T(8,128)(2,1)S(1)} %get-tuple-element.24.x_ref, bf16[64,8,768]{2,1,0:T(8,128)(2,1)S(1)} %all-to-all-done.4.across_ref, f32[1,1536]{1,0:T(1,128)} %channel_ref.3, bf16[4,384,1024]{2,1,0:T(8,128)(2,1)} %bitcast.10, bf16[4,1024,384]{2,1,0:T(8,128)(2,1)} %bitcast.13, ...), custom_call_target="tpu_custom_call" | custom-call | flops 3000000000 | bytes 11000000 | tf_op jit(solution)/shard_map/pallas_call | solution.py:28
  (9 shorter events, 0.0 us)
Async XLA Ops:
  4.0 52.8 %all-to-all-start = ((bf16[64,2,4,1536]{3,2,1,0:T(4,128)(2,1)}), bf16[64,2,4,1536]{3,2,1,0:T(4,128)(2,1)S(1)}, u32[]{:S(2)}, u32[]{:S(2)}) async-start(bf16[64,2,4,1536]{3,2,1,0:T(4,128)(2,1)} %shard_map.97), calls=%async_computation | async-start | bytes 3145728 | tf_op jit(solution)/shard_map/all_to_all | solution.py:397
  58.8 9.0 %copy-start.3 = (f32[1,1536]{1,0:T(1,128)S(1)}, f32[1,1536]{1,0:T(1,128)}, u32[]{:S(2)}) copy-start(f32[1,1536]{1,0:T(1,128)} %gain_ref.3) | copy-start | bytes 18436
  58.9 45.9 %all-to-all-start.1 = ((bf16[64,2,4,1536]{3,2,1,0:T(4,128)(2,1)}), bf16[64,2,4,1536]{3,2,1,0:T(4,128)(2,1)S(1)}, u32[]{:S(2)}, u32[]{:S(2)}) async-start(bf16[64,2,4,1536]{3,2,1,0:T(4,128)(2,1)} %shard_map.98), calls=%async_computation.1 | async-start | bytes 3145728 | tf_op jit(solution)/shard_map/all_to_all | solution.py:397
  65.0 8.4 %collective-permute-start.1 = (bf16[2,256,256]{2,1,0:T(8,128)(2,1)}, bf16[2,256,256]{2,1,0:T(8,128)(2,1)S(1)}, u32[]{:S(2)}, u32[]{:S(2)}) collective-permute-start(bf16[2,256,256]{2,1,0:T(8,128)(2,1)} %bitcast.3.factor_ref), channel_id=1, source_target_pairs={{64,0},{128,64},{192,128},{0,192},{65,1},{129,65},{193,129},{1,193... | collective-permute-start | bytes 786440 | tf_op jit(solution)/shard_map/ppermute | solution.py:415
  67.8 5.6 %collective-permute-start = (f32[1,1536]{1,0:T(1,128)S(1)}, f32[1,1536]{1,0:T(1,128)S(1)}, u32[]{:S(2)}, u32[]{:S(2)}) collective-permute-start(f32[1,1536]{1,0:T(1,128)S(1)} %copy-done.3), channel_id=1, source_target_pairs={{64,0},{128,64},{192,128},{0,192},{65,1},{129,65},{193,129},{1,193... | collective-permute-start | bytes 18440 | tf_op jit(solution)/shard_map/ppermute | solution.py:415
  114.8 7.7 %copy-start.1 = (bf16[1,4,128,128]{3,2,1,0:T(8,128)(2,1)S(1)}, bf16[1,4,128,128]{3,2,1,0:T(8,128)(2,1)}, u32[]{:S(2)}) copy-start(bf16[1,4,128,128]{3,2,1,0:T(8,128)(2,1)} %param.12) | copy-start | bytes 393220
  114.8 46.1 %all-to-all-start.2 = ((bf16[64,2,8,768]{3,2,1,0:T(8,128)(2,1)}), bf16[64,2,8,768]{3,2,1,0:T(8,128)(2,1)S(1)}, u32[]{:S(2)}, u32[]{:S(2)}) async-start(bf16[64,2,8,768]{3,2,1,0:T(8,128)(2,1)} %get-tuple-element.19), calls=%async_computation.2 | async-start | bytes 3145728 | tf_op jit(solution)/shard_map/all_to_all | solution.py:397
  121.0 49.4 %collective-permute-start.4 = (bf16[512,1536]{1,0:T(8,128)(2,1)}, bf16[512,1536]{1,0:T(8,128)(2,1)}, u32[]{:S(2)}, u32[]{:S(2)}) collective-permute-start(bf16[512,1536]{1,0:T(8,128)(2,1)} %get-tuple-element.21), channel_id=1, source_target_pairs={{0,64},{64,128},{128,192},{192,0},{1,65},{65,129},{129,193},{193,1... | collective-permute-start | bytes 4718600 | tf_op jit(solution)/shard_map/ppermute | solution.py:412
  122.4 4.4 %collective-permute-start.2 = (bf16[4,128,128]{2,1,0:T(8,128)(2,1)S(1)}, bf16[4,128,128]{2,1,0:T(8,128)(2,1)S(1)}, u32[]{:S(2)}, u32[]{:S(2)}) collective-permute-start(bf16[4,128,128]{2,1,0:T(8,128)(2,1)S(1)} %bitcast.18), channel_id=1, source_target_pairs={{64,0},{128,64},{192,128},{0,192},{65,1},{129,65},{193,129},{1,193... | collective-permute-start | bytes 393224 | tf_op jit(solution)/shard_map/ppermute | solution.py:415
  126.8 0.7 copy-start.2
  162.4 20.9 %collective-permute-start.3 = (bf16[64,8,768]{2,1,0:T(8,128)(2,1)}, bf16[64,8,768]{2,1,0:T(8,128)(2,1)S(1)}, u32[]{:S(2)}, u32[]{:S(2)}) collective-permute-start(bf16[64,8,768]{2,1,0:T(8,128)(2,1)} %get-tuple-element.20), channel_id=1, source_target_pairs={{0,64},{64,128},{128,192},{192,0},{1,65},{65,129},{129,193},{193,1... | collective-permute-start | bytes 2359304 | tf_op jit(solution)/shard_map/ppermute | solution.py:412
  164.0 29.4 %all-to-all-start.3 = ((bf16[64,8,768]{2,1,0:T(8,128)(2,1)}), bf16[64,8,768]{2,1,0:T(8,128)(2,1)S(1)}, u32[]{:S(2)}, u32[]{:S(2)}) async-start(bf16[64,8,768]{2,1,0:T(8,128)(2,1)} %get-tuple-element.23), calls=%async_computation.3 | async-start | bytes 1572864 | tf_op jit(solution)/shard_map/all_to_all | solution.py:397
  184.3 0.9 copy-start
  193.4 19.9 %collective-permute-start.5 = (bf16[64,8,768]{2,1,0:T(8,128)(2,1)S(1)}, bf16[64,8,768]{2,1,0:T(8,128)(2,1)S(1)}, u32[]{:S(2)}, u32[]{:S(2)}) collective-permute-start(bf16[64,8,768]{2,1,0:T(8,128)(2,1)S(1)} %all-to-all-done.3.other_ref), channel_id=1, source_target_pairs={{0,64},{64,128},{128,192},{192,0},{1,65},{65,129},{129,193},{193,1... | collective-permute-start | bytes 2359304 | tf_op jit(solution)/shard_map/ppermute | solution.py:412
  194.7 29.5 %all-to-all-start.4 = ((bf16[64,8,768]{2,1,0:T(8,128)(2,1)}), bf16[64,8,768]{2,1,0:T(8,128)(2,1)S(1)}, u32[]{:S(2)}, u32[]{:S(2)}) async-start(bf16[64,8,768]{2,1,0:T(8,128)(2,1)} %shard_map.104), calls=%async_computation.4 | async-start | bytes 1572864 | tf_op jit(solution)/shard_map/all_to_all | solution.py:397
